TPU v7x, 512 devices: a whole 4x8x8 slice. The times are simulated.
512 devices in a mesh: lon: 32 (over z_lo, y, core), lat: 16 (over z_hi, x).
Axes of the slice: x: 4, y: 8, z: 8 (z_hi: 4, z_lo: 2; z = z_hi * 2 + z_lo), core: 2. Of those that a mesh axis runs over, the one named last changes fastest.
Arguments:
- tokens: bfloat16 [384, 128, 1024], P('lon', 'lat'), may hold values from -6 to 6
- query_local: bfloat16 [384, 128, 1024], P('lon', 'lat'), may hold values from -21 to 21, as said below
- key_local: bfloat16 [384, 128, 1024], P('lon', 'lat'), may hold values from -21 to 21, as said below
- value_local: bfloat16 [384, 128, 1024], P('lon', 'lat'), may hold values from -6 to 6
- position_bias: float32 [16, 13, 13], replicated, may hold values from -4 to 4
- output_weight: bfloat16 [1024, 1024], P('lat'), may hold values from -0.1875 to 0.1875
- norm_gain: float32 [1024], replicated, may hold values from 0.1 to 1.9
- global_weight: bfloat16 [1024, 3072], P('lat'), may hold values from -1 to 1
Outputs:
- hidden: bfloat16 [384, 128, 1024], P('lon', 'lat')
- attended: bfloat16 [384, 128, 1024], P('lon', 'lat')
Inputs may be any that keep to these rules, and one draw needn't show every extreme that they name: `query_local`: entries of the neighbourhood queries and keys. `key_local`: entries of the neighbourhood queries and keys.
All inputs are finite; a program needn't handle non-finite values.
Results may differ from a plain program's by a relative error of at most 0.015.
Values may be sent and summed in bfloat16 or wider, within the bound.
No kernel may reach another device: no remote copies, remote signals or barrier semaphores. Data moves between devices by JAX's collectives and lax.ppermute only.
A program may use at most 64 MiB of HBM per device.

v0:
```python
import math

import jax
import jax.numpy as jnp
from jax import lax
from jax.sharding import PartitionSpec as P

STEPS = 4


def extended(block, sides, width):
    for axis, dim in sides:
        count = lax.axis_size(axis)
        forward = [(i, i + 1) for i in range(count - 1)]
        forward.append((count - 1, 0))
        backward = [(target, source) for source, target in forward]
        low = lax.ppermute(
            lax.slice_in_dim(block, block.shape[dim] - width, None, axis=dim), axis, forward
        )
        high = lax.ppermute(lax.slice_in_dim(block, 0, width, axis=dim), axis, backward)
        block = jnp.concatenate([low, block, high], axis=dim)
    return block


def from_behind(x, axis, by):
    count = lax.axis_size(axis)
    return lax.ppermute(x, axis, [(i, (i + by) % count) for i in range(count)])


def offset_table(cells, span, window):
    query_pos = lax.broadcasted_iota(jnp.int32, (cells, span, window), 0)
    key_pos = lax.broadcasted_iota(jnp.int32, (cells, span, window), 1)
    offset = lax.broadcasted_iota(jnp.int32, (cells, span, window), 2)
    return (key_pos - query_pos == offset).astype(jnp.float32)


def fold_rows(left, weight_rows):
    return jnp.dot(left, weight_rows, preferred_element_type=jnp.float32)


def block_merge(carry_state, query_heads, key_block, score_scale):
    running_max, denominator, accumulated = carry_state
    head_count = query_heads.shape[1]
    head_size = query_heads.shape[2]
    keys_part = key_block[0].reshape(key_block.shape[1], head_count, head_size)
    values_part = key_block[1].reshape(key_block.shape[1], head_count, head_size)
    scores = (
        jnp.einsum("qhd,khd->hqk", query_heads, keys_part, preferred_element_type=jnp.float32)
        * score_scale
    )
    new_max = jnp.maximum(running_max, jnp.max(scores, axis=2))
    factor = jnp.exp(running_max - new_max)
    weights = jnp.exp(scores - new_max[:, :, None])
    denominator = denominator * factor + jnp.sum(weights, axis=2)
    weighted = jnp.einsum(
        "hqk,khd->hqd",
        weights.astype(jnp.bfloat16),
        values_part,
        preferred_element_type=jnp.float32,
    )
    accumulated = accumulated * factor[:, :, None] + weighted
    return (new_max, denominator, accumulated)


def body(
    tokens,
    query_local,
    key_local,
    value_local,
    position_bias,
    output_weight,
    norm_gain,
    global_weight,
):
    lon_cells, lat_cells, model_width = tokens.shape
    head_count = position_bias.shape[0]
    radius = (position_bias.shape[1] - 1) // 2
    window = 2 * radius + 1
    head_size = model_width // head_count
    score_scale = 1.0 / math.sqrt(head_size)
    token_count = lon_cells * lat_cells
    lon_span = lon_cells + 2 * radius
    lat_span = lat_cells + 2 * radius
    stacked = jnp.stack([key_local, value_local])
    padded = extended(stacked, (("lon", 1), ("lat", 2)), radius)
    window_keys = padded[0].reshape(lon_span * lat_span, head_count, head_size)
    window_values = padded[1].reshape(lon_span * lat_span, head_count, head_size)
    query_heads = query_local.reshape(token_count, head_count, head_size)
    lon_table = offset_table(lon_cells, lon_span, window)
    lat_table = offset_table(lat_cells, lat_span, window)
    lat_start = lax.axis_index("lat") * lat_cells
    lat_total = lat_cells * lax.axis_size("lat")
    lat_global = lat_start + jnp.arange(lat_span, dtype=jnp.int32) - radius
    lat_inside = (lat_global >= 0) & (lat_global < lat_total)
    lon_near = jnp.sum(lon_table, axis=2) > 0.5
    lat_near = (jnp.sum(lat_table, axis=2) > 0.5) & lat_inside[None, :]
    allowed = (lon_near[:, None, :, None] & lat_near[None, :, None, :]).reshape(
        token_count, lon_span * lat_span
    )

    def one_head(operands):
        query_one, key_one, value_one, bias_one = operands
        bias_lat = jnp.einsum("ab,jkb->ajk", bias_one, lat_table, precision=lax.Precision.HIGHEST)
        bias_full = jnp.einsum(
            "ajk,ila->ijlk", bias_lat, lon_table, precision=lax.Precision.HIGHEST
        )
        bias_full = bias_full.reshape(token_count, lon_span * lat_span)
        scores = jnp.einsum("qd,kd->qk", query_one, key_one, preferred_element_type=jnp.float32)
        scores = jnp.where(allowed, scores * score_scale + bias_full, -1e30)
        largest = jnp.max(scores, axis=1, keepdims=True)
        weights = jnp.exp(scores - largest)
        denominator = jnp.sum(weights, axis=1, keepdims=True)
        weighted = jnp.dot(
            weights.astype(jnp.bfloat16), value_one, preferred_element_type=jnp.float32
        )
        return (weighted / denominator).astype(jnp.bfloat16)

    head_outputs = lax.map(
        one_head,
        (
            jnp.transpose(query_heads, (1, 0, 2)),
            jnp.transpose(window_keys, (1, 0, 2)),
            jnp.transpose(window_values, (1, 0, 2)),
            position_bias,
        ),
    )
    local_out = jnp.transpose(head_outputs, (1, 0, 2)).reshape(token_count, model_width)
    flat_tokens = tokens.reshape(token_count, model_width)
    projected = fold_rows(local_out, lax.all_gather(output_weight, "lat", axis=0, tiled=True))
    hidden = (flat_tokens.astype(jnp.float32) + projected).astype(jnp.bfloat16)
    widened_hidden = hidden.astype(jnp.float32)
    inverse = lax.rsqrt(jnp.mean(widened_hidden * widened_hidden, axis=1, keepdims=True) + 1e-06)
    normed = (widened_hidden * inverse * norm_gain).astype(jnp.bfloat16)
    triple = fold_rows(normed, lax.all_gather(global_weight, "lat", axis=0, tiled=True))
    triple = triple.astype(jnp.bfloat16)
    global_query = triple[:, :model_width].reshape(token_count, head_count, head_size)
    key_pair = jnp.stack([triple[:, model_width : 2 * model_width], triple[:, 2 * model_width :]])
    carry_state = (
        jnp.full((head_count, token_count), -1e30, jnp.float32),
        jnp.zeros((head_count, token_count), jnp.float32),
        jnp.zeros((head_count, token_count, head_size), jnp.float32),
    )
    carry_state = block_merge(carry_state, global_query, key_pair, score_scale)
    travelling = key_pair
    for hop_index in range(STEPS):
        travelling = from_behind(travelling, ("lon", "lat"), 1)
        carry_state = block_merge(carry_state, global_query, travelling, score_scale)
    running_max, denominator, accumulated = carry_state
    attended = accumulated / denominator[:, :, None]
    attended = (
        jnp.transpose(attended, (1, 0, 2))
        .reshape(lon_cells, lat_cells, model_width)
        .astype(jnp.bfloat16)
    )
    return (hidden.reshape(lon_cells, lat_cells, model_width), attended)


def solution(mesh):
    return jax.shard_map(
        body,
        mesh=mesh,
        in_specs=(
            P("lon", "lat", None),
            P("lon", "lat", None),
            P("lon", "lat", None),
            P("lon", "lat", None),
            P(),
            P("lat", None),
            P(),
            P("lat", None),
        ),
        out_specs=(P("lon", "lat", None), P("lon", "lat", None)),
        check_vma=False,
    )
```

profile of v0, /device:TPU:313, one launch (start us, length us, event | category | flops | bytes accessed | tf_op | source)
XLA Modules:
  0.0 309.6 jit_solution(16309423687903335286)
XLA Ops:
  7.9 1.2 copy_bitcast_fusion.2
  9.3 2.9 collective-permute-start
  12.2 2.1 collective-permute-start.1
  14.3 1.2 collective-permute-done
  15.5 6.6 %collective-permute-done.1 = bf16[2,6,8,1024]{3,1,2,0:T(8,128)(2,1)S(1)} collective-permute-done((bf16[2,6,8,1024]{3,1,2,0:T(8,128)(2,1)S(1)}, bf16[2,6,8,1024]{3,1,2,0:T(8,128)(2,1)S(1)}, u32[]{:S(2)}, u32[]{:S(2)}) %collective-permute-start.1) | collective-permute-done | bytes 196640 | tf_op jit(solution)/shard_map/ppermute | solution.py:20
  23.5 3.1 %collective-permute-start.2 = (bf16[2,24,6,1024]{3,1,2,0:T(8,128)(2,1)}, bf16[2,24,6,1024]{3,1,2,0:T(8,128)(2,1)S(1)}, u32[]{:S(2)}, u32[]{:S(2)}) collective-permute-start(bf16[2,24,6,1024]{3,1,2,0:T(8,128)(2,1)} %get-tuple-element.126), channel_id=1, source_target_pairs={{0,1},{1,2},{2,3},{3,4},{4,5},{5,6},{6,7},{7,8},{8,9},{9,10},{10,1... | collective-permute-start | bytes 1769480 | tf_op jit(solution)/shard_map/ppermute | solution.py:17
  26.6 6.4 %collective-permute-start.3 = (bf16[2,24,6,1024]{3,1,2,0:T(8,128)(2,1)S(1)}, bf16[2,24,6,1024]{3,1,2,0:T(8,128)(2,1)}, u32[]{:S(2)}, u32[]{:S(2)}) collective-permute-start(bf16[2,24,6,1024]{3,1,2,0:T(8,128)(2,1)S(1)} %get-tuple-element.127), channel_id=1, source_target_pairs={{1,0},{2,1},{3,2},{4,3},{5,4},{6,5},{7,6},{8,7},{9,8},{10,9},{11,1... | collective-permute-start | bytes 1769480 | tf_op jit(solution)/shard_map/ppermute | solution.py:20
  33.6 26.1 %collective-permute-done.2 = bf16[2,24,6,1024]{3,1,2,0:T(8,128)(2,1)S(1)} collective-permute-done((bf16[2,24,6,1024]{3,1,2,0:T(8,128)(2,1)}, bf16[2,24,6,1024]{3,1,2,0:T(8,128)(2,1)S(1)}, u32[]{:S(2)}, u32[]{:S(2)}) %collective-permute-start.2) | collective-permute-done | bytes 589856 | tf_op jit(solution)/shard_map/ppermute | solution.py:17
  59.6 1.6 pad_maximum_fusion
  62.9 1.3 reshape_squeeze.30
  64.3 1.8 copy.86
  66.7 1.3 reshape_squeeze.31
  68.0 1.8 copy.88
  69.8 103.0 %while.11 = (s32[]{:T(128)}, bf16[16,96,64]{1,2,0:T(8,128)(2,1)S(1)}, bf16[16,96,64]{2,1,0:T(8,128)(2,1)S(1)}, bf16[16,480,64]{2,1,0:T(8,128)(2,1)}, f32[16,13,1...) while((s32[]{:T(128)}, ...), condition=%wide.region_5.6_spmd.clone, body=%wide.region_2.5_spmd.clone.sunk | while | flops 19753728 | bytes 2181005 | solution.py:118
  73.7 1.2 fusion.121
  80.1 1.2 fusion.121
  86.5 1.2 fusion.121
  93.0 1.2 fusion.121
  94.4 1.2 fusion.123
  99.4 1.2 fusion.121
  105.8 1.2 fusion.121
  107.2 1.2 fusion.123
  112.3 1.2 fusion.121
  118.7 1.2 fusion.121
  125.1 1.2 fusion.121
  131.6 1.2 fusion.121
  138.0 1.2 fusion.121
  144.5 1.2 fusion.121
  150.9 1.2 fusion.121
  157.3 1.2 fusion.121
  163.8 1.2 fusion.121
  165.2 1.2 fusion.123
  170.2 1.2 fusion.121
  172.8 2.3 fusion.48
  175.1 17.7 %all-gather.5.cloned.1.call-done = bf16[1024,3072]{1,0:T(8,128)(2,1)} async-done(((bf16[64,3072]{1,0:T(8,128)(2,1)}), bf16[1024,3072]{1,0:T(8,128)(2,1)}) %all-gather.5.cloned.1.call-update) | async-done | bytes 6291472 | tf_op jit(solution)/shard_map/all_gather | solution.py:134
  192.9 4.0 %convolution_convert_fusion = bf16[96,3072]{1,0:T(8,128)(2,1)S(1)} fusion(bf16[1024,3072]{1,0:T(8,128)(2,1)} %all-gather.5.cloned.1.call-done, bf16[96,1024]{1,0:T(8,128)(2,1)S(1)} %get-tuple-element.147, f32[1024]{0:T(1024)S(1)} %copy-done.10, f32[96]{0:T(128)S(1)} %add_rsqrt_fusion), kind=kOutput, calls=%fused_computation.32 | convolution fusion | flops 604667904 | bytes 7082368 | tf_op jit(solution)/shard_map/dot_general | solution.py:38
  197.0 3.2 %collective-permute-start.4 = (bf16[2,96,1024]{2,1,0:T(8,128)(2,1)S(1)}, bf16[2,96,1024]{2,1,0:T(8,128)(2,1)S(1)}, u32[]{:S(2)}, u32[]{:S(2)}) collective-permute-start(bf16[2,96,1024]{2,1,0:T(8,128)(2,1)S(1)} %pad_maximum_fusion.2), channel_id=1, source_target_pairs={{0,1},{1,2},{2,3},{3,4},{4,5},{5,6},{6,7},{7,8},{8,9},{9,10},{10,1... | collective-permute-start | bytes 1179656 | tf_op jit(solution)/shard_map/ppermute | solution.py:27
  201.8 20.7 %collective-permute-done.4 = bf16[2,96,1024]{2,1,0:T(8,128)(2,1)S(1)} collective-permute-done((bf16[2,96,1024]{2,1,0:T(8,128)(2,1)S(1)}, bf16[2,96,1024]{2,1,0:T(8,128)(2,1)S(1)}, u32[]{:S(2)}, u32[]{:S(2)}) %collective-permute-start.4) | collective-permute-done | bytes 393248 | tf_op jit(solution)/shard_map/ppermute | solution.py:27
  222.5 1.9 collective-permute-start.5
  225.8 22.2 %collective-permute-done.5 = bf16[2,96,1024]{2,1,0:T(8,128)(2,1)} collective-permute-done((bf16[2,96,1024]{2,1,0:T(8,128)(2,1)S(1)}, bf16[2,96,1024]{2,1,0:T(8,128)(2,1)}, u32[]{:S(2)}, u32[]{:S(2)}) %collective-permute-start.5) | collective-permute-done | bytes 393248 | tf_op jit(solution)/shard_map/ppermute | solution.py:27
  247.9 1.9 collective-permute-start.6
  252.3 17.8 %collective-permute-done.6 = bf16[2,96,1024]{2,1,0:T(8,128)(2,1)} collective-permute-done((bf16[2,96,1024]{2,1,0:T(8,128)(2,1)}, bf16[2,96,1024]{2,1,0:T(8,128)(2,1)}, u32[]{:S(2)}, u32[]{:S(2)}) %collective-permute-start.6) | collective-permute-done | bytes 393248 | tf_op jit(solution)/shard_map/ppermute | solution.py:27
  270.1 2.1 collective-permute-start.7
  274.9 1.3 fusion.85
  276.2 15.4 %collective-permute-done.7 = bf16[2,96,1024]{2,1,0:T(8,128)(2,1)} collective-permute-done((bf16[2,96,1024]{2,1,0:T(8,128)(2,1)}, bf16[2,96,1024]{2,1,0:T(8,128)(2,1)}, u32[]{:S(2)}, u32[]{:S(2)}) %collective-permute-start.7) | collective-permute-done | bytes 393248 | tf_op jit(solution)/shard_map/ppermute | solution.py:27
  291.6 1.8 fusion.80
  293.3 1.8 copy.102
  295.1 2.1 fusion.84
  (216 shorter events, 97.7 us)
Async XLA Ops:
  7.2 165.7 %all-gather.3.cloned.1.call-start = ((), (), s32[]{:S(2)}) async-start(), calls=%async_computation | async-start | bytes 2228224 | tf_op jit(solution)/shard_map/all_gather | solution.py:129
  7.9 185.0 %all-gather.5.cloned.1.call-start = ((), (), s32[]{:S(2)}) async-start(), calls=%async_computation.1 | async-start | bytes 6684672 | tf_op jit(solution)/shard_map/all_gather | solution.py:134
  9.3 6.2 %collective-permute-start = (bf16[2,6,8,1024]{3,1,2,0:T(8,128)(2,1)S(1)}, bf16[2,6,8,1024]{3,1,2,0:T(8,128)(2,1)S(1)}, u32[]{:S(2)}, u32[]{:S(2)}) collective-permute-start(bf16[2,6,8,1024]{3,1,2,0:T(8,128)(2,1)S(1)} %get-tuple-element.133), channel_id=1, source_target_pairs={{0,16},{16,32},{32,48},{48,64},{64,80},{80,96},{96,112},{112,128},... | collective-permute-start | bytes 589832 | tf_op jit(solution)/shard_map/ppermute | solution.py:17
  12.2 20.9 %copy-start.9 = (bf16[12,8,1024]{2,1,0:T(8,128)(2,1)S(1)}, bf16[12,8,1024]{2,1,0:T(8,128)(2,1)}, u32[]{:S(2)}) copy-start(bf16[12,8,1024]{2,1,0:T(8,128)(2,1)} %param.11) | copy-start | bytes 589828
  12.2 9.9 %collective-permute-start.1 = (bf16[2,6,8,1024]{3,1,2,0:T(8,128)(2,1)S(1)}, bf16[2,6,8,1024]{3,1,2,0:T(8,128)(2,1)S(1)}, u32[]{:S(2)}, u32[]{:S(2)}) collective-permute-start(bf16[2,6,8,1024]{3,1,2,0:T(8,128)(2,1)S(1)} %get-tuple-element.134), channel_id=1, source_target_pairs={{16,0},{32,16},{48,32},{64,48},{80,64},{96,80},{112,96},{128,112},... | collective-permute-start | bytes 589832 | tf_op jit(solution)/shard_map/ppermute | solution.py:20
  23.5 36.1 %collective-permute-start.2 = (bf16[2,24,6,1024]{3,1,2,0:T(8,128)(2,1)}, bf16[2,24,6,1024]{3,1,2,0:T(8,128)(2,1)S(1)}, u32[]{:S(2)}, u32[]{:S(2)}) collective-permute-start(bf16[2,24,6,1024]{3,1,2,0:T(8,128)(2,1)} %get-tuple-element.126), channel_id=1, source_target_pairs={{0,1},{1,2},{2,3},{3,4},{4,5},{5,6},{6,7},{7,8},{8,9},{9,10},{10,1... | collective-permute-start | bytes 1769480 | tf_op jit(solution)/shard_map/ppermute | solution.py:17
  26.6 33.0 %collective-permute-start.3 = (bf16[2,24,6,1024]{3,1,2,0:T(8,128)(2,1)S(1)}, bf16[2,24,6,1024]{3,1,2,0:T(8,128)(2,1)}, u32[]{:S(2)}, u32[]{:S(2)}) collective-permute-start(bf16[2,24,6,1024]{3,1,2,0:T(8,128)(2,1)S(1)} %get-tuple-element.127), channel_id=1, source_target_pairs={{1,0},{2,1},{3,2},{4,3},{5,4},{6,5},{7,6},{8,7},{9,8},{10,9},{11,1... | collective-permute-start | bytes 1769480 | tf_op jit(solution)/shard_map/ppermute | solution.py:20
  64.3 1.9 copy-start
  68.0 1.8 copy-start.7
  69.8 103.1 %copy-start.8 = (bf16[12,8,1024]{2,1,0:T(8,128)(2,1)S(1)}, bf16[12,8,1024]{2,1,0:T(8,128)(2,1)}, u32[]{:S(2)}) copy-start(bf16[12,8,1024]{2,1,0:T(8,128)(2,1)} %param.10) | copy-start | bytes 589828
  172.8 20.1 %copy-start.10 = (f32[1024]{0:T(1024)S(1)}, f32[1024]{0:T(1024)}, u32[]{:S(2)}) copy-start(f32[1024]{0:T(1024)} %param.16) | copy-start | bytes 12292
  175.1 21.7 %copy-start.6 = (bf16[96,1024]{1,0:T(8,128)(2,1)}, bf16[96,1024]{1,0:T(8,128)(2,1)S(1)}, u32[]{:S(2)}) copy-start(bf16[96,1024]{1,0:T(8,128)(2,1)S(1)} %get-tuple-element.147) | copy-start | bytes 589828
  197.0 25.4 %collective-permute-start.4 = (bf16[2,96,1024]{2,1,0:T(8,128)(2,1)S(1)}, bf16[2,96,1024]{2,1,0:T(8,128)(2,1)S(1)}, u32[]{:S(2)}, u32[]{:S(2)}) collective-permute-start(bf16[2,96,1024]{2,1,0:T(8,128)(2,1)S(1)} %pad_maximum_fusion.2), channel_id=1, source_target_pairs={{0,1},{1,2},{2,3},{3,4},{4,5},{5,6},{6,7},{7,8},{8,9},{9,10},{10,1... | collective-permute-start | bytes 1179656 | tf_op jit(solution)/shard_map/ppermute | solution.py:27
  222.5 25.5 %collective-permute-start.5 = (bf16[2,96,1024]{2,1,0:T(8,128)(2,1)S(1)}, bf16[2,96,1024]{2,1,0:T(8,128)(2,1)}, u32[]{:S(2)}, u32[]{:S(2)}) collective-permute-start(bf16[2,96,1024]{2,1,0:T(8,128)(2,1)S(1)} %collective-permute-done.4), channel_id=1, source_target_pairs={{0,1},{1,2},{2,3},{3,4},{4,5},{5,6},{6,7},{7,8},{8,9},{9,10},{10,1... | collective-permute-start | bytes 1179656 | tf_op jit(solution)/shard_map/ppermute | solution.py:27
  247.9 22.1 %collective-permute-start.6 = (bf16[2,96,1024]{2,1,0:T(8,128)(2,1)}, bf16[2,96,1024]{2,1,0:T(8,128)(2,1)}, u32[]{:S(2)}, u32[]{:S(2)}) collective-permute-start(bf16[2,96,1024]{2,1,0:T(8,128)(2,1)} %collective-permute-done.5), channel_id=1, source_target_pairs={{0,1},{1,2},{2,3},{3,4},{4,5},{5,6},{6,7},{7,8},{8,9},{9,10},{10,1... | collective-permute-start | bytes 1179656 | tf_op jit(solution)/shard_map/ppermute | solution.py:27
  270.1 21.5 %collective-permute-start.7 = (bf16[2,96,1024]{2,1,0:T(8,128)(2,1)}, bf16[2,96,1024]{2,1,0:T(8,128)(2,1)}, u32[]{:S(2)}, u32[]{:S(2)}) collective-permute-start(bf16[2,96,1024]{2,1,0:T(8,128)(2,1)} %collective-permute-done.6), channel_id=1, source_target_pairs={{0,1},{1,2},{2,3},{3,4},{4,5},{5,6},{6,7},{7,8},{8,9},{9,10},{10,1... | collective-permute-start | bytes 1179656 | tf_op jit(solution)/shard_map/ppermute | solution.py:27
  298.4 1.1 copy-start.1
  298.4 1.3 copy-start.2
  298.7 1.3 copy-start.3
  299.6 1.0 copy-start.4
  300.0 1.0 copy-start.5
Sparse Core Ops, SparseCore 0:
  11.0 77.9 all-gather.2
  92.0 100.8 all-gather.4
where the time goes:
time: 312 us; the launch traced here: 310 us
  waiting for transfers between devices  128 us (41%)
  matrix products  71.3 us (23%)
  local copies, waits for them, and re-layouts  61.4 us (20%)
  starting transfers between devices  23.6 us (8%)
  between operations  14.5 us (5%)
  other arithmetic  9.46 us (3%)
    ppermute x4, waiting for transfers between devices, from_behind(): return lax.ppermute(x, axis, [(i, (i + by) % count) for i in range(count)])  76 us
    ppermute x2, waiting for transfers between devices, extended(): lax.ppermute(lax.slice_in_dim(block, block.shape[dim] - width, None, axis...  27.3 us
    dot_general x16, matrix products, one_head(): jnp.einsum('qd,kd->qk', query_one, key_one, preferred_element_type=jnp.fl...  19.4 us
    dot_general x16, matrix products, one_head(): jnp.dot(weights.astype(jnp.bfloat16), value_one, preferred_element_type=j...  18.6 us
    dot_general x16, matrix products, one_head(): jnp.einsum('ajk,ila->ijlk', bias_lat, lon_table, precision=lax.Precision....  18.3 us
    all_gather x1, waiting for transfers between devices, body(): lax.all_gather(global_weight, 'lat', axis=0, tiled=True)  17.7 us
    dynamic_slice x16, local copies, waits for them, and re-layouts, body(): lax.map(one_head, (jnp.transpose(query_heads, (1, 0, 2)), jnp.transpose(w...  13.2 us
    transpose x16, local copies, waits for them, and re-layouts, one_head(): jnp.einsum('ajk,ila->ijlk', bias_lat, lon_table, precision=lax.Precision....  10.1 us
  transfers between devices with their start and end apart: 10, of which 8 were waited for; matrix products, arithmetic and copies ran while one was open for 41% of the time, Pallas kernels for 0%

commit v1 on v0

v1 whole, which is shorter than its diff:
```python
import functools
import math

import jax
import jax.numpy as jnp
from jax import lax
from jax.experimental import pallas as pl
from jax.experimental.pallas import tpu as pltpu
from jax.sharding import Mesh, PartitionSpec as P

LON = ("zl", "y", "c")
LAT = ("zh", "x")
RADIUS = 6
WINDOW = 13
TL = 12
TJ = 8
CELLS = TL * TJ
HALF = 40
KEYS = 512
NEG = -1e30
VMEM = 48 * 1024 * 1024


def params():
    return pltpu.CompilerParams(vmem_limit_bytes=VMEM)


def vspec():
    return pl.BlockSpec(memory_space=pltpu.VMEM)


def anyspec():
    return pl.BlockSpec(memory_space=pl.ANY)


def sspec():
    return pl.BlockSpec(memory_space=pltpu.SMEM)


def edge_kernel(k_hbm, v_hbm, up_ref, down_ref, buf, sems):
    copies = [pltpu.make_async_copy(ref, buf.at[at], sems.at[at]) for at, ref in enumerate((k_hbm, v_hbm))]
    for copy in copies:
        copy.start()
    row = lax.broadcasted_iota(jnp.int32, (2 * HALF, CELLS), 0)
    col = lax.broadcasted_iota(jnp.int32, (2 * HALF, CELLS), 1)
    half = jnp.where(row >= HALF, 1, 0)
    r = row - half * HALF
    lon = half * 6 + r // 6
    lat = r % 6
    real = r < 36
    first = (real & (col == lon * TJ + lat)).astype(jnp.float32).astype(jnp.bfloat16)
    last = (real & (col == lon * TJ + lat + 2)).astype(jnp.float32).astype(jnp.bfloat16)
    for at, copy in enumerate(copies):
        copy.wait()
        x = buf[at]
        up_ref[at] = jnp.dot(last, x, preferred_element_type=jnp.float32).astype(jnp.bfloat16)
        down_ref[at] = jnp.dot(first, x, preferred_element_type=jnp.float32).astype(jnp.bfloat16)


def edges(k, v):
    shape = jax.ShapeDtypeStruct((2, 2 * HALF, k.shape[1]), jnp.bfloat16)
    return pl.pallas_call(
        edge_kernel,
        out_shape=(shape, shape),
        in_specs=[anyspec()] * 2,
        out_specs=(vspec(), vspec()),
        scratch_shapes=[pltpu.VMEM((2,) + k.shape, jnp.bfloat16), pltpu.SemaphoreType.DMA((2,))],
        compiler_params=params(),
        name="edges",
    )(k, v)


def side_kernel(low_ref, high_ref, k_ref, v_ref, east_ref, west_ref, rows):
    row = lax.broadcasted_iota(jnp.int32, (128, 256), 0)
    col = lax.broadcasted_iota(jnp.int32, (128, 256), 1)
    low = row < HALF
    own = (row >= HALF) & (row < HALF + 48)
    first = jnp.where(low, row, jnp.where(own, 80 + row - HALF, 176 + row - HALF - 48))
    last = jnp.where(own, first + 48, first + HALF)
    pick_first = jnp.where(col == first, 1.0, 0.0).astype(jnp.bfloat16)
    pick_last = jnp.where(col == last, 1.0, 0.0).astype(jnp.bfloat16)
    for at, ref in enumerate((k_ref, v_ref)):
        rows[0:80] = low_ref[at]
        rows[80:176] = ref[...]
        rows[176:256] = high_ref[at]
        x = rows[...]
        east_ref[at] = jnp.dot(pick_last, x, preferred_element_type=jnp.float32).astype(jnp.bfloat16)
        west_ref[at] = jnp.dot(pick_first, x, preferred_element_type=jnp.float32).astype(jnp.bfloat16)


def sides(low, high, k, v):
    shape = jax.ShapeDtypeStruct((2, 128, k.shape[1]), jnp.bfloat16)
    return pl.pallas_call(
        side_kernel,
        out_shape=(shape, shape),
        in_specs=[vspec()] * 4,
        out_specs=(vspec(), vspec()),
        scratch_shapes=[pltpu.VMEM((256, k.shape[1]), jnp.bfloat16)],
        compiler_params=params(),
        name="sides",
    )(low, high, k, v)


def key_places(shape, dim):
    col = lax.broadcasted_iota(jnp.int32, shape, dim)
    lon = 6 + col // TJ
    lat = 6 + col % TJ
    side = jnp.zeros_like(col)

    def halo(base, first_lon, lat_base, which, lon, lat, side):
        r = col - base
        here = (r >= 0) & (r < HALF)
        rr = jnp.clip(r, 0, HALF - 1)
        lon = jnp.where(here, first_lon + rr // 6, lon)
        lat = jnp.where(here, lat_base + rr % 6, lat)
        side = jnp.where(here, jnp.where(rr < 36, which, 3), side)
        return lon, lat, side

    for base, first_lon, lat_base, which in (
        (96, 6, 0, 1),
        (136, 12, 0, 1),
        (176, 6, 14, 2),
        (216, 12, 14, 2),
        (256, 0, 0, 1),
        (344, 0, 14, 2),
        (384, 18, 0, 1),
        (472, 18, 14, 2),
    ):
        lon, lat, side = halo(base, first_lon, lat_base, which, lon, lat, side)
    for base, first_lon in ((296, 0), (424, 18)):
        r = col - base
        here = (r >= 0) & (r < 48)
        rr = jnp.clip(r, 0, 47)
        lon = jnp.where(here, first_lon + rr // TJ, lon)
        lat = jnp.where(here, 6 + rr % TJ, lat)
        side = jnp.where(here, 0, side)
    return lon, lat, side


def bias_kernel(place_ref, table_ref, out_ref):
    heads = out_ref.shape[0]
    rows = heads * TJ
    table = jnp.broadcast_to(table_ref[...][:, None, :], (heads, TJ, 256)).reshape(rows, 256)
    high = table.astype(jnp.bfloat16).astype(jnp.float32)
    mid = (table - high).astype(jnp.bfloat16).astype(jnp.float32)
    low = table - high - mid
    parts = jnp.concatenate([high, mid, low], axis=0)
    lat_of_row = lax.broadcasted_iota(jnp.int32, parts.shape, 0) % TJ
    index = lax.broadcasted_iota(jnp.int32, (256, 384), 0)
    column = lax.broadcasted_iota(jnp.int32, (1, 384), 1)
    lon_gap, key_lat = column // 20, column % 20
    strip = jnp.zeros((3 * rows, 384), jnp.float32)
    for j in range(TJ):
        here = jnp.where(lat_of_row == j, parts, 0.0).astype(jnp.bfloat16)
        fits = (key_lat >= j) & (key_lat < j + WINDOW) & (lon_gap < WINDOW)
        wanted = jnp.where(fits, lon_gap * WINDOW + key_lat - j, -1)
        hot = jnp.where(index == wanted, 1.0, 0.0).astype(jnp.bfloat16)
        strip += jnp.dot(here, hot, preferred_element_type=jnp.float32)
    strip = strip.astype(jnp.bfloat16)
    strip = jnp.concatenate([strip[:rows], strip[rows : 2 * rows], strip[2 * rows :]], axis=1)

    lon, lat, side = key_places((1, KEYS), 1)
    at_south = place_ref[3] == 0
    at_north = place_ref[3] == place_ref[4] - 1
    closed = (side == 3) | ((side == 1) & at_south) | ((side == 2) & at_north)
    row = lax.broadcasted_iota(jnp.int32, (384, KEYS), 0)
    lat_gap = lat - lax.broadcasted_iota(jnp.int32, (TJ, KEYS), 0)
    near = (lat_gap >= 0) & (lat_gap < WINDOW) & jnp.logical_not(closed)
    for i in range(TL):
        gap = lon - i
        inside = (gap >= 0) & (gap < WINDOW)
        hot = jnp.where(row == jnp.where(inside, gap * 20 + lat, -1), 1.0, 0.0).astype(jnp.bfloat16)
        hot = jnp.concatenate([hot, hot, hot], axis=0)
        found = jnp.dot(strip, hot, preferred_element_type=jnp.float32)
        found = jnp.where((near & inside)[None], found.reshape(heads, TJ, KEYS), NEG)
        out_ref[:, TJ * i : TJ * i + TJ, :] = found


def bias_table(position_bias, place):
    heads = position_bias.shape[0]
    table = position_bias.reshape(heads, WINDOW * WINDOW)
    table = jnp.pad(table, ((0, 0), (0, 256 - WINDOW * WINDOW)))
    return pl.pallas_call(
        bias_kernel,
        out_shape=jax.ShapeDtypeStruct((heads, CELLS, KEYS), jnp.float32),
        in_specs=[sspec(), vspec()],
        out_specs=vspec(),
        compiler_params=params(),
        name="bias",
    )(place, table)


def pair_attention(q, k, v, bias):
    n = q.shape[0]
    lane = lax.broadcasted_iota(jnp.int32, (n, 128), 1)
    zero = jnp.zeros_like(q)
    both = jnp.concatenate([jnp.where(lane < 64, q, zero), jnp.where(lane >= 64, q, zero)], axis=0)
    scores = lax.dot_general(both, k, (((1,), (1,)), ((), ())), preferred_element_type=jnp.float32)
    if bias is not None:
        scores = scores + bias
    largest = jnp.max(scores, axis=1, keepdims=True)
    weights = jnp.exp(scores - largest)
    total = jnp.sum(weights, axis=1, keepdims=True)
    out = jnp.dot(weights.astype(jnp.bfloat16), v, preferred_element_type=jnp.float32) / total
    return jnp.where(lane < 64, out[:n], out[n:]).astype(jnp.bfloat16)


def attend_kernel(
    q_ref, k_ref, v_ref, low_ref, high_ref, west_ref, east_ref, bias_ref, out_ref, kbuf, vbuf
):
    width = q_ref.shape[1]
    for buf, own, at in ((kbuf, k_ref, 0), (vbuf, v_ref, 1)):
        buf[0:96] = own[...]
        buf[96:176] = low_ref[at]
        buf[176:256] = high_ref[at]
        buf[256:384] = west_ref[at]
        buf[384:512] = east_ref[at]
    for p in range(width // 128):
        lanes = slice(128 * p, 128 * p + 128)
        q = q_ref[:, lanes] * jnp.bfloat16(0.125)
        bias = bias_ref[2 * p : 2 * p + 2].reshape(2 * CELLS, KEYS)
        out = pair_attention(q, kbuf[:, lanes], vbuf[:, lanes], bias)
        for e in range(2):
            at = turned(2 * p + e) * 64
            out_ref[:, at : at + 64] = out[:, 64 * e : 64 * e + 64]


def turned(chunk):
    return (chunk % 4) * 4 + chunk // 4


def attend(q, k, v, low, high, west, east, bias):
    width = q.shape[1]
    return pl.pallas_call(
        attend_kernel,
        out_shape=jax.ShapeDtypeStruct(q.shape, jnp.bfloat16),
        in_specs=[vspec()] * 8,
        out_specs=vspec(),
        scratch_shapes=[
            pltpu.VMEM((KEYS, width), jnp.bfloat16),
            pltpu.VMEM((KEYS, width), jnp.bfloat16),
        ],
        compiler_params=params(),
        name="local",
    )(q, k, v, low, high, west, east, bias)


def project_kernel(at_ref, x_ref, tok_ref, mine_ref, other_ref, gain_ref, hid_ref, norm_ref, pbuf):
    width = x_ref.shape[1]
    core, xpos = at_ref[0], at_ref[1]
    side = width // 2
    deep = width // 4
    for ref, where in ((mine_ref, core), (other_ref, 1 - core)):
        total = jnp.zeros((CELLS, side), jnp.float32)
        for u in range(4):
            lanes = pl.ds(pl.multiple_of(lax.rem(xpos + u, 4) * deep, deep), deep)
            total += jnp.dot(
                x_ref[:, lanes], ref[deep * u : deep * u + deep], preferred_element_type=jnp.float32
            )
        pbuf[:, pl.ds(pl.multiple_of(where * side, side), side)] = total
    hidden = (tok_ref[...].astype(jnp.float32) + pbuf[...]).astype(jnp.bfloat16)
    hid_ref[...] = hidden
    wide = hidden.astype(jnp.float32)
    inverse = lax.rsqrt(jnp.mean(wide * wide, axis=1, keepdims=True) + 1e-06)
    normed = (wide * inverse * gain_ref[...]).astype(jnp.bfloat16)
    for chunk in range(width // 64):
        at = turned(chunk) * 64
        norm_ref[:, at : at + 64] = normed[:, 64 * chunk : 64 * chunk + 64]


def project(at, x, tok, mine, other, gain):
    shape = jax.ShapeDtypeStruct(x.shape, jnp.bfloat16)
    return pl.pallas_call(
        project_kernel,
        out_shape=(shape, shape),
        in_specs=[sspec()] + [vspec()] * 5,
        out_specs=(vspec(), vspec()),
        scratch_shapes=[pltpu.VMEM(x.shape, jnp.float32)],
        compiler_params=params(),
        name="project",
    )(at, x, tok, mine, other, gain)


def global_kernel(side_ref, x0, x1, x2, x3, x4, wq, wk, wv, *rest):
    out_ref, xbuf = rest[-2:]

    @pl.when(pl.program_id(0) == 0)
    def _():
        for at, ref in enumerate((x0, x1, x2, x3, x4)):
            xbuf[CELLS * at : CELLS * at + CELLS] = ref[...]

    def part(rows, w):
        return jnp.dot(rows, w[...], preferred_element_type=jnp.float32).astype(jnp.bfloat16)

    q = part(xbuf[0:CELLS], wq) * jnp.bfloat16(0.125)
    k = part(xbuf[...], wk)
    v = part(xbuf[...], wv)
    for p in range(q.shape[1] // 128):
        lanes = slice(128 * p, 128 * p + 128)
        out_ref[:, lanes] = pair_attention(q[:, lanes], k[:, lanes], v[:, lanes], None)


def global_layer(side, blocks, weights, before):
    cells, width = blocks[0].shape
    whole = pl.BlockSpec((cells, width), lambda g, c: (0, 0))
    weight = [pl.BlockSpec((width, 256), lambda g, c, t=t: (0, 2 * t + g)) for t in range(3)]
    more = [] if before is None else [before]
    return pl.pallas_call(
        global_kernel,
        out_shape=jax.ShapeDtypeStruct((cells, width), jnp.bfloat16),
        grid_spec=pltpu.PrefetchScalarGridSpec(
            num_scalar_prefetch=1,
            grid=(2,),
            in_specs=[whole] * 5 + weight + [pl.BlockSpec(memory_space=pl.ANY)] * len(more),
            out_specs=pl.BlockSpec((cells, 256), lambda g, c: (0, 2 * c[0] + g)),
            scratch_shapes=[pltpu.VMEM((5 * cells, width), jnp.bfloat16)],
        ),
        input_output_aliases={9: 0} if more else {},
        compiler_params=params(),
        name="global",
    )(side, *blocks, weights, weights, weights, *more)


def pick_kernel(at_ref, o_ref, g_ref, half_ref, again_ref, sems):
    core = at_ref[0]
    side = half_ref.shape[1] // 4
    copies = []
    for t in range(4):
        ref, first = (o_ref, 0) if t == 0 else (g_ref, 2 * side * (t - 1))
        lanes = pl.ds(pl.multiple_of(first + core * side, side), side)
        to = half_ref.at[:, pl.ds(side * t, side)]
        copies.append(pltpu.make_async_copy(ref.at[:, lanes], to, sems.at[t]))
    for copy in copies:
        copy.start()
    for i in range(at_ref.shape[0]):
        again_ref[i] = at_ref[i]
    for copy in copies:
        copy.wait()


def pick(at, o, g):
    rows, columns = o.shape[0], (o.shape[1] + g.shape[1]) // 2
    return pl.pallas_call(
        pick_kernel,
        out_shape=[jax.ShapeDtypeStruct((rows, columns), o.dtype), jax.ShapeDtypeStruct(at.shape, at.dtype)],
        in_specs=[sspec(), anyspec(), anyspec()],
        out_specs=[vspec(), sspec()],
        scratch_shapes=[pltpu.SemaphoreType.DMA((4,))],
        compiler_params=params(),
        name="pick",
    )(at, o, g)


def place_kernel(at_ref, p0, p1, p2, p3, *rest):
    out_o, out_g = rest[-2:]
    rows, side = p0.shape[0], out_o.shape[1]
    for u, ref in enumerate((p0, p1, p2, p3)):
        to = pl.ds(pl.multiple_of(lax.rem(at_ref[2] + u, 4) * rows, rows), rows)
        out_o[to] = ref[:, :side]
        out_g[to] = ref[:, side:]


def place_rows(at, pieces, after):
    rows, columns = pieces[0].shape
    shapes = [jax.ShapeDtypeStruct((rows * 4, c), pieces[0].dtype) for c in (columns // 4, columns * 3 // 4)]
    return pl.pallas_call(
        place_kernel,
        out_shape=shapes,
        in_specs=[sspec()] + [vspec()] * len(pieces) + [anyspec()] * len(after),
        out_specs=[vspec(), vspec()],
        compiler_params=params(),
        name="place",
    )(at, *pieces, *after)


def join_kernel(p0, p1, p2, p3, *rest):
    out_ref = rest[-1]
    rows = p0.shape[0]
    for u, ref in enumerate((p0, p1, p2, p3)):
        out_ref[rows * u : rows * u + rows] = ref[...]


def join(pieces, after):
    rows, columns = pieces[0].shape
    return pl.pallas_call(
        join_kernel,
        out_shape=jax.ShapeDtypeStruct((rows * len(pieces), columns), pieces[0].dtype),
        in_specs=[vspec()] * len(pieces) + [anyspec()] * len(after),
        out_specs=vspec(),
        compiler_params=params(),
        name="join",
    )(*pieces, *after)


def ring(count, by):
    return [(i, (i + by) % count) for i in range(count)]


def body(tokens, query_local, key_local, value_local, position_bias, output_weight, norm_gain, global_weight):
    width = tokens.shape[2]
    half = width // 2
    flat = lambda a: a.reshape(CELLS, width)
    q, k, v, tok = flat(query_local), flat(key_local), flat(value_local), flat(tokens)
    core = lax.axis_index("c")
    lat = lax.axis_index(LAT)
    lat_count = lax.axis_size(LAT)
    lon_count = lax.axis_size(LON)
    xs, zs = lax.axis_size("x"), lax.axis_size("zh")
    x, zh = lax.axis_index("x"), lax.axis_index("zh")
    at = jnp.stack([core, x, zh, lat, jnp.int32(lat_count)]).astype(jnp.int32)
    swap = [(0, 1), (1, 0)]

    up, down = edges(k, v)
    low = lax.ppermute(up, LAT, [(i, i + 1) for i in range(lat_count - 1)])
    high = lax.ppermute(down, LAT, [(i + 1, i) for i in range(lat_count - 1)])
    columns, at = pick(at, output_weight, global_weight)
    pieces = [columns] + [lax.ppermute(columns, "zh", ring(zs, -by)) for by in range(1, zs)]
    bias = bias_table(position_bias, at)

    to_east, to_west = sides(low, high, k, v)
    west = lax.ppermute(to_east, LON, ring(lon_count, 1))
    east = lax.ppermute(to_west, LON, ring(lon_count, -1))

    rows_o, rows_g = place_rows(at, pieces, [bias, to_east, to_west])
    pieces = [rows_o] + [lax.ppermute(rows_o, "x", ring(xs, -by)) for by in range(1, xs)]
    mine_o = join(pieces, [west, east])
    other_o = lax.ppermute(mine_o, "c", swap)
    mine_g = lax.all_gather(rows_g, "x", axis=0, tiled=True)

    local_out = attend(q, k, v, low, high, west, east, bias)
    hidden, normed = project(at, local_out, tok, mine_o, other_o, norm_gain.reshape(1, width))
    behind = lax.ppermute(normed, LON + ("zh",), ring(lon_count * zs, 1))
    blocks = [normed]
    for by in range(1, xs):
        sent = jnp.where(x + by < xs, normed, behind)
        blocks.append(lax.ppermute(sent, "x", ring(xs, by)))
    blocks.append(behind)
    mine_g, *blocks = lax.optimization_barrier((mine_g, *blocks))
    other_g = lax.ppermute(mine_g, "c", swap)
    attended = global_layer(at[:1], blocks, mine_g, None)
    attended = global_layer(1 - at[:1], blocks, other_g, attended)
    return hidden.reshape(tokens.shape), attended.reshape(tokens.shape)


def solution(mesh):
    fine = Mesh(mesh.devices.reshape(2, 8, 2, 4, 4), LON + LAT)
    grid = P(LON, LAT, None)
    return jax.shard_map(
        body,
        mesh=fine,
        in_specs=(grid, grid, grid, grid, P(), P(LAT, None), P(), P(LAT, None)),
        out_specs=(grid, grid),
        check_vma=False,
    )
```

time: 312 us -> 159 us (0.51)
  the two profiles are of different devices: /device:TPU:313 before, /device:TPU:1 now
where the time goes in v1:
time: 159 us
  starting transfers between devices  88.1 us (55%)
  waiting for transfers between devices  24.5 us (15%)
  Pallas kernels  19.8 us (12%)
  between operations  14.4 us (9%)
  local copies, waits for them, and re-layouts  11.9 us (7%)
    ppermute x3, starting transfers between devices, body(): lax.ppermute(columns, 'zh', ring(zs, -by))  21.9 us
    ppermute x1, starting transfers between devices, body(): other_o = lax.ppermute(mine_o, 'c', swap)  21.2 us
    ppermute x3, starting transfers between devices, body(): blocks.append(lax.ppermute(sent, 'x', ring(xs, by)))  14.7 us
    unnamed x43, local copies, waits for them, and re-layouts  11.7 us
    pallas_call x2, Pallas kernels, global_layer(): pl.pallas_call(global_kernel, out_shape=jax.ShapeDtypeStruct((cells, widt...  7.6 us
    ppermute x3, starting transfers between devices, body(): lax.ppermute(rows_o, 'x', ring(xs, -by))  7.2 us
    ppermute x3, waiting for transfers between devices, body(): lax.ppermute(rows_o, 'x', ring(xs, -by))  7.19 us
    ppermute x3, waiting for transfers between devices, body(): lax.ppermute(columns, 'zh', ring(zs, -by))  7.03 us
  transfers between devices with their start and end apart: 17, of which 7 were waited for; matrix products, arithmetic and copies ran while one was open for 1% of the time, Pallas kernels for 9%

profile of v1, /device:TPU:1, one launch (start us, length us, event | category | flops | bytes accessed | tf_op | source)
XLA Modules:
  0.0 158.7 jit_solution(15365400060700741446)
XLA Ops:
  7.2 0.0 all-gather.2.cloned.1.call-start
  7.2 0.9 copy-done.3
  8.1 0.9 copy-done.5
  9.1 1.0 edges.1
  10.1 4.0 %collective-permute-start = (bf16[2,80,1024]{2,1,0:T(8,128)(2,1)S(1)}, bf16[2,80,1024]{2,1,0:T(8,128)(2,1)S(1)}, u32[]{:S(2)}, u32[]{:S(2)}) collective-permute-start(bf16[2,80,1024]{2,1,0:T(8,128)(2,1)S(1)} %get-tuple-element.19), channel_id=1, source_target_pairs={{0,1},{1,2},{2,3},{3,4},{4,5},{5,6},{6,7},{7,8},{8,9},{9,10},{10,1... | collective-permute-start | bytes 983048 | tf_op jit(solution)/shard_map/ppermute | solution.py:414
  14.1 1.3 collective-permute-start.1
  15.4 0.1 stack.19.at_ref
  15.4 1.0 copy-done.14
  16.4 0.9 copy-done.19
  17.3 1.2 pick.1
  18.6 14.5 %collective-permute-start.4 = (bf16[64,2048]{1,0:T(8,128)(2,1)S(1)}, bf16[64,2048]{1,0:T(8,128)(2,1)S(1)}, u32[]{:S(2)}, u32[]{:S(2)}) collective-permute-start(bf16[64,2048]{1,0:T(8,128)(2,1)S(1)} %get-tuple-element.23.p0), channel_id=1, source_target_pairs={{0,12},{4,0},{8,4},{12,8},{1,13},{5,1},{9,5},{13,9},{2,14},{6,2},{... | collective-permute-start | bytes 786440 | tf_op jit(solution)/shard_map/ppermute | solution.py:417
  33.1 3.1 %collective-permute-start.5 = (bf16[64,2048]{1,0:T(8,128)(2,1)S(1)}, bf16[64,2048]{1,0:T(8,128)(2,1)S(1)}, u32[]{:S(2)}, u32[]{:S(2)}) collective-permute-start(bf16[64,2048]{1,0:T(8,128)(2,1)S(1)} %get-tuple-element.23.p0), channel_id=1, source_target_pairs={{0,8},{4,12},{8,0},{12,4},{1,9},{5,13},{9,1},{13,5},{2,10},{6,14},... | collective-permute-start | bytes 786440 | tf_op jit(solution)/shard_map/ppermute | solution.py:417
  36.2 4.3 %collective-permute-start.6 = (bf16[64,2048]{1,0:T(8,128)(2,1)S(1)}, bf16[64,2048]{1,0:T(8,128)(2,1)S(1)}, u32[]{:S(2)}, u32[]{:S(2)}) collective-permute-start(bf16[64,2048]{1,0:T(8,128)(2,1)S(1)} %get-tuple-element.23.p0), channel_id=1, source_target_pairs={{0,4},{4,8},{8,12},{12,0},{1,5},{5,9},{9,13},{13,1},{2,6},{6,10},{... | collective-permute-start | bytes 786440 | tf_op jit(solution)/shard_map/ppermute | solution.py:417
  40.5 0.9 copy.12
  41.4 0.1 reshape.31
  41.6 3.8 %bias.1.bias_ref.rest_0_ = f32[16,96,512]{2,1,0:T(8,128)S(1)} custom-call(s32[5]{0:T(128)S(1)} %get-tuple-element.18.place_ref.at_ref, f32[16,256]{1,0:T(8,128)S(1)} %pad.4.table_ref), custom_call_target="tpu_custom_call" | custom-call | tf_op jit(solution)/shard_map/bias/pallas_call | solution.py:183
  45.4 1.6 %copy-done.1 = f32[16,96,512]{2,1,0:T(8,128)} copy-done((f32[16,96,512]{2,1,0:T(8,128)}, f32[16,96,512]{2,1,0:T(8,128)S(1)}, u32[]{:S(2)}) %copy-start.1) | copy-done | bytes 3145752
  47.1 0.5 sides.1
  47.6 7.0 %collective-permute-done.4.p1 = bf16[64,2048]{1,0:T(8,128)(2,1)S(1)} collective-permute-done((bf16[64,2048]{1,0:T(8,128)(2,1)S(1)}, bf16[64,2048]{1,0:T(8,128)(2,1)S(1)}, u32[]{:S(2)}, u32[]{:S(2)}) %collective-permute-start.4) | collective-permute-done | bytes 262176 | tf_op jit(solution)/shard_map/ppermute | solution.py:417
  54.6 0.6 place.1
  55.3 0.9 copy-done.11
  56.2 0.7 copy-done.15
  56.9 0.0 all-gather.2.cloned.1.call-update
  56.9 5.2 %collective-permute-start.2 = (bf16[2,128,1024]{2,1,0:T(8,128)(2,1)}, bf16[2,128,1024]{2,1,0:T(8,128)(2,1)S(1)}, u32[]{:S(2)}, u32[]{:S(2)}) collective-permute-start(bf16[2,128,1024]{2,1,0:T(8,128)(2,1)} %copy-done.13), channel_id=1, source_target_pairs={{0,16},{16,32},{32,48},{48,64},{64,80},{80,96},{96,112},{112,128},... | collective-permute-start | bytes 1572872 | tf_op jit(solution)/shard_map/ppermute | solution.py:421
  62.2 1.9 %collective-permute-start.3 = (bf16[2,128,1024]{2,1,0:T(8,128)(2,1)}, bf16[2,128,1024]{2,1,0:T(8,128)(2,1)S(1)}, u32[]{:S(2)}, u32[]{:S(2)}) collective-permute-start(bf16[2,128,1024]{2,1,0:T(8,128)(2,1)} %copy-done.12), channel_id=1, source_target_pairs={{0,496},{16,0},{32,16},{48,32},{64,48},{80,64},{96,80},{112,96},{1... | collective-permute-start | bytes 1572872 | tf_op jit(solution)/shard_map/ppermute | solution.py:422
  64.1 2.5 %collective-permute-start.7 = (bf16[256,512]{1,0:T(8,128)(2,1)}, bf16[256,512]{1,0:T(8,128)(2,1)S(1)}, u32[]{:S(2)}, u32[]{:S(2)}) collective-permute-start(bf16[256,512]{1,0:T(8,128)(2,1)} %copy-done.15), channel_id=1, source_target_pairs={{0,3},{1,0},{2,1},{3,2},{4,7},{5,4},{6,5},{7,6},{8,11},{9,8},{10,9... | collective-permute-start | bytes 786440 | tf_op jit(solution)/shard_map/ppermute | solution.py:425
  66.6 1.9 %collective-permute-start.8 = (bf16[256,512]{1,0:T(8,128)(2,1)}, bf16[256,512]{1,0:T(8,128)(2,1)S(1)}, u32[]{:S(2)}, u32[]{:S(2)}) collective-permute-start(bf16[256,512]{1,0:T(8,128)(2,1)} %copy-done.15), channel_id=1, source_target_pairs={{0,2},{1,3},{2,0},{3,1},{4,6},{5,7},{6,4},{7,5},{8,10},{9,11},{10,... | collective-permute-start | bytes 786440 | tf_op jit(solution)/shard_map/ppermute | solution.py:425
  68.5 2.8 %collective-permute-start.9 = (bf16[256,512]{1,0:T(8,128)(2,1)}, bf16[256,512]{1,0:T(8,128)(2,1)S(1)}, u32[]{:S(2)}, u32[]{:S(2)}) collective-permute-start(bf16[256,512]{1,0:T(8,128)(2,1)} %copy-done.15), channel_id=1, source_target_pairs={{0,1},{1,2},{2,3},{3,0},{4,5},{5,6},{6,7},{7,4},{8,9},{9,10},{10,1... | collective-permute-start | bytes 786440 | tf_op jit(solution)/shard_map/ppermute | solution.py:425
  71.3 0.1 collective-permute-done.7.p1
  71.4 4.3 %collective-permute-done.8.p2 = bf16[256,512]{1,0:T(8,128)(2,1)S(1)} collective-permute-done((bf16[256,512]{1,0:T(8,128)(2,1)}, bf16[256,512]{1,0:T(8,128)(2,1)S(1)}, u32[]{:S(2)}, u32[]{:S(2)}) %collective-permute-start.8) | collective-permute-done | bytes 262176 | tf_op jit(solution)/shard_map/ppermute | solution.py:425
  75.7 2.8 %collective-permute-done.9.p3 = bf16[256,512]{1,0:T(8,128)(2,1)S(1)} collective-permute-done((bf16[256,512]{1,0:T(8,128)(2,1)}, bf16[256,512]{1,0:T(8,128)(2,1)S(1)}, u32[]{:S(2)}, u32[]{:S(2)}) %collective-permute-start.9) | collective-permute-done | bytes 262176 | tf_op jit(solution)/shard_map/ppermute | solution.py:425
  78.5 1.0 copy-done.16
  79.5 0.1 join.1.mine_ref
  79.6 21.2 %collective-permute-start.10 = (bf16[1024,512]{1,0:T(8,128)(2,1)S(1)}, bf16[1024,512]{1,0:T(8,128)(2,1)S(1)}, u32[]{:S(2)}, u32[]{:S(2)}) collective-permute-start(bf16[1024,512]{1,0:T(8,128)(2,1)S(1)} %join.1.mine_ref), channel_id=1, source_target_pairs={{0,16},{16,0},{1,17},{17,1},{2,18},{18,2},{3,19},{19,3},{4,20},{20... | collective-permute-start | bytes 3145736 | tf_op jit(solution)/shard_map/ppermute | solution.py:427
  100.8 0.9 copy-done.17
  101.7 3.0 %local.1.x_ref = bf16[96,1024]{1,0:T(8,128)(2,1)S(1)} custom-call(bf16[96,1024]{1,0:T(8,128)(2,1)S(1)} %bitcast.18, bf16[96,1024]{1,0:T(8,128)(2,1)S(1)} %bitcast.14, bf16[96,1024]{1,0:T(8,128)(2,1)S(1)} %bitcast.17, bf16[2,80,1024]{2,1,0:T(8,128)(2,1)S(1)} %copy-done.8, bf16[2,80,1024]{2,1,0:T(8,128)(2,1)S(1)} %copy-done.10, ...), custom_call_target="tpu_custom_call" | custom-call | tf_op jit(solution)/shard_map/local/pallas_call | solution.py:234
  104.8 1.9 %project.1 = (bf16[96,1024]{1,0:T(8,128)(2,1)}, bf16[96,1024]{1,0:T(8,128)(2,1)S(1)}) custom-call(s32[5]{0:T(128)S(1)} %get-tuple-element.18.place_ref.at_ref, bf16[96,1024]{1,0:T(8,128)(2,1)S(1)} %local.1.x_ref, bf16[96,1024]{1,0:T(8,128)(2,1)S(1)} %bitcast.19, bf16[1024,512]{1,0:T(8,128)(2,1)S(1)} %join.1.mine_ref, ...), custom_call_target="tpu_custom_call" | custom-call | tf_op jit(solution)/shard_map/project/pallas_call | solution.py:273
  106.7 6.7 %collective-permute-start.11 = (bf16[96,1024]{1,0:T(8,128)(2,1)S(1)}, bf16[96,1024]{1,0:T(8,128)(2,1)S(1)}, u32[]{:S(2)}, u32[]{:S(2)}) collective-permute-start(bf16[96,1024]{1,0:T(8,128)(2,1)S(1)} %get-tuple-element.28.x0), channel_id=1, source_target_pairs={{0,4},{4,8},{8,12},{12,16},{16,20},{20,24},{24,28},{28,32},{32,36}... | collective-permute-start | bytes 589832 | tf_op jit(solution)/shard_map/ppermute | solution.py:432
  113.5 4.7 %collective-permute-done.11.x4 = bf16[96,1024]{1,0:T(8,128)(2,1)S(1)} collective-permute-done((bf16[96,1024]{1,0:T(8,128)(2,1)S(1)}, bf16[96,1024]{1,0:T(8,128)(2,1)S(1)}, u32[]{:S(2)}, u32[]{:S(2)}) %collective-permute-start.11) | collective-permute-done | bytes 196640 | tf_op jit(solution)/shard_map/ppermute | solution.py:432
  118.2 7.7 %collective-permute-start.12 = (bf16[96,1024]{1,0:T(8,128)(2,1)S(1)}, bf16[96,1024]{1,0:T(8,128)(2,1)S(1)}, u32[]{:S(2)}, u32[]{:S(2)}) collective-permute-start(bf16[96,1024]{1,0:T(8,128)(2,1)S(1)} %get-tuple-element.36), channel_id=1, source_target_pairs={{0,1},{1,2},{2,3},{3,0},{4,5},{5,6},{6,7},{7,4},{8,9},{9,10},{10,1... | collective-permute-start | bytes 589832 | tf_op jit(solution)/shard_map/ppermute | solution.py:436
  125.9 5.1 %collective-permute-start.13 = (bf16[96,1024]{1,0:T(8,128)(2,1)S(1)}, bf16[96,1024]{1,0:T(8,128)(2,1)S(1)}, u32[]{:S(2)}, u32[]{:S(2)}) collective-permute-start(bf16[96,1024]{1,0:T(8,128)(2,1)S(1)} %get-tuple-element.35), channel_id=1, source_target_pairs={{0,2},{1,3},{2,0},{3,1},{4,6},{5,7},{6,4},{7,5},{8,10},{9,11},{10,... | collective-permute-start | bytes 589832 | tf_op jit(solution)/shard_map/ppermute | solution.py:436
  131.0 1.9 %collective-permute-start.14 = (bf16[96,1024]{1,0:T(8,128)(2,1)S(1)}, bf16[96,1024]{1,0:T(8,128)(2,1)S(1)}, u32[]{:S(2)}, u32[]{:S(2)}) collective-permute-start(bf16[96,1024]{1,0:T(8,128)(2,1)S(1)} %get-tuple-element.34), channel_id=1, source_target_pairs={{0,3},{1,0},{2,1},{3,2},{4,7},{5,4},{6,5},{7,6},{8,11},{9,8},{10,9... | collective-permute-start | bytes 589832 | tf_op jit(solution)/shard_map/ppermute | solution.py:436
  132.9 4.3 %collective-permute-done.13.x2 = bf16[96,1024]{1,0:T(8,128)(2,1)S(1)} collective-permute-done((bf16[96,1024]{1,0:T(8,128)(2,1)S(1)}, bf16[96,1024]{1,0:T(8,128)(2,1)S(1)}, u32[]{:S(2)}, u32[]{:S(2)}) %collective-permute-start.13) | collective-permute-done | bytes 196640 | tf_op jit(solution)/shard_map/ppermute | solution.py:436
  137.3 1.2 collective-permute-done.14.x3
  138.5 3.9 %collective-permute-start.15 = (bf16[1024,1536]{1,0:T(8,128)(2,1)}, bf16[1024,1536]{1,0:T(8,128)(2,1)S(1)}, u32[]{:S(2)}, u32[]{:S(2)}) collective-permute-start(bf16[1024,1536]{1,0:T(8,128)(2,1)} %all-gather.2.cloned.1.call-done.wq.wk.wv), channel_id=1, source_target_pairs={{0,16},{16,0},{1,17},{17,1},{2,18},{18,2},{3,19},{19,3},{4,20},{20... | collective-permute-start | bytes 9437192 | tf_op jit(solution)/shard_map/ppermute | solution.py:439
  142.4 1.9 %copy-done = bf16[1024,1536]{1,0:T(8,128)(2,1)S(1)} copy-done((bf16[1024,1536]{1,0:T(8,128)(2,1)S(1)}, bf16[1024,1536]{1,0:T(8,128)(2,1)}, u32[]{:S(2)}) %copy-start) | copy-done | bytes 3145752
  144.3 3.8 %global.2.rest_0_ = bf16[96,1024]{1,0:T(8,128)(2,1)} custom-call(s32[1]{0:T(128)S(1)} %bitcast.21, bf16[96,1024]{1,0:T(8,128)(2,1)S(1)} %get-tuple-element.28.x0, bf16[96,1024]{1,0:T(8,128)(2,1)S(1)} %collective-permute-done.12.x1, bf16[96,1024]{1,0:T(8,128)(2,1)S(1)} %collective-permute-done.13.x2, bf16[96,1024]{1,0:T(8,128)(2,1)S(1)} %collective-permute-done.14.x3, ...), custom_call_target="tpu_custom_call" | custom-call | tf_op jit(solution)/shard_map/global/pallas_call | solution.py:308
  148.1 3.8 %global.3 = bf16[96,1024]{1,0:T(8,128)(2,1)} custom-call(s32[1]{0:T(128)S(6)} %sub.3.side_ref, bf16[96,1024]{1,0:T(8,128)(2,1)S(1)} %get-tuple-element.28.x0, bf16[96,1024]{1,0:T(8,128)(2,1)S(1)} %collective-permute-done.12.x1, bf16[96,1024]{1,0:T(8,128)(2,1)S(1)} %collective-permute-done.13.x2, ...), custom_call_target="tpu_custom_call", output_to_operand_aliasing={{}: (9, {})} | custom-call | tf_op jit(solution)/shard_map/global/pallas_call | solution.py:308
  (44 shorter events, 0.1 us)
Async XLA Ops:
  7.2 131.3 %all-gather.2.cloned.1.call-start = ((), (), s32[]{:S(2)}) async-start(), calls=%async_computation | async-start | bytes 3932160 | tf_op jit(solution)/shard_map/all_gather | solution.py:428
  7.2 0.9 copy-start.3
  8.1 0.9 copy-start.5
  9.1 38.0 %copy-start.4 = (bf16[12,8,1024]{2,1,0:T(8,128)(2,1)S(1)}, bf16[12,8,1024]{2,1,0:T(8,128)(2,1)}, u32[]{:S(2)}) copy-start(bf16[12,8,1024]{2,1,0:T(8,128)(2,1)} %param.10) | copy-start | bytes 589828
  9.1 38.0 %copy-start.6 = (bf16[12,8,1024]{2,1,0:T(8,128)(2,1)S(1)}, bf16[12,8,1024]{2,1,0:T(8,128)(2,1)}, u32[]{:S(2)}) copy-start(bf16[12,8,1024]{2,1,0:T(8,128)(2,1)} %param.11) | copy-start | bytes 589828
  10.1 37.0 %collective-permute-start = (bf16[2,80,1024]{2,1,0:T(8,128)(2,1)S(1)}, bf16[2,80,1024]{2,1,0:T(8,128)(2,1)S(1)}, u32[]{:S(2)}, u32[]{:S(2)}) collective-permute-start(bf16[2,80,1024]{2,1,0:T(8,128)(2,1)S(1)} %get-tuple-element.19), channel_id=1, source_target_pairs={{0,1},{1,2},{2,3},{3,4},{4,5},{5,6},{6,7},{7,8},{8,9},{9,10},{10,1... | collective-permute-start | bytes 983048 | tf_op jit(solution)/shard_map/ppermute | solution.py:414
  14.1 33.0 %collective-permute-start.1 = (bf16[2,80,1024]{2,1,0:T(8,128)(2,1)S(1)}, bf16[2,80,1024]{2,1,0:T(8,128)(2,1)S(1)}, u32[]{:S(2)}, u32[]{:S(2)}) collective-permute-start(bf16[2,80,1024]{2,1,0:T(8,128)(2,1)S(1)} %get-tuple-element.20), channel_id=1, source_target_pairs={{1,0},{2,1},{3,2},{4,3},{5,4},{6,5},{7,6},{8,7},{9,8},{10,9},{11,1... | collective-permute-start | bytes 983048 | tf_op jit(solution)/shard_map/ppermute | solution.py:415
  15.4 1.0 copy-start.14
  16.4 0.9 copy-start.19
  18.6 36.0 %collective-permute-start.4 = (bf16[64,2048]{1,0:T(8,128)(2,1)S(1)}, bf16[64,2048]{1,0:T(8,128)(2,1)S(1)}, u32[]{:S(2)}, u32[]{:S(2)}) collective-permute-start(bf16[64,2048]{1,0:T(8,128)(2,1)S(1)} %get-tuple-element.23.p0), channel_id=1, source_target_pairs={{0,12},{4,0},{8,4},{12,8},{1,13},{5,1},{9,5},{13,9},{2,14},{6,2},{... | collective-permute-start | bytes 786440 | tf_op jit(solution)/shard_map/ppermute | solution.py:417
  33.1 21.5 %collective-permute-start.5 = (bf16[64,2048]{1,0:T(8,128)(2,1)S(1)}, bf16[64,2048]{1,0:T(8,128)(2,1)S(1)}, u32[]{:S(2)}, u32[]{:S(2)}) collective-permute-start(bf16[64,2048]{1,0:T(8,128)(2,1)S(1)} %get-tuple-element.23.p0), channel_id=1, source_target_pairs={{0,8},{4,12},{8,0},{12,4},{1,9},{5,13},{9,1},{13,5},{2,10},{6,14},... | collective-permute-start | bytes 786440 | tf_op jit(solution)/shard_map/ppermute | solution.py:417
  36.2 18.4 %collective-permute-start.6 = (bf16[64,2048]{1,0:T(8,128)(2,1)S(1)}, bf16[64,2048]{1,0:T(8,128)(2,1)S(1)}, u32[]{:S(2)}, u32[]{:S(2)}) collective-permute-start(bf16[64,2048]{1,0:T(8,128)(2,1)S(1)} %get-tuple-element.23.p0), channel_id=1, source_target_pairs={{0,4},{4,8},{8,12},{12,0},{1,5},{5,9},{9,13},{13,1},{2,6},{6,10},{... | collective-permute-start | bytes 786440 | tf_op jit(solution)/shard_map/ppermute | solution.py:417
  45.4 1.7 %copy-start.1 = (f32[16,96,512]{2,1,0:T(8,128)}, f32[16,96,512]{2,1,0:T(8,128)S(1)}, u32[]{:S(2)}) copy-start(f32[16,96,512]{2,1,0:T(8,128)S(1)} %bias.1.bias_ref.rest_0_) | copy-start | bytes 9437188
  47.1 7.6 %copy-start.7 = (bf16[2,80,1024]{2,1,0:T(8,128)(2,1)}, bf16[2,80,1024]{2,1,0:T(8,128)(2,1)S(1)}, u32[]{:S(2)}) copy-start(bf16[2,80,1024]{2,1,0:T(8,128)(2,1)S(1)} %collective-permute-done.low_ref) | copy-start | bytes 983044
  47.1 7.5 %copy-start.9 = (bf16[2,80,1024]{2,1,0:T(8,128)(2,1)}, bf16[2,80,1024]{2,1,0:T(8,128)(2,1)S(1)}, u32[]{:S(2)}) copy-start(bf16[2,80,1024]{2,1,0:T(8,128)(2,1)S(1)} %collective-permute-done.1.high_ref) | copy-start | bytes 983044
  47.6 7.7 %copy-start.12 = (bf16[2,128,1024]{2,1,0:T(8,128)(2,1)}, bf16[2,128,1024]{2,1,0:T(8,128)(2,1)S(1)}, u32[]{:S(2)}) copy-start(bf16[2,128,1024]{2,1,0:T(8,128)(2,1)S(1)} %get-tuple-element.22.rest_2_) | copy-start | bytes 1572868
  47.6 7.7 %copy-start.13 = (bf16[2,128,1024]{2,1,0:T(8,128)(2,1)}, bf16[2,128,1024]{2,1,0:T(8,128)(2,1)S(1)}, u32[]{:S(2)}) copy-start(bf16[2,128,1024]{2,1,0:T(8,128)(2,1)S(1)} %get-tuple-element.21.rest_1_) | copy-start | bytes 1572868
  55.3 0.9 copy-start.11
  56.2 0.7 copy-start.15
  56.9 43.9 %copy-start.2 = (f32[16,96,512]{2,1,0:T(8,128)S(1)}, f32[16,96,512]{2,1,0:T(8,128)}, u32[]{:S(2)}) copy-start(f32[16,96,512]{2,1,0:T(8,128)} %copy-done.1) | copy-start | bytes 9437188
  56.9 43.9 %copy-start.8 = (bf16[2,80,1024]{2,1,0:T(8,128)(2,1)S(1)}, bf16[2,80,1024]{2,1,0:T(8,128)(2,1)}, u32[]{:S(2)}) copy-start(bf16[2,80,1024]{2,1,0:T(8,128)(2,1)} %copy-done.7) | copy-start | bytes 983044
  56.9 43.9 %copy-start.10 = (bf16[2,80,1024]{2,1,0:T(8,128)(2,1)S(1)}, bf16[2,80,1024]{2,1,0:T(8,128)(2,1)}, u32[]{:S(2)}) copy-start(bf16[2,80,1024]{2,1,0:T(8,128)(2,1)} %copy-done.9) | copy-start | bytes 983044
  56.9 21.6 %collective-permute-start.2 = (bf16[2,128,1024]{2,1,0:T(8,128)(2,1)}, bf16[2,128,1024]{2,1,0:T(8,128)(2,1)S(1)}, u32[]{:S(2)}, u32[]{:S(2)}) collective-permute-start(bf16[2,128,1024]{2,1,0:T(8,128)(2,1)} %copy-done.13), channel_id=1, source_target_pairs={{0,16},{16,32},{32,48},{48,64},{64,80},{80,96},{96,112},{112,128},... | collective-permute-start | bytes 1572872 | tf_op jit(solution)/shard_map/ppermute | solution.py:421
  62.2 16.4 %collective-permute-start.3 = (bf16[2,128,1024]{2,1,0:T(8,128)(2,1)}, bf16[2,128,1024]{2,1,0:T(8,128)(2,1)S(1)}, u32[]{:S(2)}, u32[]{:S(2)}) collective-permute-start(bf16[2,128,1024]{2,1,0:T(8,128)(2,1)} %copy-done.12), channel_id=1, source_target_pairs={{0,496},{16,0},{32,16},{48,32},{64,48},{80,64},{96,80},{112,96},{1... | collective-permute-start | bytes 1572872 | tf_op jit(solution)/shard_map/ppermute | solution.py:422
  64.1 7.3 %collective-permute-start.7 = (bf16[256,512]{1,0:T(8,128)(2,1)}, bf16[256,512]{1,0:T(8,128)(2,1)S(1)}, u32[]{:S(2)}, u32[]{:S(2)}) collective-permute-start(bf16[256,512]{1,0:T(8,128)(2,1)} %copy-done.15), channel_id=1, source_target_pairs={{0,3},{1,0},{2,1},{3,2},{4,7},{5,4},{6,5},{7,6},{8,11},{9,8},{10,9... | collective-permute-start | bytes 786440 | tf_op jit(solution)/shard_map/ppermute | solution.py:425
  66.6 9.1 %collective-permute-start.8 = (bf16[256,512]{1,0:T(8,128)(2,1)}, bf16[256,512]{1,0:T(8,128)(2,1)S(1)}, u32[]{:S(2)}, u32[]{:S(2)}) collective-permute-start(bf16[256,512]{1,0:T(8,128)(2,1)} %copy-done.15), channel_id=1, source_target_pairs={{0,2},{1,3},{2,0},{3,1},{4,6},{5,7},{6,4},{7,5},{8,10},{9,11},{10,... | collective-permute-start | bytes 786440 | tf_op jit(solution)/shard_map/ppermute | solution.py:425
  68.5 10.0 %collective-permute-start.9 = (bf16[256,512]{1,0:T(8,128)(2,1)}, bf16[256,512]{1,0:T(8,128)(2,1)S(1)}, u32[]{:S(2)}, u32[]{:S(2)}) collective-permute-start(bf16[256,512]{1,0:T(8,128)(2,1)} %copy-done.15), channel_id=1, source_target_pairs={{0,1},{1,2},{2,3},{3,0},{4,5},{5,6},{6,7},{7,4},{8,9},{9,10},{10,1... | collective-permute-start | bytes 786440 | tf_op jit(solution)/shard_map/ppermute | solution.py:425
  78.5 1.0 copy-start.16
  79.5 25.3 %copy-start.20 = (f32[1024]{0:T(1024)S(1)}, f32[1024]{0:T(1024)}, u32[]{:S(2)}) copy-start(f32[1024]{0:T(1024)} %param.14) | copy-start | bytes 12292
  79.6 25.2 %collective-permute-start.10 = (bf16[1024,512]{1,0:T(8,128)(2,1)S(1)}, bf16[1024,512]{1,0:T(8,128)(2,1)S(1)}, u32[]{:S(2)}, u32[]{:S(2)}) collective-permute-start(bf16[1024,512]{1,0:T(8,128)(2,1)S(1)} %join.1.mine_ref), channel_id=1, source_target_pairs={{0,16},{16,0},{1,17},{17,1},{2,18},{18,2},{3,19},{19,3},{4,20},{20... | collective-permute-start | bytes 3145736 | tf_op jit(solution)/shard_map/ppermute | solution.py:427
  100.8 0.9 copy-start.17
  101.7 3.0 %copy-start.18 = (bf16[12,8,1024]{2,1,0:T(8,128)(2,1)S(1)}, bf16[12,8,1024]{2,1,0:T(8,128)(2,1)}, u32[]{:S(2)}) copy-start(bf16[12,8,1024]{2,1,0:T(8,128)(2,1)} %param.8) | copy-start | bytes 589828
  106.7 11.5 %collective-permute-start.11 = (bf16[96,1024]{1,0:T(8,128)(2,1)S(1)}, bf16[96,1024]{1,0:T(8,128)(2,1)S(1)}, u32[]{:S(2)}, u32[]{:S(2)}) collective-permute-start(bf16[96,1024]{1,0:T(8,128)(2,1)S(1)} %get-tuple-element.28.x0), channel_id=1, source_target_pairs={{0,4},{4,8},{8,12},{12,16},{16,20},{20,24},{24,28},{28,32},{32,36}... | collective-permute-start | bytes 589832 | tf_op jit(solution)/shard_map/ppermute | solution.py:432
  118.2 14.7 %collective-permute-start.12 = (bf16[96,1024]{1,0:T(8,128)(2,1)S(1)}, bf16[96,1024]{1,0:T(8,128)(2,1)S(1)}, u32[]{:S(2)}, u32[]{:S(2)}) collective-permute-start(bf16[96,1024]{1,0:T(8,128)(2,1)S(1)} %get-tuple-element.36), channel_id=1, source_target_pairs={{0,1},{1,2},{2,3},{3,0},{4,5},{5,6},{6,7},{7,4},{8,9},{9,10},{10,1... | collective-permute-start | bytes 589832 | tf_op jit(solution)/shard_map/ppermute | solution.py:436
  125.9 11.4 %collective-permute-start.13 = (bf16[96,1024]{1,0:T(8,128)(2,1)S(1)}, bf16[96,1024]{1,0:T(8,128)(2,1)S(1)}, u32[]{:S(2)}, u32[]{:S(2)}) collective-permute-start(bf16[96,1024]{1,0:T(8,128)(2,1)S(1)} %get-tuple-element.35), channel_id=1, source_target_pairs={{0,2},{1,3},{2,0},{3,1},{4,6},{5,7},{6,4},{7,5},{8,10},{9,11},{10,... | collective-permute-start | bytes 589832 | tf_op jit(solution)/shard_map/ppermute | solution.py:436
  131.0 7.5 %collective-permute-start.14 = (bf16[96,1024]{1,0:T(8,128)(2,1)S(1)}, bf16[96,1024]{1,0:T(8,128)(2,1)S(1)}, u32[]{:S(2)}, u32[]{:S(2)}) collective-permute-start(bf16[96,1024]{1,0:T(8,128)(2,1)S(1)} %get-tuple-element.34), channel_id=1, source_target_pairs={{0,3},{1,0},{2,1},{3,2},{4,7},{5,4},{6,5},{7,6},{8,11},{9,8},{10,9... | collective-permute-start | bytes 589832 | tf_op jit(solution)/shard_map/ppermute | solution.py:436
  138.5 9.7 %collective-permute-start.15 = (bf16[1024,1536]{1,0:T(8,128)(2,1)}, bf16[1024,1536]{1,0:T(8,128)(2,1)S(1)}, u32[]{:S(2)}, u32[]{:S(2)}) collective-permute-start(bf16[1024,1536]{1,0:T(8,128)(2,1)} %all-gather.2.cloned.1.call-done.wq.wk.wv), channel_id=1, source_target_pairs={{0,16},{16,0},{1,17},{17,1},{2,18},{18,2},{3,19},{19,3},{4,20},{20... | collective-permute-start | bytes 9437192 | tf_op jit(solution)/shard_map/ppermute | solution.py:439
  142.4 1.9 %copy-start = (bf16[1024,1536]{1,0:T(8,128)(2,1)S(1)}, bf16[1024,1536]{1,0:T(8,128)(2,1)}, u32[]{:S(2)}) copy-start(bf16[1024,1536]{1,0:T(8,128)(2,1)} %all-gather.2.cloned.1.call-done.wq.wk.wv) | copy-start | bytes 9437188
Sparse Core Ops, SparseCore 0:
  57.0 56.8 all-gather.1

commit v2 on v1

--- a/solution.py
+++ b/solution.py
@@ -18,11 +18,11 @@
 HALF = 40
 KEYS = 512
 NEG = -1e30
-VMEM = 48 * 1024 * 1024
-
-
-def params():
-    return pltpu.CompilerParams(vmem_limit_bytes=VMEM)
+MIB = 1024 * 1024
+
+
+def params(mib):
+    return pltpu.CompilerParams(vmem_limit_bytes=mib * MIB)
 
 
 def vspec():
@@ -65,12 +65,12 @@
         in_specs=[anyspec()] * 2,
         out_specs=(vspec(), vspec()),
         scratch_shapes=[pltpu.VMEM((2,) + k.shape, jnp.bfloat16), pltpu.SemaphoreType.DMA((2,))],
-        compiler_params=params(),
+        compiler_params=params(6),
         name="edges",
     )(k, v)
 
 
-def side_kernel(low_ref, high_ref, k_ref, v_ref, east_ref, west_ref, rows):
+def side_kernel(low_ref, high_ref, k_ref, v_ref, after_ref, east_ref, west_ref, rows):
     row = lax.broadcasted_iota(jnp.int32, (128, 256), 0)
     col = lax.broadcasted_iota(jnp.int32, (128, 256), 1)
     low = row < HALF
@@ -88,17 +88,17 @@
         west_ref[at] = jnp.dot(pick_first, x, preferred_element_type=jnp.float32).astype(jnp.bfloat16)
 
 
-def sides(low, high, k, v):
+def sides(low, high, k, v, after):
     shape = jax.ShapeDtypeStruct((2, 128, k.shape[1]), jnp.bfloat16)
     return pl.pallas_call(
         side_kernel,
         out_shape=(shape, shape),
-        in_specs=[vspec()] * 4,
+        in_specs=[vspec()] * 4 + [anyspec()],
         out_specs=(vspec(), vspec()),
         scratch_shapes=[pltpu.VMEM((256, k.shape[1]), jnp.bfloat16)],
-        compiler_params=params(),
+        compiler_params=params(6),
         name="sides",
-    )(low, high, k, v)
+    )(low, high, k, v, after)
 
 
 def key_places(shape, dim):
@@ -185,7 +185,7 @@
         out_shape=jax.ShapeDtypeStruct((heads, CELLS, KEYS), jnp.float32),
         in_specs=[sspec(), vspec()],
         out_specs=vspec(),
-        compiler_params=params(),
+        compiler_params=params(12),
         name="bias",
     )(place, table)
 
@@ -240,25 +240,32 @@
             pltpu.VMEM((KEYS, width), jnp.bfloat16),
             pltpu.VMEM((KEYS, width), jnp.bfloat16),
         ],
-        compiler_params=params(),
+        compiler_params=params(16),
         name="local",
     )(q, k, v, low, high, west, east, bias)
 
 
-def project_kernel(at_ref, x_ref, tok_ref, mine_ref, other_ref, gain_ref, hid_ref, norm_ref, pbuf):
+def piece_lanes(at_ref, deep):
+    core, x = at_ref[0], at_ref[1]
+    half = deep // 2
+    far = lax.rem(x + 2, 4) * deep
+    starts = (
+        x * deep,
+        lax.rem(x + 3 + 2 * core, 4) * deep,
+        lax.rem(x + 5 - 2 * core, 4) * deep,
+        far + core * half,
+        far + (1 - core) * half,
+    )
+    return [pl.ds(pl.multiple_of(start, half), deep if n < 3 else half) for n, start in enumerate(starts)]
+
+
+def project_kernel(at_ref, x_ref, tok_ref, gain_ref, p0, p1, p2, p3, p4, hid_ref, norm_ref):
     width = x_ref.shape[1]
-    core, xpos = at_ref[0], at_ref[1]
-    side = width // 2
-    deep = width // 4
-    for ref, where in ((mine_ref, core), (other_ref, 1 - core)):
-        total = jnp.zeros((CELLS, side), jnp.float32)
-        for u in range(4):
-            lanes = pl.ds(pl.multiple_of(lax.rem(xpos + u, 4) * deep, deep), deep)
-            total += jnp.dot(
-                x_ref[:, lanes], ref[deep * u : deep * u + deep], preferred_element_type=jnp.float32
-            )
-        pbuf[:, pl.ds(pl.multiple_of(where * side, side), side)] = total
-    hidden = (tok_ref[...].astype(jnp.float32) + pbuf[...]).astype(jnp.bfloat16)
+    total = None
+    for lanes, ref in zip(piece_lanes(at_ref, width // 4), (p0, p1, p2, p3, p4)):
+        term = jnp.dot(x_ref[:, lanes], ref[...], preferred_element_type=jnp.float32)
+        total = term if total is None else total + term
+    hidden = (tok_ref[...].astype(jnp.float32) + total).astype(jnp.bfloat16)
     hid_ref[...] = hidden
     wide = hidden.astype(jnp.float32)
     inverse = lax.rsqrt(jnp.mean(wide * wide, axis=1, keepdims=True) + 1e-06)
@@ -268,68 +275,72 @@
         norm_ref[:, at : at + 64] = normed[:, 64 * chunk : 64 * chunk + 64]
 
 
-def project(at, x, tok, mine, other, gain):
+def project(at, x, tok, gain, pieces):
     shape = jax.ShapeDtypeStruct(x.shape, jnp.bfloat16)
     return pl.pallas_call(
         project_kernel,
         out_shape=(shape, shape),
-        in_specs=[sspec()] + [vspec()] * 5,
+        in_specs=[sspec()] + [vspec()] * (3 + len(pieces)),
         out_specs=(vspec(), vspec()),
-        scratch_shapes=[pltpu.VMEM(x.shape, jnp.float32)],
-        compiler_params=params(),
+        compiler_params=params(8),
         name="project",
-    )(at, x, tok, mine, other, gain)
-
-
-def global_kernel(side_ref, x0, x1, x2, x3, x4, wq, wk, wv, *rest):
-    out_ref, xbuf = rest[-2:]
+    )(at, x, tok, gain, *pieces)
+
+
+def global_kernel(at_ref, x0, x1, x2, x3, x4, *rest):
+    weights, (out_ref, xbuf) = rest[:15], rest[15:]
+    width = x0.shape[1]
 
     @pl.when(pl.program_id(0) == 0)
     def _():
         for at, ref in enumerate((x0, x1, x2, x3, x4)):
             xbuf[CELLS * at : CELLS * at + CELLS] = ref[...]
 
-    def part(rows, w):
-        return jnp.dot(rows, w[...], preferred_element_type=jnp.float32).astype(jnp.bfloat16)
-
-    q = part(xbuf[0:CELLS], wq) * jnp.bfloat16(0.125)
-    k = part(xbuf[...], wk)
-    v = part(xbuf[...], wv)
+    spans = piece_lanes(at_ref, width // 4)
+
+    def part(rows, refs):
+        total = None
+        for lanes, ref in zip(spans, refs):
+            term = jnp.dot(xbuf[0:rows, lanes], ref[...], preferred_element_type=jnp.float32)
+            total = term if total is None else total + term
+        return total.astype(jnp.bfloat16)
+
+    q = part(CELLS, weights[0:5]) * jnp.bfloat16(0.125)
+    k = part(5 * CELLS, weights[5:10])
+    v = part(5 * CELLS, weights[10:15])
     for p in range(q.shape[1] // 128):
         lanes = slice(128 * p, 128 * p + 128)
         out_ref[:, lanes] = pair_attention(q[:, lanes], k[:, lanes], v[:, lanes], None)
 
 
-def global_layer(side, blocks, weights, before):
+def global_layer(at, blocks, pieces):
     cells, width = blocks[0].shape
+    steps = width // 256
     whole = pl.BlockSpec((cells, width), lambda g, c: (0, 0))
-    weight = [pl.BlockSpec((width, 256), lambda g, c, t=t: (0, 2 * t + g)) for t in range(3)]
-    more = [] if before is None else [before]
+    weights = [
+        pl.BlockSpec((piece.shape[0], 256), lambda g, c, t=t: (0, steps * t + g)) for t in range(3) for piece in pieces
+    ]
     return pl.pallas_call(
         global_kernel,
         out_shape=jax.ShapeDtypeStruct((cells, width), jnp.bfloat16),
         grid_spec=pltpu.PrefetchScalarGridSpec(
             num_scalar_prefetch=1,
-            grid=(2,),
-            in_specs=[whole] * 5 + weight + [pl.BlockSpec(memory_space=pl.ANY)] * len(more),
-            out_specs=pl.BlockSpec((cells, 256), lambda g, c: (0, 2 * c[0] + g)),
+            grid=(steps,),
+            in_specs=[whole] * 5 + weights,
+            out_specs=pl.BlockSpec((cells, 256), lambda g, c: (0, g)),
             scratch_shapes=[pltpu.VMEM((5 * cells, width), jnp.bfloat16)],
         ),
-        input_output_aliases={9: 0} if more else {},
-        compiler_params=params(),
+        compiler_params=params(20),
         name="global",
-    )(side, *blocks, weights, weights, weights, *more)
-
-
-def pick_kernel(at_ref, o_ref, g_ref, half_ref, again_ref, sems):
-    core = at_ref[0]
-    side = half_ref.shape[1] // 4
-    copies = []
-    for t in range(4):
-        ref, first = (o_ref, 0) if t == 0 else (g_ref, 2 * side * (t - 1))
-        lanes = pl.ds(pl.multiple_of(first + core * side, side), side)
-        to = half_ref.at[:, pl.ds(side * t, side)]
-        copies.append(pltpu.make_async_copy(ref.at[:, lanes], to, sems.at[t]))
+    )(at, *blocks, *(pieces * 3))
+
+
+def pick_kernel(at_ref, o_ref, g_ref, after_ref, out_ref, again_ref, sems):
+    side = o_ref.shape[1]
+    copies = [
+        pltpu.make_async_copy(o_ref, out_ref.at[:, pl.ds(0, side)], sems.at[0]),
+        pltpu.make_async_copy(g_ref, out_ref.at[:, pl.ds(side, g_ref.shape[1])], sems.at[1]),
+    ]
     for copy in copies:
         copy.start()
     for i in range(at_ref.shape[0]):
@@ -338,58 +349,72 @@
         copy.wait()
 
 
-def pick(at, o, g):
-    rows, columns = o.shape[0], (o.shape[1] + g.shape[1]) // 2
+def pick(at, o, g, after):
+    shape = jax.ShapeDtypeStruct((o.shape[0], o.shape[1] + g.shape[1]), o.dtype)
     return pl.pallas_call(
         pick_kernel,
-        out_shape=[jax.ShapeDtypeStruct((rows, columns), o.dtype), jax.ShapeDtypeStruct(at.shape, at.dtype)],
-        in_specs=[sspec(), anyspec(), anyspec()],
+        out_shape=[shape, jax.ShapeDtypeStruct(at.shape, at.dtype)],
+        in_specs=[sspec()] + [anyspec()] * 3,
         out_specs=[vspec(), sspec()],
-        scratch_shapes=[pltpu.SemaphoreType.DMA((4,))],
-        compiler_params=params(),
+        scratch_shapes=[pltpu.SemaphoreType.DMA((2,))],
+        compiler_params=params(4),
         name="pick",
-    )(at, o, g)
-
-
-def place_kernel(at_ref, p0, p1, p2, p3, *rest):
-    out_o, out_g = rest[-2:]
-    rows, side = p0.shape[0], out_o.shape[1]
-    for u, ref in enumerate((p0, p1, p2, p3)):
-        to = pl.ds(pl.multiple_of(lax.rem(at_ref[2] + u, 4) * rows, rows), rows)
-        out_o[to] = ref[:, :side]
-        out_g[to] = ref[:, side:]
-
-
-def place_rows(at, pieces, after):
-    rows, columns = pieces[0].shape
-    shapes = [jax.ShapeDtypeStruct((rows * 4, c), pieces[0].dtype) for c in (columns // 4, columns * 3 // 4)]
-    return pl.pallas_call(
-        place_kernel,
-        out_shape=shapes,
+    )(at, o, g, after)
+
+
+def place_kernel(at_ref, p0, p1, p2, p3, p4, *rest, first):
+    out_ref = rest[-1]
+    rows, side = p0.shape[0], out_ref.shape[1]
+    half = rows // 2
+    core, zh = at_ref[0], at_ref[2]
+    far = lax.rem(zh + 2, 4) * rows
+    starts = (
+        zh * rows,
+        lax.rem(zh + 3 + 2 * core, 4) * rows,
+        lax.rem(zh + 5 - 2 * core, 4) * rows,
+        far + core * half,
+        far + (1 - core) * half,
+    )
+    for start, ref in zip(starts, (p0, p1, p2, p3, p4)):
+        to = pl.ds(pl.multiple_of(start, half), ref.shape[0])
+        out_ref[to] = ref[:, first : first + side]
+
+
+def place_rows(at, pieces, first, count, after):
+    rows = pieces[0].shape[0]
+    return pl.pallas_call(
+        functools.partial(place_kernel, first=first),
+        out_shape=jax.ShapeDtypeStruct((rows * 4, count), pieces[0].dtype),
         in_specs=[sspec()] + [vspec()] * len(pieces) + [anyspec()] * len(after),
-        out_specs=[vspec(), vspec()],
-        compiler_params=params(),
+        out_specs=vspec(),
+        compiler_params=params(8),
         name="place",
     )(at, *pieces, *after)
 
 
-def join_kernel(p0, p1, p2, p3, *rest):
+def half_kernel(at_ref, x_ref, *rest):
     out_ref = rest[-1]
-    rows = p0.shape[0]
-    for u, ref in enumerate((p0, p1, p2, p3)):
-        out_ref[rows * u : rows * u + rows] = ref[...]
-
-
-def join(pieces, after):
-    rows, columns = pieces[0].shape
-    return pl.pallas_call(
-        join_kernel,
-        out_shape=jax.ShapeDtypeStruct((rows * len(pieces), columns), pieces[0].dtype),
-        in_specs=[vspec()] * len(pieces) + [anyspec()] * len(after),
+    rows = out_ref.shape[0]
+    out_ref[...] = x_ref[pl.ds(pl.multiple_of(at_ref[0] * rows, rows), rows)]
+
+
+def half_of(at, x, after):
+    return pl.pallas_call(
+        half_kernel,
+        out_shape=jax.ShapeDtypeStruct((x.shape[0] // 2, x.shape[1]), x.dtype),
+        in_specs=[sspec(), vspec()] + [anyspec()] * len(after),
         out_specs=vspec(),
-        compiler_params=params(),
-        name="join",
-    )(*pieces, *after)
+        compiler_params=params(8),
+        name="half",
+    )(at, x, *after)
+
+
+def gathered(rows, axis, at, after):
+    roles = [(i, (i + 1) % 4) for i in range(4)] + [(4 + i, 4 + (i + 3) % 4) for i in range(4)]
+    swap = [(0, 1), (1, 0)]
+    near = lax.ppermute(rows, ("c", axis), roles)
+    far = lax.ppermute(half_of(at, near, after), ("c", axis), roles)
+    return [rows, near, lax.ppermute(near, "c", swap), far, lax.ppermute(far, "c", swap)]
 
 
 def ring(count, by):
@@ -398,7 +423,6 @@
 
 def body(tokens, query_local, key_local, value_local, position_bias, output_weight, norm_gain, global_weight):
     width = tokens.shape[2]
-    half = width // 2
     flat = lambda a: a.reshape(CELLS, width)
     q, k, v, tok = flat(query_local), flat(key_local), flat(value_local), flat(tokens)
     core = lax.axis_index("c")
@@ -408,37 +432,28 @@
     xs, zs = lax.axis_size("x"), lax.axis_size("zh")
     x, zh = lax.axis_index("x"), lax.axis_index("zh")
     at = jnp.stack([core, x, zh, lat, jnp.int32(lat_count)]).astype(jnp.int32)
-    swap = [(0, 1), (1, 0)]
-
     up, down = edges(k, v)
     low = lax.ppermute(up, LAT, [(i, i + 1) for i in range(lat_count - 1)])
     high = lax.ppermute(down, LAT, [(i + 1, i) for i in range(lat_count - 1)])
-    columns, at = pick(at, output_weight, global_weight)
-    pieces = [columns] + [lax.ppermute(columns, "zh", ring(zs, -by)) for by in range(1, zs)]
+    weights, at = pick(at, output_weight, global_weight, up)
     bias = bias_table(position_bias, at)
-
-    to_east, to_west = sides(low, high, k, v)
+    to_east, to_west = sides(low, high, k, v, bias)
     west = lax.ppermute(to_east, LON, ring(lon_count, 1))
     east = lax.ppermute(to_west, LON, ring(lon_count, -1))
-
-    rows_o, rows_g = place_rows(at, pieces, [bias, to_east, to_west])
-    pieces = [rows_o] + [lax.ppermute(rows_o, "x", ring(xs, -by)) for by in range(1, xs)]
-    mine_o = join(pieces, [west, east])
-    other_o = lax.ppermute(mine_o, "c", swap)
-    mine_g = lax.all_gather(rows_g, "x", axis=0, tiled=True)
-
+    pieces = gathered(weights, "zh", at, [])
+    rows_o = place_rows(at, pieces, 0, width, [west, east])
+    pieces_o = gathered(rows_o, "x", at, [])
     local_out = attend(q, k, v, low, high, west, east, bias)
-    hidden, normed = project(at, local_out, tok, mine_o, other_o, norm_gain.reshape(1, width))
+    rows_g = place_rows(at, pieces, width, 3 * width, [pieces_o[1], local_out])
+    hidden, normed = project(at, local_out, tok, norm_gain.reshape(1, width), pieces_o)
     behind = lax.ppermute(normed, LON + ("zh",), ring(lon_count * zs, 1))
+    pieces_g = gathered(rows_g, "x", at, [behind])
     blocks = [normed]
     for by in range(1, xs):
         sent = jnp.where(x + by < xs, normed, behind)
         blocks.append(lax.ppermute(sent, "x", ring(xs, by)))
     blocks.append(behind)
-    mine_g, *blocks = lax.optimization_barrier((mine_g, *blocks))
-    other_g = lax.ppermute(mine_g, "c", swap)
-    attended = global_layer(at[:1], blocks, mine_g, None)
-    attended = global_layer(1 - at[:1], blocks, other_g, attended)
+    attended = global_layer(at, blocks, pieces_g)
     return hidden.reshape(tokens.shape), attended.reshape(tokens.shape)
 
 

time: 159 us -> 173 us (1.088)
  waiting for transfers between devices: 24.5 us -> 53.6 us
  between operations: 14.4 us -> 0.98 us
  local copies, waits for them, and re-layouts: 11.9 us -> 4.91 us
  Pallas kernels: 19.8 us -> 23.4 us
    ppermute x8 -> x12, waiting for transfers between devices: 14.2 us -> 32.3 us  [the longest x3 24.8 us: gathered(): far = lax.ppermute(half_of(at, near, after), ('c', axis), roles)]
    ppermute x8 -> x12, starting transfers between devices: 54.2 us -> 71.2 us  [the longest x3 28.7 us: gathered(): far = lax.ppermute(half_of(at, near, after), ('c', axis), roles)]
    ppermute x3, starting transfers between devices: 14.7 us -> 7.2 us  [body(): blocks.append(lax.ppermute(sent, 'x', ring(xs, by)))]
    unnamed x43 -> x19, local copies, waits for them, and re-layouts: 11.7 us -> 4.71 us
    ppermute x1, waiting for transfers between devices: 4.72 us -> 11.4 us  [body(): behind = lax.ppermute(normed, LON + ('zh',), ring(lon_count * zs, 1))]
    ppermute x1, starting transfers between devices: 6.74 us -> 1.91 us  [body(): behind = lax.ppermute(normed, LON + ('zh',), ring(lon_count * zs, 1))]
    ppermute x3, waiting for transfers between devices: 5.52 us -> 9.26 us  [body(): blocks.append(lax.ppermute(sent, 'x', ring(xs, by)))]
    ppermute x1, starting transfers between devices: 5.24 us -> 1.92 us  [body(): west = lax.ppermute(to_east, LON, ring(lon_count, 1))]
  transfers between devices with their start and end apart: 17 -> 20, of which waited for: 7 -> 10; matrix products, arithmetic and copies ran while one was open for 1% -> 1% of each run, Pallas kernels for 9% -> 6%
where the time goes in v2:
time: 173 us; the launch traced here: 172 us
  starting transfers between devices  89.6 us (52%)
  waiting for transfers between devices  53.6 us (31%)
  Pallas kernels  23.4 us (14%)
  local copies, waits for them, and re-layouts  4.91 us (3%)
    ppermute x3, starting transfers between devices, gathered(): far = lax.ppermute(half_of(at, near, after), ('c', axis), roles)  28.7 us
    ppermute x3, waiting for transfers between devices, gathered(): far = lax.ppermute(half_of(at, near, after), ('c', axis), roles)  24.8 us
    ppermute x3, starting transfers between devices, gathered(): near = lax.ppermute(rows, ('c', axis), roles)  16.2 us
    ppermute x3, starting transfers between devices, gathered(): lax.ppermute(far, 'c', swap)  16.2 us
    ppermute x1, waiting for transfers between devices, body(): behind = lax.ppermute(normed, LON + ('zh',), ring(lon_count * zs, 1))  11.4 us
    ppermute x3, starting transfers between devices, gathered(): lax.ppermute(near, 'c', swap)  10 us
    ppermute x3, waiting for transfers between devices, body(): blocks.append(lax.ppermute(sent, 'x', ring(xs, by)))  9.26 us
    pallas_call x1, Pallas kernels, global_layer(): pl.pallas_call(global_kernel, out_shape=jax.ShapeDtypeStruct((cells, widt...  9.04 us
  transfers between devices with their start and end apart: 20, of which 10 were waited for; matrix products, arithmetic and copies ran while one was open for 1% of the time, Pallas kernels for 6%

profile of v2, /device:TPU:1, one launch (start us, length us, event | category | flops | bytes accessed | tf_op | source)
XLA Modules:
  0.0 172.5 jit_solution(13640361899133601211)
XLA Ops:
  0.6 0.9 copy-done
  1.6 0.9 copy-done.2
  2.5 1.0 edges.1
  3.6 1.0 copy-done.4
  4.6 0.9 copy-done.7
  5.5 1.2 pick.1
  6.7 11.5 %collective-permute-start.4 = (bf16[64,4096]{1,0:T(8,128)(2,1)S(1)}, bf16[64,4096]{1,0:T(8,128)(2,1)S(1)}, u32[]{:S(2)}, u32[]{:S(2)}) collective-permute-start(bf16[64,4096]{1,0:T(8,128)(2,1)S(1)} %get-tuple-element.15.p0), channel_id=1, source_target_pairs={{0,4},{4,8},{8,12},{12,0},{16,28},{20,16},{24,20},{28,24},{1,5},{5... | collective-permute-start | bytes 1572872 | tf_op jit(solution)/shard_map/ppermute | solution.py:415
  18.2 1.3 collective-permute-start.1
  19.5 4.0 %collective-permute-start = (bf16[2,80,1024]{2,1,0:T(8,128)(2,1)S(1)}, bf16[2,80,1024]{2,1,0:T(8,128)(2,1)S(1)}, u32[]{:S(2)}, u32[]{:S(2)}) collective-permute-start(bf16[2,80,1024]{2,1,0:T(8,128)(2,1)S(1)} %get-tuple-element.10.after_ref), channel_id=1, source_target_pairs={{0,1},{1,2},{2,3},{3,4},{4,5},{5,6},{6,7},{7,8},{8,9},{9,10},{10,1... | collective-permute-start | bytes 983048 | tf_op jit(solution)/shard_map/ppermute | solution.py:436
  23.5 0.9 copy.11
  24.5 0.1 reshape.31
  24.6 3.8 %bias.1.after_ref.bias_ref = f32[16,96,512]{2,1,0:T(8,128)S(1)} custom-call(s32[5]{0:T(128)S(1)} %get-tuple-element.11.place_ref.at_ref, f32[16,256]{1,0:T(8,128)S(1)} %pad.4.table_ref), custom_call_target="tpu_custom_call" | custom-call | tf_op jit(solution)/shard_map/bias/pallas_call | solution.py:183
  28.5 0.6 collective-permute-done.low_ref
  29.1 0.5 sides.1
  29.5 1.9 %collective-permute-start.2 = (bf16[2,128,1024]{2,1,0:T(8,128)(2,1)S(1)}, bf16[2,128,1024]{2,1,0:T(8,128)(2,1)S(1)}, u32[]{:S(2)}, u32[]{:S(2)}) collective-permute-start(bf16[2,128,1024]{2,1,0:T(8,128)(2,1)S(1)} %get-tuple-element.13), channel_id=1, source_target_pairs={{0,16},{16,32},{32,48},{48,64},{64,80},{80,96},{96,112},{112,128},... | collective-permute-start | bytes 1572872 | tf_op jit(solution)/shard_map/ppermute | solution.py:441
  31.5 0.6 half.3
  32.0 24.8 %collective-permute-start.6 = (bf16[32,4096]{1,0:T(8,128)(2,1)S(1)}, bf16[32,4096]{1,0:T(8,128)(2,1)S(1)}, u32[]{:S(2)}, u32[]{:S(2)}) collective-permute-start(bf16[32,4096]{1,0:T(8,128)(2,1)S(1)} %half.3), channel_id=1, source_target_pairs={{0,4},{4,8},{8,12},{12,0},{16,28},{20,16},{24,20},{28,24},{1,5},{5... | collective-permute-start | bytes 786440 | tf_op jit(solution)/shard_map/ppermute | solution.py:416
  56.9 2.1 %collective-permute-start.3 = (bf16[2,128,1024]{2,1,0:T(8,128)(2,1)S(1)}, bf16[2,128,1024]{2,1,0:T(8,128)(2,1)S(1)}, u32[]{:S(2)}, u32[]{:S(2)}) collective-permute-start(bf16[2,128,1024]{2,1,0:T(8,128)(2,1)S(1)} %get-tuple-element.14), channel_id=1, source_target_pairs={{0,496},{16,0},{32,16},{48,32},{64,48},{80,64},{96,80},{112,96},{1... | collective-permute-start | bytes 1572872 | tf_op jit(solution)/shard_map/ppermute | solution.py:442
  59.0 4.7 %collective-permute-start.5 = (bf16[64,4096]{1,0:T(8,128)(2,1)S(1)}, bf16[64,4096]{1,0:T(8,128)(2,1)S(1)}, u32[]{:S(2)}, u32[]{:S(2)}) collective-permute-start(bf16[64,4096]{1,0:T(8,128)(2,1)S(1)} %collective-permute-done.4.x_ref.p1), channel_id=1, source_target_pairs={{0,16},{16,0},{1,17},{17,1},{2,18},{18,2},{3,19},{19,3},{4,20},{20... | collective-permute-start | bytes 1572872 | tf_op jit(solution)/shard_map/ppermute | solution.py:417
  63.6 7.1 %collective-permute-start.7 = (bf16[32,4096]{1,0:T(8,128)(2,1)S(1)}, bf16[32,4096]{1,0:T(8,128)(2,1)S(1)}, u32[]{:S(2)}, u32[]{:S(2)}) collective-permute-start(bf16[32,4096]{1,0:T(8,128)(2,1)S(1)} %collective-permute-done.6.p3), channel_id=1, source_target_pairs={{0,16},{16,0},{1,17},{17,1},{2,18},{18,2},{3,19},{19,3},{4,20},{20... | collective-permute-start | bytes 786440 | tf_op jit(solution)/shard_map/ppermute | solution.py:417
  70.8 1.1 collective-permute-done.7.p4
  71.9 0.6 place.2.p0
  72.5 1.9 %collective-permute-start.8 = (bf16[256,1024]{1,0:T(8,128)(2,1)S(1)}, bf16[256,1024]{1,0:T(8,128)(2,1)S(1)}, u32[]{:S(2)}, u32[]{:S(2)}) collective-permute-start(bf16[256,1024]{1,0:T(8,128)(2,1)S(1)} %place.2.p0), channel_id=1, source_target_pairs={{0,1},{1,2},{2,3},{3,0},{16,19},{17,16},{18,17},{19,18},{4,5},{5,6... | collective-permute-start | bytes 1572872 | tf_op jit(solution)/shard_map/ppermute | solution.py:415
  74.4 3.0 %local.1.x_ref.rest_1_ = bf16[96,1024]{1,0:T(8,128)(2,1)S(1)} custom-call(bf16[96,1024]{1,0:T(8,128)(2,1)S(1)} %bitcast.17, bf16[96,1024]{1,0:T(8,128)(2,1)S(1)} %bitcast.13, bf16[96,1024]{1,0:T(8,128)(2,1)S(1)} %bitcast.16, bf16[2,80,1024]{2,1,0:T(8,128)(2,1)S(1)} %collective-permute-done.low_ref, bf16[2,80,1024]{2,1,0:T(8,128)(2,1)S(1)} %collective-permute-done.1.high_ref, ...), custom_call_target="tpu_custom_call" | custom-call | tf_op jit(solution)/shard_map/local/pallas_call | solution.py:234
  77.4 5.3 %collective-permute-done.8.x_ref.p1.rest_0_ = bf16[256,1024]{1,0:T(8,128)(2,1)S(1)} collective-permute-done((bf16[256,1024]{1,0:T(8,128)(2,1)S(1)}, bf16[256,1024]{1,0:T(8,128)(2,1)S(1)}, u32[]{:S(2)}, u32[]{:S(2)}) %collective-permute-start.8) | collective-permute-done | bytes 524320 | tf_op jit(solution)/shard_map/ppermute | solution.py:415
  82.7 0.7 place.3.rest_0_.rest_5_.rest_10_
  83.4 2.8 %collective-permute-start.16 = (bf16[256,3072]{1,0:T(8,128)(2,1)S(1)}, bf16[256,3072]{1,0:T(8,128)(2,1)S(1)}, u32[]{:S(2)}, u32[]{:S(2)}) collective-permute-start(bf16[256,3072]{1,0:T(8,128)(2,1)S(1)} %place.3.rest_0_.rest_5_.rest_10_), channel_id=1, source_target_pairs={{0,1},{1,2},{2,3},{3,0},{16,19},{17,16},{18,17},{19,18},{4,5},{5,6... | collective-permute-start | bytes 4718600 | tf_op jit(solution)/shard_map/ppermute | solution.py:415
  86.2 0.6 half.4
  86.8 1.9 %collective-permute-start.10 = (bf16[128,1024]{1,0:T(8,128)(2,1)S(1)}, bf16[128,1024]{1,0:T(8,128)(2,1)S(1)}, u32[]{:S(2)}, u32[]{:S(2)}) collective-permute-start(bf16[128,1024]{1,0:T(8,128)(2,1)S(1)} %half.4), channel_id=1, source_target_pairs={{0,1},{1,2},{2,3},{3,0},{16,19},{17,16},{18,17},{19,18},{4,5},{5,6... | collective-permute-start | bytes 786440 | tf_op jit(solution)/shard_map/ppermute | solution.py:416
  88.7 3.4 %collective-permute-start.9 = (bf16[256,1024]{1,0:T(8,128)(2,1)S(1)}, bf16[256,1024]{1,0:T(8,128)(2,1)S(1)}, u32[]{:S(2)}, u32[]{:S(2)}) collective-permute-start(bf16[256,1024]{1,0:T(8,128)(2,1)S(1)} %collective-permute-done.8.x_ref.p1.rest_0_), channel_id=1, source_target_pairs={{0,16},{16,0},{1,17},{17,1},{2,18},{18,2},{3,19},{19,3},{4,20},{20... | collective-permute-start | bytes 1572872 | tf_op jit(solution)/shard_map/ppermute | solution.py:417
  92.2 15.5 %collective-permute-done.10.p3 = bf16[128,1024]{1,0:T(8,128)(2,1)S(1)} collective-permute-done((bf16[128,1024]{1,0:T(8,128)(2,1)S(1)}, bf16[128,1024]{1,0:T(8,128)(2,1)S(1)}, u32[]{:S(2)}, u32[]{:S(2)}) %collective-permute-start.10) | collective-permute-done | bytes 262176 | tf_op jit(solution)/shard_map/ppermute | solution.py:416
  107.6 6.4 %collective-permute-start.11 = (bf16[128,1024]{1,0:T(8,128)(2,1)S(1)}, bf16[128,1024]{1,0:T(8,128)(2,1)S(1)}, u32[]{:S(2)}, u32[]{:S(2)}) collective-permute-start(bf16[128,1024]{1,0:T(8,128)(2,1)S(1)} %collective-permute-done.10.p3), channel_id=1, source_target_pairs={{0,16},{16,0},{1,17},{17,1},{2,18},{18,2},{3,19},{19,3},{4,20},{20... | collective-permute-start | bytes 786440 | tf_op jit(solution)/shard_map/ppermute | solution.py:417
  114.1 1.1 collective-permute-done.11.p4
  115.2 1.9 %project.1 = (bf16[96,1024]{1,0:T(8,128)(2,1)}, bf16[96,1024]{1,0:T(8,128)(2,1)S(1)}) custom-call(s32[5]{0:T(128)S(1)} %get-tuple-element.11.place_ref.at_ref, bf16[96,1024]{1,0:T(8,128)(2,1)S(1)} %local.1.x_ref.rest_1_, bf16[96,1024]{1,0:T(8,128)(2,1)S(1)} %bitcast.18, f32[1,1024]{1,0:T(1,128)S(1)} %bitcast.19, bf16[256,1024]{1,0:T(8,128)(2,1)S(1)} %place.2.p0, ...), custom_call_target="tpu_custom_call" | custom-call | tf_op jit(solution)/shard_map/project/pallas_call | solution.py:280
  117.1 1.9 %collective-permute-start.12 = (bf16[96,1024]{1,0:T(8,128)(2,1)S(1)}, bf16[96,1024]{1,0:T(8,128)(2,1)S(1)}, u32[]{:S(2)}, u32[]{:S(2)}) collective-permute-start(bf16[96,1024]{1,0:T(8,128)(2,1)S(1)} %get-tuple-element.17.x0), channel_id=1, source_target_pairs={{0,4},{4,8},{8,12},{12,16},{16,20},{20,24},{24,28},{28,32},{32,36}... | collective-permute-start | bytes 589832 | tf_op jit(solution)/shard_map/ppermute | solution.py:449
  119.0 11.4 %collective-permute-done.12.rest_0_.x4 = bf16[96,1024]{1,0:T(8,128)(2,1)S(1)} collective-permute-done((bf16[96,1024]{1,0:T(8,128)(2,1)S(1)}, bf16[96,1024]{1,0:T(8,128)(2,1)S(1)}, u32[]{:S(2)}, u32[]{:S(2)}) %collective-permute-start.12) | collective-permute-done | bytes 196640 | tf_op jit(solution)/shard_map/ppermute | solution.py:449
  130.4 0.6 half.5
  131.0 1.9 %collective-permute-start.18 = (bf16[128,3072]{1,0:T(8,128)(2,1)S(1)}, bf16[128,3072]{1,0:T(8,128)(2,1)}, u32[]{:S(2)}, u32[]{:S(2)}) collective-permute-start(bf16[128,3072]{1,0:T(8,128)(2,1)S(1)} %half.5), channel_id=1, source_target_pairs={{0,1},{1,2},{2,3},{3,0},{16,19},{17,16},{18,17},{19,18},{4,5},{5,6... | collective-permute-start | bytes 2359304 | tf_op jit(solution)/shard_map/ppermute | solution.py:416
  132.9 1.9 %collective-permute-start.17 = (bf16[256,3072]{1,0:T(8,128)(2,1)S(1)}, bf16[256,3072]{1,0:T(8,128)(2,1)}, u32[]{:S(2)}, u32[]{:S(2)}) collective-permute-start(bf16[256,3072]{1,0:T(8,128)(2,1)S(1)} %collective-permute-done.16.x_ref.rest_1_.rest_6_.rest_11_), channel_id=1, source_target_pairs={{0,16},{16,0},{1,17},{17,1},{2,18},{18,2},{3,19},{19,3},{4,20},{20... | collective-permute-start | bytes 4718600 | tf_op jit(solution)/shard_map/ppermute | solution.py:417
  134.9 9.3 %collective-permute-done.18.rest_3_.rest_8_.rest_13_ = bf16[128,3072]{1,0:T(8,128)(2,1)} collective-permute-done((bf16[128,3072]{1,0:T(8,128)(2,1)S(1)}, bf16[128,3072]{1,0:T(8,128)(2,1)}, u32[]{:S(2)}, u32[]{:S(2)}) %collective-permute-start.18) | collective-permute-done | bytes 786464 | tf_op jit(solution)/shard_map/ppermute | solution.py:416
  144.2 2.7 %collective-permute-start.19 = (bf16[128,3072]{1,0:T(8,128)(2,1)}, bf16[128,3072]{1,0:T(8,128)(2,1)}, u32[]{:S(2)}, u32[]{:S(2)}) collective-permute-start(bf16[128,3072]{1,0:T(8,128)(2,1)} %collective-permute-done.18.rest_3_.rest_8_.rest_13_), channel_id=1, source_target_pairs={{0,16},{16,0},{1,17},{17,1},{2,18},{18,2},{3,19},{19,3},{4,20},{20... | collective-permute-start | bytes 2359304 | tf_op jit(solution)/shard_map/ppermute | solution.py:417
  147.0 2.0 %collective-permute-start.15 = (bf16[96,1024]{1,0:T(8,128)(2,1)S(1)}, bf16[96,1024]{1,0:T(8,128)(2,1)S(1)}, u32[]{:S(2)}, u32[]{:S(2)}) collective-permute-start(bf16[96,1024]{1,0:T(8,128)(2,1)S(1)} %get-tuple-element.18), channel_id=1, source_target_pairs={{0,3},{1,0},{2,1},{3,2},{4,7},{5,4},{6,5},{7,6},{8,11},{9,8},{10,9... | collective-permute-start | bytes 589832 | tf_op jit(solution)/shard_map/ppermute | solution.py:454
  149.0 2.1 %collective-permute-start.14 = (bf16[96,1024]{1,0:T(8,128)(2,1)S(1)}, bf16[96,1024]{1,0:T(8,128)(2,1)S(1)}, u32[]{:S(2)}, u32[]{:S(2)}) collective-permute-start(bf16[96,1024]{1,0:T(8,128)(2,1)S(1)} %get-tuple-element.19), channel_id=1, source_target_pairs={{0,2},{1,3},{2,0},{3,1},{4,6},{5,7},{6,4},{7,5},{8,10},{9,11},{10,... | collective-permute-start | bytes 589832 | tf_op jit(solution)/shard_map/ppermute | solution.py:454
  151.1 3.1 %collective-permute-start.13 = (bf16[96,1024]{1,0:T(8,128)(2,1)S(1)}, bf16[96,1024]{1,0:T(8,128)(2,1)S(1)}, u32[]{:S(2)}, u32[]{:S(2)}) collective-permute-start(bf16[96,1024]{1,0:T(8,128)(2,1)S(1)} %get-tuple-element.20), channel_id=1, source_target_pairs={{0,1},{1,2},{2,3},{3,0},{4,5},{5,6},{6,7},{7,4},{8,9},{9,10},{10,1... | collective-permute-start | bytes 589832 | tf_op jit(solution)/shard_map/ppermute | solution.py:454
  154.2 1.2 collective-permute-done.15.x3
  155.4 2.7 %collective-permute-done.14.x2 = bf16[96,1024]{1,0:T(8,128)(2,1)S(1)} collective-permute-done((bf16[96,1024]{1,0:T(8,128)(2,1)S(1)}, bf16[96,1024]{1,0:T(8,128)(2,1)S(1)}, u32[]{:S(2)}, u32[]{:S(2)}) %collective-permute-start.14) | collective-permute-done | bytes 196640 | tf_op jit(solution)/shard_map/ppermute | solution.py:454
  158.0 5.4 %collective-permute-done.13.x1 = bf16[96,1024]{1,0:T(8,128)(2,1)S(1)} collective-permute-done((bf16[96,1024]{1,0:T(8,128)(2,1)S(1)}, bf16[96,1024]{1,0:T(8,128)(2,1)S(1)}, u32[]{:S(2)}, u32[]{:S(2)}) %collective-permute-start.13) | collective-permute-done | bytes 196640 | tf_op jit(solution)/shard_map/ppermute | solution.py:454
  163.4 9.0 %global.1 = bf16[96,1024]{1,0:T(8,128)(2,1)} custom-call(s32[5]{0:T(128)S(1)} %get-tuple-element.11.place_ref.at_ref, bf16[96,1024]{1,0:T(8,128)(2,1)S(1)} %get-tuple-element.17.x0, bf16[96,1024]{1,0:T(8,128)(2,1)S(1)} %collective-permute-done.13.x1, bf16[96,1024]{1,0:T(8,128)(2,1)S(1)} %collective-permute-done.14.x2, ...), custom_call_target="tpu_custom_call" | custom-call | tf_op jit(solution)/shard_map/global/pallas_call | solution.py:323
  (27 shorter events, 0.2 us)
Async XLA Ops:
  0.6 0.9 copy-start
  1.6 0.9 copy-start.2
  3.6 1.0 copy-start.4
  4.6 0.9 copy-start.7
  6.7 24.7 %collective-permute-start.4 = (bf16[64,4096]{1,0:T(8,128)(2,1)S(1)}, bf16[64,4096]{1,0:T(8,128)(2,1)S(1)}, u32[]{:S(2)}, u32[]{:S(2)}) collective-permute-start(bf16[64,4096]{1,0:T(8,128)(2,1)S(1)} %get-tuple-element.15.p0), channel_id=1, source_target_pairs={{0,4},{4,8},{8,12},{12,0},{16,28},{20,16},{24,20},{28,24},{1,5},{5... | collective-permute-start | bytes 1572872 | tf_op jit(solution)/shard_map/ppermute | solution.py:415
  18.2 10.2 %collective-permute-start.1 = (bf16[2,80,1024]{2,1,0:T(8,128)(2,1)S(1)}, bf16[2,80,1024]{2,1,0:T(8,128)(2,1)S(1)}, u32[]{:S(2)}, u32[]{:S(2)}) collective-permute-start(bf16[2,80,1024]{2,1,0:T(8,128)(2,1)S(1)} %get-tuple-element.12), channel_id=1, source_target_pairs={{1,0},{2,1},{3,2},{4,3},{5,4},{6,5},{7,6},{8,7},{9,8},{10,9},{11,1... | collective-permute-start | bytes 983048 | tf_op jit(solution)/shard_map/ppermute | solution.py:437
  19.5 9.6 %collective-permute-start = (bf16[2,80,1024]{2,1,0:T(8,128)(2,1)S(1)}, bf16[2,80,1024]{2,1,0:T(8,128)(2,1)S(1)}, u32[]{:S(2)}, u32[]{:S(2)}) collective-permute-start(bf16[2,80,1024]{2,1,0:T(8,128)(2,1)S(1)} %get-tuple-element.10.after_ref), channel_id=1, source_target_pairs={{0,1},{1,2},{2,3},{3,4},{4,5},{5,6},{6,7},{7,8},{8,9},{9,10},{10,1... | collective-permute-start | bytes 983048 | tf_op jit(solution)/shard_map/ppermute | solution.py:436
  24.6 4.5 %copy-start.1 = (bf16[12,8,1024]{2,1,0:T(8,128)(2,1)S(1)}, bf16[12,8,1024]{2,1,0:T(8,128)(2,1)}, u32[]{:S(2)}) copy-start(bf16[12,8,1024]{2,1,0:T(8,128)(2,1)} %param.10) | copy-start | bytes 589828
  24.6 4.5 %copy-start.3 = (bf16[12,8,1024]{2,1,0:T(8,128)(2,1)S(1)}, bf16[12,8,1024]{2,1,0:T(8,128)(2,1)}, u32[]{:S(2)}) copy-start(bf16[12,8,1024]{2,1,0:T(8,128)(2,1)} %param.11) | copy-start | bytes 589828
  29.5 41.2 %collective-permute-start.2 = (bf16[2,128,1024]{2,1,0:T(8,128)(2,1)S(1)}, bf16[2,128,1024]{2,1,0:T(8,128)(2,1)S(1)}, u32[]{:S(2)}, u32[]{:S(2)}) collective-permute-start(bf16[2,128,1024]{2,1,0:T(8,128)(2,1)S(1)} %get-tuple-element.13), channel_id=1, source_target_pairs={{0,16},{16,32},{32,48},{48,64},{64,80},{80,96},{96,112},{112,128},... | collective-permute-start | bytes 1572872 | tf_op jit(solution)/shard_map/ppermute | solution.py:441
  32.0 31.6 %collective-permute-start.6 = (bf16[32,4096]{1,0:T(8,128)(2,1)S(1)}, bf16[32,4096]{1,0:T(8,128)(2,1)S(1)}, u32[]{:S(2)}, u32[]{:S(2)}) collective-permute-start(bf16[32,4096]{1,0:T(8,128)(2,1)S(1)} %half.3), channel_id=1, source_target_pairs={{0,4},{4,8},{8,12},{12,0},{16,28},{20,16},{24,20},{28,24},{1,5},{5... | collective-permute-start | bytes 786440 | tf_op jit(solution)/shard_map/ppermute | solution.py:416
  56.9 17.5 %copy-start.5 = (bf16[12,8,1024]{2,1,0:T(8,128)(2,1)S(1)}, bf16[12,8,1024]{2,1,0:T(8,128)(2,1)}, u32[]{:S(2)}) copy-start(bf16[12,8,1024]{2,1,0:T(8,128)(2,1)} %param.9) | copy-start | bytes 589828
  56.9 13.9 %collective-permute-start.3 = (bf16[2,128,1024]{2,1,0:T(8,128)(2,1)S(1)}, bf16[2,128,1024]{2,1,0:T(8,128)(2,1)S(1)}, u32[]{:S(2)}, u32[]{:S(2)}) collective-permute-start(bf16[2,128,1024]{2,1,0:T(8,128)(2,1)S(1)} %get-tuple-element.14), channel_id=1, source_target_pairs={{0,496},{16,0},{32,16},{48,32},{64,48},{80,64},{96,80},{112,96},{1... | collective-permute-start | bytes 1572872 | tf_op jit(solution)/shard_map/ppermute | solution.py:442
  59.0 13.0 %collective-permute-start.5 = (bf16[64,4096]{1,0:T(8,128)(2,1)S(1)}, bf16[64,4096]{1,0:T(8,128)(2,1)S(1)}, u32[]{:S(2)}, u32[]{:S(2)}) collective-permute-start(bf16[64,4096]{1,0:T(8,128)(2,1)S(1)} %collective-permute-done.4.x_ref.p1), channel_id=1, source_target_pairs={{0,16},{16,0},{1,17},{17,1},{2,18},{18,2},{3,19},{19,3},{4,20},{20... | collective-permute-start | bytes 1572872 | tf_op jit(solution)/shard_map/ppermute | solution.py:417
  63.6 8.3 %collective-permute-start.7 = (bf16[32,4096]{1,0:T(8,128)(2,1)S(1)}, bf16[32,4096]{1,0:T(8,128)(2,1)S(1)}, u32[]{:S(2)}, u32[]{:S(2)}) collective-permute-start(bf16[32,4096]{1,0:T(8,128)(2,1)S(1)} %collective-permute-done.6.p3), channel_id=1, source_target_pairs={{0,16},{16,0},{1,17},{17,1},{2,18},{18,2},{3,19},{19,3},{4,20},{20... | collective-permute-start | bytes 786440 | tf_op jit(solution)/shard_map/ppermute | solution.py:417
  72.5 10.2 %collective-permute-start.8 = (bf16[256,1024]{1,0:T(8,128)(2,1)S(1)}, bf16[256,1024]{1,0:T(8,128)(2,1)S(1)}, u32[]{:S(2)}, u32[]{:S(2)}) collective-permute-start(bf16[256,1024]{1,0:T(8,128)(2,1)S(1)} %place.2.p0), channel_id=1, source_target_pairs={{0,1},{1,2},{2,3},{3,0},{16,19},{17,16},{18,17},{19,18},{4,5},{5,6... | collective-permute-start | bytes 1572872 | tf_op jit(solution)/shard_map/ppermute | solution.py:415
  77.4 37.8 %copy-start.6 = (bf16[12,8,1024]{2,1,0:T(8,128)(2,1)S(1)}, bf16[12,8,1024]{2,1,0:T(8,128)(2,1)}, u32[]{:S(2)}) copy-start(bf16[12,8,1024]{2,1,0:T(8,128)(2,1)} %param.8) | copy-start | bytes 589828
  77.4 37.8 %copy-start.8 = (f32[1024]{0:T(1024)S(1)}, f32[1024]{0:T(1024)}, u32[]{:S(2)}) copy-start(f32[1024]{0:T(1024)} %param.14) | copy-start | bytes 12292
  83.4 47.0 %collective-permute-start.16 = (bf16[256,3072]{1,0:T(8,128)(2,1)S(1)}, bf16[256,3072]{1,0:T(8,128)(2,1)S(1)}, u32[]{:S(2)}, u32[]{:S(2)}) collective-permute-start(bf16[256,3072]{1,0:T(8,128)(2,1)S(1)} %place.3.rest_0_.rest_5_.rest_10_), channel_id=1, source_target_pairs={{0,1},{1,2},{2,3},{3,0},{16,19},{17,16},{18,17},{19,18},{4,5},{5,6... | collective-permute-start | bytes 4718600 | tf_op jit(solution)/shard_map/ppermute | solution.py:415
  86.8 20.8 %collective-permute-start.10 = (bf16[128,1024]{1,0:T(8,128)(2,1)S(1)}, bf16[128,1024]{1,0:T(8,128)(2,1)S(1)}, u32[]{:S(2)}, u32[]{:S(2)}) collective-permute-start(bf16[128,1024]{1,0:T(8,128)(2,1)S(1)} %half.4), channel_id=1, source_target_pairs={{0,1},{1,2},{2,3},{3,0},{16,19},{17,16},{18,17},{19,18},{4,5},{5,6... | collective-permute-start | bytes 786440 | tf_op jit(solution)/shard_map/ppermute | solution.py:416
  88.7 26.5 %collective-permute-start.9 = (bf16[256,1024]{1,0:T(8,128)(2,1)S(1)}, bf16[256,1024]{1,0:T(8,128)(2,1)S(1)}, u32[]{:S(2)}, u32[]{:S(2)}) collective-permute-start(bf16[256,1024]{1,0:T(8,128)(2,1)S(1)} %collective-permute-done.8.x_ref.p1.rest_0_), channel_id=1, source_target_pairs={{0,16},{16,0},{1,17},{17,1},{2,18},{18,2},{3,19},{19,3},{4,20},{20... | collective-permute-start | bytes 1572872 | tf_op jit(solution)/shard_map/ppermute | solution.py:417
  107.6 7.5 %collective-permute-start.11 = (bf16[128,1024]{1,0:T(8,128)(2,1)S(1)}, bf16[128,1024]{1,0:T(8,128)(2,1)S(1)}, u32[]{:S(2)}, u32[]{:S(2)}) collective-permute-start(bf16[128,1024]{1,0:T(8,128)(2,1)S(1)} %collective-permute-done.10.p3), channel_id=1, source_target_pairs={{0,16},{16,0},{1,17},{17,1},{2,18},{18,2},{3,19},{19,3},{4,20},{20... | collective-permute-start | bytes 786440 | tf_op jit(solution)/shard_map/ppermute | solution.py:417
  117.1 13.3 %collective-permute-start.12 = (bf16[96,1024]{1,0:T(8,128)(2,1)S(1)}, bf16[96,1024]{1,0:T(8,128)(2,1)S(1)}, u32[]{:S(2)}, u32[]{:S(2)}) collective-permute-start(bf16[96,1024]{1,0:T(8,128)(2,1)S(1)} %get-tuple-element.17.x0), channel_id=1, source_target_pairs={{0,4},{4,8},{8,12},{12,16},{16,20},{20,24},{24,28},{28,32},{32,36}... | collective-permute-start | bytes 589832 | tf_op jit(solution)/shard_map/ppermute | solution.py:449
  131.0 13.1 %collective-permute-start.18 = (bf16[128,3072]{1,0:T(8,128)(2,1)S(1)}, bf16[128,3072]{1,0:T(8,128)(2,1)}, u32[]{:S(2)}, u32[]{:S(2)}) collective-permute-start(bf16[128,3072]{1,0:T(8,128)(2,1)S(1)} %half.5), channel_id=1, source_target_pairs={{0,1},{1,2},{2,3},{3,0},{16,19},{17,16},{18,17},{19,18},{4,5},{5,6... | collective-permute-start | bytes 2359304 | tf_op jit(solution)/shard_map/ppermute | solution.py:416
  132.9 30.5 %collective-permute-start.17 = (bf16[256,3072]{1,0:T(8,128)(2,1)S(1)}, bf16[256,3072]{1,0:T(8,128)(2,1)}, u32[]{:S(2)}, u32[]{:S(2)}) collective-permute-start(bf16[256,3072]{1,0:T(8,128)(2,1)S(1)} %collective-permute-done.16.x_ref.rest_1_.rest_6_.rest_11_), channel_id=1, source_target_pairs={{0,16},{16,0},{1,17},{17,1},{2,18},{18,2},{3,19},{19,3},{4,20},{20... | collective-permute-start | bytes 4718600 | tf_op jit(solution)/shard_map/ppermute | solution.py:417
  144.2 19.3 %collective-permute-start.19 = (bf16[128,3072]{1,0:T(8,128)(2,1)}, bf16[128,3072]{1,0:T(8,128)(2,1)}, u32[]{:S(2)}, u32[]{:S(2)}) collective-permute-start(bf16[128,3072]{1,0:T(8,128)(2,1)} %collective-permute-done.18.rest_3_.rest_8_.rest_13_), channel_id=1, source_target_pairs={{0,16},{16,0},{1,17},{17,1},{2,18},{18,2},{3,19},{19,3},{4,20},{20... | collective-permute-start | bytes 2359304 | tf_op jit(solution)/shard_map/ppermute | solution.py:417
  147.0 8.4 %collective-permute-start.15 = (bf16[96,1024]{1,0:T(8,128)(2,1)S(1)}, bf16[96,1024]{1,0:T(8,128)(2,1)S(1)}, u32[]{:S(2)}, u32[]{:S(2)}) collective-permute-start(bf16[96,1024]{1,0:T(8,128)(2,1)S(1)} %get-tuple-element.18), channel_id=1, source_target_pairs={{0,3},{1,0},{2,1},{3,2},{4,7},{5,4},{6,5},{7,6},{8,11},{9,8},{10,9... | collective-permute-start | bytes 589832 | tf_op jit(solution)/shard_map/ppermute | solution.py:454
  149.0 9.0 %collective-permute-start.14 = (bf16[96,1024]{1,0:T(8,128)(2,1)S(1)}, bf16[96,1024]{1,0:T(8,128)(2,1)S(1)}, u32[]{:S(2)}, u32[]{:S(2)}) collective-permute-start(bf16[96,1024]{1,0:T(8,128)(2,1)S(1)} %get-tuple-element.19), channel_id=1, source_target_pairs={{0,2},{1,3},{2,0},{3,1},{4,6},{5,7},{6,4},{7,5},{8,10},{9,11},{10,... | collective-permute-start | bytes 589832 | tf_op jit(solution)/shard_map/ppermute | solution.py:454
  151.1 12.3 %collective-permute-start.13 = (bf16[96,1024]{1,0:T(8,128)(2,1)S(1)}, bf16[96,1024]{1,0:T(8,128)(2,1)S(1)}, u32[]{:S(2)}, u32[]{:S(2)}) collective-permute-start(bf16[96,1024]{1,0:T(8,128)(2,1)S(1)} %get-tuple-element.20), channel_id=1, source_target_pairs={{0,1},{1,2},{2,3},{3,0},{4,5},{5,6},{6,7},{7,4},{8,9},{9,10},{10,1... | collective-permute-start | bytes 589832 | tf_op jit(solution)/shard_map/ppermute | solution.py:454

commit v3 on v2

--- a/solution.py
+++ b/solution.py
@@ -137,7 +137,7 @@
     return lon, lat, side
 
 
-def bias_kernel(place_ref, table_ref, out_ref):
+def bias_kernel(place_ref, table_ref, after_ref, out_ref):
     heads = out_ref.shape[0]
     rows = heads * TJ
     table = jnp.broadcast_to(table_ref[...][:, None, :], (heads, TJ, 256)).reshape(rows, 256)
@@ -176,18 +176,18 @@
         out_ref[:, TJ * i : TJ * i + TJ, :] = found
 
 
-def bias_table(position_bias, place):
+def bias_table(position_bias, place, after):
     heads = position_bias.shape[0]
     table = position_bias.reshape(heads, WINDOW * WINDOW)
     table = jnp.pad(table, ((0, 0), (0, 256 - WINDOW * WINDOW)))
     return pl.pallas_call(
         bias_kernel,
         out_shape=jax.ShapeDtypeStruct((heads, CELLS, KEYS), jnp.float32),
-        in_specs=[sspec(), vspec()],
+        in_specs=[sspec(), vspec(), anyspec()],
         out_specs=vspec(),
         compiler_params=params(12),
         name="bias",
-    )(place, table)
+    )(place, table, after)
 
 
 def pair_attention(q, k, v, bias):
@@ -335,36 +335,9 @@
     )(at, *blocks, *(pieces * 3))
 
 
-def pick_kernel(at_ref, o_ref, g_ref, after_ref, out_ref, again_ref, sems):
-    side = o_ref.shape[1]
-    copies = [
-        pltpu.make_async_copy(o_ref, out_ref.at[:, pl.ds(0, side)], sems.at[0]),
-        pltpu.make_async_copy(g_ref, out_ref.at[:, pl.ds(side, g_ref.shape[1])], sems.at[1]),
-    ]
-    for copy in copies:
-        copy.start()
-    for i in range(at_ref.shape[0]):
-        again_ref[i] = at_ref[i]
-    for copy in copies:
-        copy.wait()
-
-
-def pick(at, o, g, after):
-    shape = jax.ShapeDtypeStruct((o.shape[0], o.shape[1] + g.shape[1]), o.dtype)
-    return pl.pallas_call(
-        pick_kernel,
-        out_shape=[shape, jax.ShapeDtypeStruct(at.shape, at.dtype)],
-        in_specs=[sspec()] + [anyspec()] * 3,
-        out_specs=[vspec(), sspec()],
-        scratch_shapes=[pltpu.SemaphoreType.DMA((2,))],
-        compiler_params=params(4),
-        name="pick",
-    )(at, o, g, after)
-
-
-def place_kernel(at_ref, p0, p1, p2, p3, p4, *rest, first):
+def place_kernel(at_ref, p0, p1, p2, p3, p4, *rest):
     out_ref = rest[-1]
-    rows, side = p0.shape[0], out_ref.shape[1]
+    rows = p0.shape[0]
     half = rows // 2
     core, zh = at_ref[0], at_ref[2]
     far = lax.rem(zh + 2, 4) * rows
@@ -377,14 +350,14 @@
     )
     for start, ref in zip(starts, (p0, p1, p2, p3, p4)):
         to = pl.ds(pl.multiple_of(start, half), ref.shape[0])
-        out_ref[to] = ref[:, first : first + side]
-
-
-def place_rows(at, pieces, first, count, after):
-    rows = pieces[0].shape[0]
-    return pl.pallas_call(
-        functools.partial(place_kernel, first=first),
-        out_shape=jax.ShapeDtypeStruct((rows * 4, count), pieces[0].dtype),
+        out_ref[to] = ref[...]
+
+
+def place_rows(at, pieces, after):
+    rows, columns = pieces[0].shape
+    return pl.pallas_call(
+        place_kernel,
+        out_shape=jax.ShapeDtypeStruct((rows * 4, columns), pieces[0].dtype),
         in_specs=[sspec()] + [vspec()] * len(pieces) + [anyspec()] * len(after),
         out_specs=vspec(),
         compiler_params=params(8),
@@ -435,24 +408,25 @@
     up, down = edges(k, v)
     low = lax.ppermute(up, LAT, [(i, i + 1) for i in range(lat_count - 1)])
     high = lax.ppermute(down, LAT, [(i + 1, i) for i in range(lat_count - 1)])
-    weights, at = pick(at, output_weight, global_weight, up)
-    bias = bias_table(position_bias, at)
+    bias = bias_table(position_bias, at, up)
+    pieces_o = gathered(output_weight, "zh", at, [up])
     to_east, to_west = sides(low, high, k, v, bias)
     west = lax.ppermute(to_east, LON, ring(lon_count, 1))
     east = lax.ppermute(to_west, LON, ring(lon_count, -1))
-    pieces = gathered(weights, "zh", at, [])
-    rows_o = place_rows(at, pieces, 0, width, [west, east])
-    pieces_o = gathered(rows_o, "x", at, [])
+    rows_o = place_rows(at, pieces_o, [to_east, to_west])
+    global_weight, pieces_o[3] = lax.optimization_barrier((global_weight, pieces_o[3]))
+    pieces_g = gathered(global_weight, "zh", at, [rows_o])
+    pieces_o = gathered(rows_o, "x", at, [west, east])
     local_out = attend(q, k, v, low, high, west, east, bias)
-    rows_g = place_rows(at, pieces, width, 3 * width, [pieces_o[1], local_out])
+    rows_g = place_rows(at, pieces_g, [pieces_o[3], local_out])
     hidden, normed = project(at, local_out, tok, norm_gain.reshape(1, width), pieces_o)
     behind = lax.ppermute(normed, LON + ("zh",), ring(lon_count * zs, 1))
-    pieces_g = gathered(rows_g, "x", at, [behind])
     blocks = [normed]
     for by in range(1, xs):
         sent = jnp.where(x + by < xs, normed, behind)
         blocks.append(lax.ppermute(sent, "x", ring(xs, by)))
     blocks.append(behind)
+    pieces_g = gathered(rows_g, "x", at, blocks[1:xs])
     attended = global_layer(at, blocks, pieces_g)
     return hidden.reshape(tokens.shape), attended.reshape(tokens.shape)
 

time: 173 us -> 158 us (0.913)
  waiting for transfers between devices: 53.6 us -> 40.9 us
  local copies, waits for them, and re-layouts: 4.91 us -> 3.02 us
    ppermute x3 -> x4, waiting for transfers between devices: 24.8 us -> 8.68 us  [gathered(): far = lax.ppermute(half_of(at, near, after), ('c', axis), roles)]
    ppermute x3 -> x4, starting transfers between devices: 28.7 us -> 14.6 us  [gathered(): far = lax.ppermute(half_of(at, near, after), ('c', axis), roles)]
    ppermute x3 -> x4, starting transfers between devices: 16.2 us -> 25.4 us  [gathered(): near = lax.ppermute(rows, ('c', axis), roles)]
    ppermute x3 -> x4, waiting for transfers between devices: 5.27 us -> 10.9 us  [gathered(): near = lax.ppermute(rows, ('c', axis), roles)]
    ppermute x3 -> x4, starting transfers between devices: 16.2 us -> 11.6 us  [gathered(): lax.ppermute(far, 'c', swap)]
    ppermute x3, waiting for transfers between devices: 9.26 us -> 5.12 us  [body(): blocks.append(lax.ppermute(sent, 'x', ring(xs, by)))]
    ppermute x3 -> x4, starting transfers between devices: 10 us -> 13.7 us  [gathered(): lax.ppermute(near, 'c', swap)]
    ppermute x1, starting transfers between devices: 1.92 us -> 5.55 us  [body(): west = lax.ppermute(to_east, LON, ring(lon_count, 1))]
  transfers between devices with their start and end apart: 20 -> 24, of which waited for: 10 -> 9; matrix products, arithmetic and copies ran while one was open for 1% -> 1% of each run, Pallas kernels for 6% -> 7%
where the time goes in v3:
time: 158 us; the launch traced here: 157 us
  starting transfers between devices  89.4 us (57%)
  waiting for transfers between devices  40.9 us (26%)
  Pallas kernels  22.3 us (14%)
  local copies, waits for them, and re-layouts  3.02 us (2%)
    ppermute x4, starting transfers between devices, gathered(): near = lax.ppermute(rows, ('c', axis), roles)  25.4 us
    ppermute x4, starting transfers between devices, gathered(): far = lax.ppermute(half_of(at, near, after), ('c', axis), roles)  14.6 us
    ppermute x4, starting transfers between devices, gathered(): lax.ppermute(near, 'c', swap)  13.7 us
    ppermute x1, waiting for transfers between devices, body(): behind = lax.ppermute(normed, LON + ('zh',), ring(lon_count * zs, 1))  13.2 us
    ppermute x4, starting transfers between devices, gathered(): lax.ppermute(far, 'c', swap)  11.6 us
    ppermute x4, waiting for transfers between devices, gathered(): near = lax.ppermute(rows, ('c', axis), roles)  10.9 us
    ppermute x3, starting transfers between devices, body(): blocks.append(lax.ppermute(sent, 'x', ring(xs, by)))  9.23 us
    ppermute x4, waiting for transfers between devices, gathered(): far = lax.ppermute(half_of(at, near, after), ('c', axis), roles)  8.68 us
  transfers between devices with their start and end apart: 24, of which 9 were waited for; matrix products, arithmetic and copies ran while one was open for 1% of the time, Pallas kernels for 7%

profile of v3, /device:TPU:1, one launch (start us, length us, event | category | flops | bytes accessed | tf_op | source)
XLA Modules:
  0.0 156.8 jit_solution(10877669072332653966)
XLA Ops:
  0.6 0.9 copy-done
  1.6 0.9 copy-done.2
  2.5 1.0 edges.1
  3.5 4.0 %collective-permute-start = (bf16[2,80,1024]{2,1,0:T(8,128)(2,1)S(1)}, bf16[2,80,1024]{2,1,0:T(8,128)(2,1)S(1)}, u32[]{:S(2)}, u32[]{:S(2)}) collective-permute-start(bf16[2,80,1024]{2,1,0:T(8,128)(2,1)S(1)} %get-tuple-element.9.after_ref.rest_0_), channel_id=1, source_target_pairs={{0,1},{1,2},{2,3},{3,4},{4,5},{5,6},{6,7},{7,8},{8,9},{9,10},{10,1... | collective-permute-start | bytes 983048 | tf_op jit(solution)/shard_map/ppermute | solution.py:409
  7.5 1.3 collective-permute-start.1
  8.8 14.5 %collective-permute-start.4 = (bf16[64,1024]{1,0:T(8,128)(2,1)}, bf16[64,1024]{1,0:T(8,128)(2,1)S(1)}, u32[]{:S(2)}, u32[]{:S(2)}) collective-permute-start(bf16[64,1024]{1,0:T(8,128)(2,1)} %p0.1), channel_id=1, source_target_pairs={{0,4},{4,8},{8,12},{12,0},{16,28},{20,16},{24,20},{28,24},{1,5},{5... | collective-permute-start | bytes 393224 | tf_op jit(solution)/shard_map/ppermute | solution.py:388
  23.4 10.8 %collective-permute-done.4.x_ref.p1 = bf16[64,1024]{1,0:T(8,128)(2,1)S(1)} collective-permute-done((bf16[64,1024]{1,0:T(8,128)(2,1)}, bf16[64,1024]{1,0:T(8,128)(2,1)S(1)}, u32[]{:S(2)}, u32[]{:S(2)}) %collective-permute-start.4) | collective-permute-done | bytes 131104 | tf_op jit(solution)/shard_map/ppermute | solution.py:388
  34.2 0.6 half.4
  34.8 6.5 %collective-permute-start.6 = (bf16[32,1024]{1,0:T(8,128)(2,1)S(1)}, bf16[32,1024]{1,0:T(8,128)(2,1)S(1)}, u32[]{:S(2)}, u32[]{:S(2)}) collective-permute-start(bf16[32,1024]{1,0:T(8,128)(2,1)S(1)} %half.4), channel_id=1, source_target_pairs={{0,4},{4,8},{8,12},{12,0},{16,28},{20,16},{24,20},{28,24},{1,5},{5... | collective-permute-start | bytes 196616 | tf_op jit(solution)/shard_map/ppermute | solution.py:389
  41.3 1.9 %collective-permute-start.5 = (bf16[64,1024]{1,0:T(8,128)(2,1)S(1)}, bf16[64,1024]{1,0:T(8,128)(2,1)S(1)}, u32[]{:S(2)}, u32[]{:S(2)}) collective-permute-start(bf16[64,1024]{1,0:T(8,128)(2,1)S(1)} %collective-permute-done.4.x_ref.p1), channel_id=1, source_target_pairs={{0,16},{16,0},{1,17},{17,1},{2,18},{18,2},{3,19},{19,3},{4,20},{20... | collective-permute-start | bytes 393224 | tf_op jit(solution)/shard_map/ppermute | solution.py:390
  43.2 1.6 %collective-permute-done.6.p3 = bf16[32,1024]{1,0:T(8,128)(2,1)S(1)} collective-permute-done((bf16[32,1024]{1,0:T(8,128)(2,1)S(1)}, bf16[32,1024]{1,0:T(8,128)(2,1)S(1)}, u32[]{:S(2)}, u32[]{:S(2)}) %collective-permute-start.6) | collective-permute-done | bytes 65568 | tf_op jit(solution)/shard_map/ppermute | solution.py:389
  44.8 1.9 %collective-permute-start.7 = (bf16[32,1024]{1,0:T(8,128)(2,1)S(1)}, bf16[32,1024]{1,0:T(8,128)(2,1)S(1)}, u32[]{:S(2)}, u32[]{:S(2)}) collective-permute-start(bf16[32,1024]{1,0:T(8,128)(2,1)S(1)} %collective-permute-done.6.p3), channel_id=1, source_target_pairs={{0,16},{16,0},{1,17},{17,1},{2,18},{18,2},{3,19},{19,3},{4,20},{20... | collective-permute-start | bytes 196616 | tf_op jit(solution)/shard_map/ppermute | solution.py:390
  46.7 0.9 copy.11
  47.8 3.8 %bias.1.after_ref.bias_ref = f32[16,96,512]{2,1,0:T(8,128)S(1)} custom-call(s32[5]{0:T(128)S(1)} %stack.19.place_ref.at_ref, f32[16,256]{1,0:T(8,128)S(1)} %pad.4.table_ref, bf16[2,80,1024]{2,1,0:T(8,128)(2,1)S(1)} %get-tuple-element.9.after_ref.rest_0_), custom_call_target="tpu_custom_call" | custom-call | tf_op jit(solution)/shard_map/bias/pallas_call | solution.py:183
  51.7 3.9 %collective-permute-start.16 = (bf16[64,3072]{1,0:T(8,128)(2,1)S(1)}, bf16[64,3072]{1,0:T(8,128)(2,1)S(1)}, u32[]{:S(2)}, u32[]{:S(2)}) collective-permute-start(bf16[64,3072]{1,0:T(8,128)(2,1)S(1)} %copy-done.4), channel_id=1, source_target_pairs={{0,4},{4,8},{8,12},{12,0},{16,28},{20,16},{24,20},{28,24},{1,5},{5... | collective-permute-start | bytes 1179656 | tf_op jit(solution)/shard_map/ppermute | solution.py:388
  55.7 0.4 sides.1
  56.1 5.5 %collective-permute-start.2 = (bf16[2,128,1024]{2,1,0:T(8,128)(2,1)S(1)}, bf16[2,128,1024]{2,1,0:T(8,128)(2,1)S(1)}, u32[]{:S(2)}, u32[]{:S(2)}) collective-permute-start(bf16[2,128,1024]{2,1,0:T(8,128)(2,1)S(1)} %get-tuple-element.11.rest_0_), channel_id=1, source_target_pairs={{0,16},{16,32},{32,48},{48,64},{64,80},{80,96},{96,112},{112,128},... | collective-permute-start | bytes 1572872 | tf_op jit(solution)/shard_map/ppermute | solution.py:414
  61.7 1.9 %collective-permute-start.3 = (bf16[2,128,1024]{2,1,0:T(8,128)(2,1)S(1)}, bf16[2,128,1024]{2,1,0:T(8,128)(2,1)S(1)}, u32[]{:S(2)}, u32[]{:S(2)}) collective-permute-start(bf16[2,128,1024]{2,1,0:T(8,128)(2,1)S(1)} %get-tuple-element.12.rest_1_), channel_id=1, source_target_pairs={{0,496},{16,0},{32,16},{48,32},{64,48},{80,64},{96,80},{112,96},{1... | collective-permute-start | bytes 1572872 | tf_op jit(solution)/shard_map/ppermute | solution.py:415
  63.6 0.6 place.2.p0.rest_0_
  64.2 2.1 %collective-permute-start.8 = (bf16[256,1024]{1,0:T(8,128)(2,1)S(1)}, bf16[256,1024]{1,0:T(8,128)(2,1)S(1)}, u32[]{:S(2)}, u32[]{:S(2)}) collective-permute-start(bf16[256,1024]{1,0:T(8,128)(2,1)S(1)} %place.2.p0.rest_0_), channel_id=1, source_target_pairs={{0,1},{1,2},{2,3},{3,0},{16,19},{17,16},{18,17},{19,18},{4,5},{5,6... | collective-permute-start | bytes 1572872 | tf_op jit(solution)/shard_map/ppermute | solution.py:388
  66.3 0.6 half.6
  66.9 1.9 %collective-permute-start.18 = (bf16[32,3072]{1,0:T(8,128)(2,1)S(1)}, bf16[32,3072]{1,0:T(8,128)(2,1)S(1)}, u32[]{:S(2)}, u32[]{:S(2)}) collective-permute-start(bf16[32,3072]{1,0:T(8,128)(2,1)S(1)} %half.6), channel_id=1, source_target_pairs={{0,4},{4,8},{8,12},{12,0},{16,28},{20,16},{24,20},{28,24},{1,5},{5... | collective-permute-start | bytes 589832 | tf_op jit(solution)/shard_map/ppermute | solution.py:389
  68.8 7.9 %collective-permute-start.17 = (bf16[64,3072]{1,0:T(8,128)(2,1)S(1)}, bf16[64,3072]{1,0:T(8,128)(2,1)S(1)}, u32[]{:S(2)}, u32[]{:S(2)}) collective-permute-start(bf16[64,3072]{1,0:T(8,128)(2,1)S(1)} %collective-permute-done.16.x_ref.p1), channel_id=1, source_target_pairs={{0,16},{16,0},{1,17},{17,1},{2,18},{18,2},{3,19},{19,3},{4,20},{20... | collective-permute-start | bytes 1179656 | tf_op jit(solution)/shard_map/ppermute | solution.py:390
  76.8 0.6 half.5
  77.4 2.2 %collective-permute-start.10 = (bf16[128,1024]{1,0:T(8,128)(2,1)S(1)}, bf16[128,1024]{1,0:T(8,128)(2,1)S(1)}, u32[]{:S(2)}, u32[]{:S(2)}) collective-permute-start(bf16[128,1024]{1,0:T(8,128)(2,1)S(1)} %half.5), channel_id=1, source_target_pairs={{0,1},{1,2},{2,3},{3,0},{16,19},{17,16},{18,17},{19,18},{4,5},{5,6... | collective-permute-start | bytes 786440 | tf_op jit(solution)/shard_map/ppermute | solution.py:389
  79.6 4.2 %collective-permute-start.19 = (bf16[32,3072]{1,0:T(8,128)(2,1)S(1)}, bf16[32,3072]{1,0:T(8,128)(2,1)S(1)}, u32[]{:S(2)}, u32[]{:S(2)}) collective-permute-start(bf16[32,3072]{1,0:T(8,128)(2,1)S(1)} %collective-permute-done.18.p3), channel_id=1, source_target_pairs={{0,16},{16,0},{1,17},{17,1},{2,18},{18,2},{3,19},{19,3},{4,20},{20... | collective-permute-start | bytes 589832 | tf_op jit(solution)/shard_map/ppermute | solution.py:390
  83.8 3.0 %local.1.x_ref.rest_1_ = bf16[96,1024]{1,0:T(8,128)(2,1)S(1)} custom-call(bf16[96,1024]{1,0:T(8,128)(2,1)S(1)} %bitcast.17, bf16[96,1024]{1,0:T(8,128)(2,1)S(1)} %bitcast.13, bf16[96,1024]{1,0:T(8,128)(2,1)S(1)} %bitcast.16, bf16[2,80,1024]{2,1,0:T(8,128)(2,1)S(1)} %collective-permute-done.low_ref, bf16[2,80,1024]{2,1,0:T(8,128)(2,1)S(1)} %collective-permute-done.1.high_ref, ...), custom_call_target="tpu_custom_call" | custom-call | tf_op jit(solution)/shard_map/local/pallas_call | solution.py:234
  86.8 0.7 place.3.rest_0_.rest_5_.rest_10_
  87.5 4.9 %collective-permute-start.20 = (bf16[256,3072]{1,0:T(8,128)(2,1)S(1)}, bf16[256,3072]{1,0:T(8,128)(2,1)S(1)}, u32[]{:S(2)}, u32[]{:S(2)}) collective-permute-start(bf16[256,3072]{1,0:T(8,128)(2,1)S(1)} %place.3.rest_0_.rest_5_.rest_10_), channel_id=1, source_target_pairs={{0,1},{1,2},{2,3},{3,0},{16,19},{17,16},{18,17},{19,18},{4,5},{5,6... | collective-permute-start | bytes 4718600 | tf_op jit(solution)/shard_map/ppermute | solution.py:388
  92.3 1.9 %collective-permute-start.9 = (bf16[256,1024]{1,0:T(8,128)(2,1)S(1)}, bf16[256,1024]{1,0:T(8,128)(2,1)S(1)}, u32[]{:S(2)}, u32[]{:S(2)}) collective-permute-start(bf16[256,1024]{1,0:T(8,128)(2,1)S(1)} %collective-permute-done.8.x_ref.p1), channel_id=1, source_target_pairs={{0,16},{16,0},{1,17},{17,1},{2,18},{18,2},{3,19},{19,3},{4,20},{20... | collective-permute-start | bytes 1572872 | tf_op jit(solution)/shard_map/ppermute | solution.py:390
  94.3 2.4 %collective-permute-start.11 = (bf16[128,1024]{1,0:T(8,128)(2,1)S(1)}, bf16[128,1024]{1,0:T(8,128)(2,1)S(1)}, u32[]{:S(2)}, u32[]{:S(2)}) collective-permute-start(bf16[128,1024]{1,0:T(8,128)(2,1)S(1)} %collective-permute-done.10.p3.rest_0_), channel_id=1, source_target_pairs={{0,16},{16,0},{1,17},{17,1},{2,18},{18,2},{3,19},{19,3},{4,20},{20... | collective-permute-start | bytes 786440 | tf_op jit(solution)/shard_map/ppermute | solution.py:390
  96.7 1.1 collective-permute-done.11.p4
  97.8 1.9 %project.1 = (bf16[96,1024]{1,0:T(8,128)(2,1)}, bf16[96,1024]{1,0:T(8,128)(2,1)S(1)}) custom-call(s32[5]{0:T(128)S(1)} %stack.19.place_ref.at_ref, bf16[96,1024]{1,0:T(8,128)(2,1)S(1)} %local.1.x_ref.rest_1_, bf16[96,1024]{1,0:T(8,128)(2,1)S(1)} %bitcast.18, f32[1,1024]{1,0:T(1,128)S(1)} %bitcast.19, bf16[256,1024]{1,0:T(8,128)(2,1)S(1)} %place.2.p0.rest_0_, ...), custom_call_target="tpu_custom_call" | custom-call | tf_op jit(solution)/shard_map/project/pallas_call | solution.py:280
  99.7 2.2 %collective-permute-start.12 = (bf16[96,1024]{1,0:T(8,128)(2,1)S(1)}, bf16[96,1024]{1,0:T(8,128)(2,1)S(1)}, u32[]{:S(2)}, u32[]{:S(2)}) collective-permute-start(bf16[96,1024]{1,0:T(8,128)(2,1)S(1)} %get-tuple-element.14.x0), channel_id=1, source_target_pairs={{0,4},{4,8},{8,12},{12,16},{16,20},{20,24},{24,28},{28,32},{32,36}... | collective-permute-start | bytes 589832 | tf_op jit(solution)/shard_map/ppermute | solution.py:423
  101.9 13.2 %collective-permute-done.12.x4 = bf16[96,1024]{1,0:T(8,128)(2,1)S(1)} collective-permute-done((bf16[96,1024]{1,0:T(8,128)(2,1)S(1)}, bf16[96,1024]{1,0:T(8,128)(2,1)S(1)}, u32[]{:S(2)}, u32[]{:S(2)}) %collective-permute-start.12) | collective-permute-done | bytes 196640 | tf_op jit(solution)/shard_map/ppermute | solution.py:423
  115.2 1.9 %collective-permute-start.13 = (bf16[96,1024]{1,0:T(8,128)(2,1)S(1)}, bf16[96,1024]{1,0:T(8,128)(2,1)S(1)}, u32[]{:S(2)}, u32[]{:S(2)}) collective-permute-start(bf16[96,1024]{1,0:T(8,128)(2,1)S(1)} %get-tuple-element.18), channel_id=1, source_target_pairs={{0,1},{1,2},{2,3},{3,0},{4,5},{5,6},{6,7},{7,4},{8,9},{9,10},{10,1... | collective-permute-start | bytes 589832 | tf_op jit(solution)/shard_map/ppermute | solution.py:427
  117.1 5.4 %collective-permute-start.14 = (bf16[96,1024]{1,0:T(8,128)(2,1)S(1)}, bf16[96,1024]{1,0:T(8,128)(2,1)S(1)}, u32[]{:S(2)}, u32[]{:S(2)}) collective-permute-start(bf16[96,1024]{1,0:T(8,128)(2,1)S(1)} %get-tuple-element.17), channel_id=1, source_target_pairs={{0,2},{1,3},{2,0},{3,1},{4,6},{5,7},{6,4},{7,5},{8,10},{9,11},{10,... | collective-permute-start | bytes 589832 | tf_op jit(solution)/shard_map/ppermute | solution.py:427
  122.5 1.9 %collective-permute-start.15 = (bf16[96,1024]{1,0:T(8,128)(2,1)S(1)}, bf16[96,1024]{1,0:T(8,128)(2,1)S(1)}, u32[]{:S(2)}, u32[]{:S(2)}) collective-permute-start(bf16[96,1024]{1,0:T(8,128)(2,1)S(1)} %get-tuple-element.16), channel_id=1, source_target_pairs={{0,3},{1,0},{2,1},{3,2},{4,7},{5,4},{6,5},{7,6},{8,11},{9,8},{10,9... | collective-permute-start | bytes 589832 | tf_op jit(solution)/shard_map/ppermute | solution.py:427
  124.4 0.4 collective-permute-done.13.rest_0_.x1
  124.8 2.1 %collective-permute-done.14.rest_1_.x2 = bf16[96,1024]{1,0:T(8,128)(2,1)S(1)} collective-permute-done((bf16[96,1024]{1,0:T(8,128)(2,1)S(1)}, bf16[96,1024]{1,0:T(8,128)(2,1)S(1)}, u32[]{:S(2)}, u32[]{:S(2)}) %collective-permute-start.14) | collective-permute-done | bytes 196640 | tf_op jit(solution)/shard_map/ppermute | solution.py:427
  126.9 2.6 %collective-permute-done.15.rest_2_.x3 = bf16[96,1024]{1,0:T(8,128)(2,1)S(1)} collective-permute-done((bf16[96,1024]{1,0:T(8,128)(2,1)S(1)}, bf16[96,1024]{1,0:T(8,128)(2,1)S(1)}, u32[]{:S(2)}, u32[]{:S(2)}) %collective-permute-start.15) | collective-permute-done | bytes 196640 | tf_op jit(solution)/shard_map/ppermute | solution.py:427
  129.6 0.6 half.7
  130.2 4.0 %collective-permute-start.22 = (bf16[128,3072]{1,0:T(8,128)(2,1)S(1)}, bf16[128,3072]{1,0:T(8,128)(2,1)S(1)}, u32[]{:S(2)}, u32[]{:S(2)}) collective-permute-start(bf16[128,3072]{1,0:T(8,128)(2,1)S(1)} %half.7), channel_id=1, source_target_pairs={{0,1},{1,2},{2,3},{3,0},{16,19},{17,16},{18,17},{19,18},{4,5},{5,6... | collective-permute-start | bytes 2359304 | tf_op jit(solution)/shard_map/ppermute | solution.py:389
  134.2 1.9 %collective-permute-start.21 = (bf16[256,3072]{1,0:T(8,128)(2,1)S(1)}, bf16[256,3072]{1,0:T(8,128)(2,1)S(1)}, u32[]{:S(2)}, u32[]{:S(2)}) collective-permute-start(bf16[256,3072]{1,0:T(8,128)(2,1)S(1)} %collective-permute-done.20.x_ref.rest_1_.rest_6_.rest_11_), channel_id=1, source_target_pairs={{0,16},{16,0},{1,17},{17,1},{2,18},{18,2},{3,19},{19,3},{4,20},{20... | collective-permute-start | bytes 4718600 | tf_op jit(solution)/shard_map/ppermute | solution.py:390
  136.1 7.1 %collective-permute-done.22.rest_3_.rest_8_.rest_13_ = bf16[128,3072]{1,0:T(8,128)(2,1)S(1)} collective-permute-done((bf16[128,3072]{1,0:T(8,128)(2,1)S(1)}, bf16[128,3072]{1,0:T(8,128)(2,1)S(1)}, u32[]{:S(2)}, u32[]{:S(2)}) %collective-permute-start.22) | collective-permute-done | bytes 786464 | tf_op jit(solution)/shard_map/ppermute | solution.py:389
  143.2 3.1 %collective-permute-start.23 = (bf16[128,3072]{1,0:T(8,128)(2,1)S(1)}, bf16[128,3072]{1,0:T(8,128)(2,1)S(1)}, u32[]{:S(2)}, u32[]{:S(2)}) collective-permute-start(bf16[128,3072]{1,0:T(8,128)(2,1)S(1)} %collective-permute-done.22.rest_3_.rest_8_.rest_13_), channel_id=1, source_target_pairs={{0,16},{16,0},{1,17},{17,1},{2,18},{18,2},{3,19},{19,3},{4,20},{20... | collective-permute-start | bytes 2359304 | tf_op jit(solution)/shard_map/ppermute | solution.py:390
  146.3 1.9 %collective-permute-done.23.rest_4_.rest_9_.rest_14_ = bf16[128,3072]{1,0:T(8,128)(2,1)S(1)} collective-permute-done((bf16[128,3072]{1,0:T(8,128)(2,1)S(1)}, bf16[128,3072]{1,0:T(8,128)(2,1)S(1)}, u32[]{:S(2)}, u32[]{:S(2)}) %collective-permute-start.23) | collective-permute-done | bytes 786464 | tf_op jit(solution)/shard_map/ppermute | solution.py:390
  148.2 8.6 %global.1 = bf16[96,1024]{1,0:T(8,128)(2,1)} custom-call(s32[5]{0:T(128)S(1)} %stack.19.place_ref.at_ref, bf16[96,1024]{1,0:T(8,128)(2,1)S(1)} %get-tuple-element.14.x0, bf16[96,1024]{1,0:T(8,128)(2,1)S(1)} %collective-permute-done.13.rest_0_.x1, bf16[96,1024]{1,0:T(8,128)(2,1)S(1)} %collective-permute-done.14.rest_1_.x2, ...), custom_call_target="tpu_custom_call" | custom-call | tf_op jit(solution)/shard_map/global/pallas_call | solution.py:323
  (35 shorter events, 0.3 us)
Async XLA Ops:
  0.6 0.9 copy-start
  1.6 0.9 copy-start.2
  3.5 52.2 %collective-permute-start = (bf16[2,80,1024]{2,1,0:T(8,128)(2,1)S(1)}, bf16[2,80,1024]{2,1,0:T(8,128)(2,1)S(1)}, u32[]{:S(2)}, u32[]{:S(2)}) collective-permute-start(bf16[2,80,1024]{2,1,0:T(8,128)(2,1)S(1)} %get-tuple-element.9.after_ref.rest_0_), channel_id=1, source_target_pairs={{0,1},{1,2},{2,3},{3,4},{4,5},{5,6},{6,7},{7,8},{8,9},{9,10},{10,1... | collective-permute-start | bytes 983048 | tf_op jit(solution)/shard_map/ppermute | solution.py:409
  7.5 48.2 %collective-permute-start.1 = (bf16[2,80,1024]{2,1,0:T(8,128)(2,1)S(1)}, bf16[2,80,1024]{2,1,0:T(8,128)(2,1)S(1)}, u32[]{:S(2)}, u32[]{:S(2)}) collective-permute-start(bf16[2,80,1024]{2,1,0:T(8,128)(2,1)S(1)} %get-tuple-element.10), channel_id=1, source_target_pairs={{1,0},{2,1},{3,2},{4,3},{5,4},{6,5},{7,6},{8,7},{9,8},{10,9},{11,1... | collective-permute-start | bytes 983048 | tf_op jit(solution)/shard_map/ppermute | solution.py:410
  8.8 25.5 %collective-permute-start.4 = (bf16[64,1024]{1,0:T(8,128)(2,1)}, bf16[64,1024]{1,0:T(8,128)(2,1)S(1)}, u32[]{:S(2)}, u32[]{:S(2)}) collective-permute-start(bf16[64,1024]{1,0:T(8,128)(2,1)} %p0.1), channel_id=1, source_target_pairs={{0,4},{4,8},{8,12},{12,0},{16,28},{20,16},{24,20},{28,24},{1,5},{5... | collective-permute-start | bytes 393224 | tf_op jit(solution)/shard_map/ppermute | solution.py:388
  34.8 10.0 %collective-permute-start.6 = (bf16[32,1024]{1,0:T(8,128)(2,1)S(1)}, bf16[32,1024]{1,0:T(8,128)(2,1)S(1)}, u32[]{:S(2)}, u32[]{:S(2)}) collective-permute-start(bf16[32,1024]{1,0:T(8,128)(2,1)S(1)} %half.4), channel_id=1, source_target_pairs={{0,4},{4,8},{8,12},{12,0},{16,28},{20,16},{24,20},{28,24},{1,5},{5... | collective-permute-start | bytes 196616 | tf_op jit(solution)/shard_map/ppermute | solution.py:389
  41.3 22.3 %collective-permute-start.5 = (bf16[64,1024]{1,0:T(8,128)(2,1)S(1)}, bf16[64,1024]{1,0:T(8,128)(2,1)S(1)}, u32[]{:S(2)}, u32[]{:S(2)}) collective-permute-start(bf16[64,1024]{1,0:T(8,128)(2,1)S(1)} %collective-permute-done.4.x_ref.p1), channel_id=1, source_target_pairs={{0,16},{16,0},{1,17},{17,1},{2,18},{18,2},{3,19},{19,3},{4,20},{20... | collective-permute-start | bytes 393224 | tf_op jit(solution)/shard_map/ppermute | solution.py:390
  44.8 18.8 %collective-permute-start.7 = (bf16[32,1024]{1,0:T(8,128)(2,1)S(1)}, bf16[32,1024]{1,0:T(8,128)(2,1)S(1)}, u32[]{:S(2)}, u32[]{:S(2)}) collective-permute-start(bf16[32,1024]{1,0:T(8,128)(2,1)S(1)} %collective-permute-done.6.p3), channel_id=1, source_target_pairs={{0,16},{16,0},{1,17},{17,1},{2,18},{18,2},{3,19},{19,3},{4,20},{20... | collective-permute-start | bytes 196616 | tf_op jit(solution)/shard_map/ppermute | solution.py:390
  47.8 3.9 %copy-start.4 = (bf16[64,3072]{1,0:T(8,128)(2,1)S(1)}, bf16[64,3072]{1,0:T(8,128)(2,1)}, u32[]{:S(2)}) copy-start(bf16[64,3072]{1,0:T(8,128)(2,1)} %p0.2) | copy-start | bytes 1179652
  47.8 7.9 %copy-start.1 = (bf16[12,8,1024]{2,1,0:T(8,128)(2,1)S(1)}, bf16[12,8,1024]{2,1,0:T(8,128)(2,1)}, u32[]{:S(2)}) copy-start(bf16[12,8,1024]{2,1,0:T(8,128)(2,1)} %param.10) | copy-start | bytes 589828
  47.8 7.9 %copy-start.3 = (bf16[12,8,1024]{2,1,0:T(8,128)(2,1)S(1)}, bf16[12,8,1024]{2,1,0:T(8,128)(2,1)}, u32[]{:S(2)}) copy-start(bf16[12,8,1024]{2,1,0:T(8,128)(2,1)} %param.11) | copy-start | bytes 589828
  51.7 11.9 %copy-start.7 = (bf16[64,1024]{1,0:T(8,128)(2,1)S(1)}, bf16[64,1024]{1,0:T(8,128)(2,1)}, u32[]{:S(2)}) copy-start(bf16[64,1024]{1,0:T(8,128)(2,1)} %p0.1) | copy-start | bytes 393220
  51.7 14.6 %collective-permute-start.16 = (bf16[64,3072]{1,0:T(8,128)(2,1)S(1)}, bf16[64,3072]{1,0:T(8,128)(2,1)S(1)}, u32[]{:S(2)}, u32[]{:S(2)}) collective-permute-start(bf16[64,3072]{1,0:T(8,128)(2,1)S(1)} %copy-done.4), channel_id=1, source_target_pairs={{0,4},{4,8},{8,12},{12,0},{16,28},{20,16},{24,20},{28,24},{1,5},{5... | collective-permute-start | bytes 1179656 | tf_op jit(solution)/shard_map/ppermute | solution.py:388
  56.1 20.6 %collective-permute-start.2 = (bf16[2,128,1024]{2,1,0:T(8,128)(2,1)S(1)}, bf16[2,128,1024]{2,1,0:T(8,128)(2,1)S(1)}, u32[]{:S(2)}, u32[]{:S(2)}) collective-permute-start(bf16[2,128,1024]{2,1,0:T(8,128)(2,1)S(1)} %get-tuple-element.11.rest_0_), channel_id=1, source_target_pairs={{0,16},{16,32},{32,48},{48,64},{64,80},{80,96},{96,112},{112,128},... | collective-permute-start | bytes 1572872 | tf_op jit(solution)/shard_map/ppermute | solution.py:414
  61.7 15.1 %collective-permute-start.3 = (bf16[2,128,1024]{2,1,0:T(8,128)(2,1)S(1)}, bf16[2,128,1024]{2,1,0:T(8,128)(2,1)S(1)}, u32[]{:S(2)}, u32[]{:S(2)}) collective-permute-start(bf16[2,128,1024]{2,1,0:T(8,128)(2,1)S(1)} %get-tuple-element.12.rest_1_), channel_id=1, source_target_pairs={{0,496},{16,0},{32,16},{48,32},{64,48},{80,64},{96,80},{112,96},{1... | collective-permute-start | bytes 1572872 | tf_op jit(solution)/shard_map/ppermute | solution.py:415
  64.2 19.5 %copy-start.5 = (bf16[12,8,1024]{2,1,0:T(8,128)(2,1)S(1)}, bf16[12,8,1024]{2,1,0:T(8,128)(2,1)}, u32[]{:S(2)}) copy-start(bf16[12,8,1024]{2,1,0:T(8,128)(2,1)} %param.9) | copy-start | bytes 589828
  64.2 12.5 %collective-permute-start.8 = (bf16[256,1024]{1,0:T(8,128)(2,1)S(1)}, bf16[256,1024]{1,0:T(8,128)(2,1)S(1)}, u32[]{:S(2)}, u32[]{:S(2)}) collective-permute-start(bf16[256,1024]{1,0:T(8,128)(2,1)S(1)} %place.2.p0.rest_0_), channel_id=1, source_target_pairs={{0,1},{1,2},{2,3},{3,0},{16,19},{17,16},{18,17},{19,18},{4,5},{5,6... | collective-permute-start | bytes 1572872 | tf_op jit(solution)/shard_map/ppermute | solution.py:388
  66.9 12.7 %collective-permute-start.18 = (bf16[32,3072]{1,0:T(8,128)(2,1)S(1)}, bf16[32,3072]{1,0:T(8,128)(2,1)S(1)}, u32[]{:S(2)}, u32[]{:S(2)}) collective-permute-start(bf16[32,3072]{1,0:T(8,128)(2,1)S(1)} %half.6), channel_id=1, source_target_pairs={{0,4},{4,8},{8,12},{12,0},{16,28},{20,16},{24,20},{28,24},{1,5},{5... | collective-permute-start | bytes 589832 | tf_op jit(solution)/shard_map/ppermute | solution.py:389
  68.8 18.0 %collective-permute-start.17 = (bf16[64,3072]{1,0:T(8,128)(2,1)S(1)}, bf16[64,3072]{1,0:T(8,128)(2,1)S(1)}, u32[]{:S(2)}, u32[]{:S(2)}) collective-permute-start(bf16[64,3072]{1,0:T(8,128)(2,1)S(1)} %collective-permute-done.16.x_ref.p1), channel_id=1, source_target_pairs={{0,16},{16,0},{1,17},{17,1},{2,18},{18,2},{3,19},{19,3},{4,20},{20... | collective-permute-start | bytes 1179656 | tf_op jit(solution)/shard_map/ppermute | solution.py:390
  77.4 9.4 %collective-permute-start.10 = (bf16[128,1024]{1,0:T(8,128)(2,1)S(1)}, bf16[128,1024]{1,0:T(8,128)(2,1)S(1)}, u32[]{:S(2)}, u32[]{:S(2)}) collective-permute-start(bf16[128,1024]{1,0:T(8,128)(2,1)S(1)} %half.5), channel_id=1, source_target_pairs={{0,1},{1,2},{2,3},{3,0},{16,19},{17,16},{18,17},{19,18},{4,5},{5,6... | collective-permute-start | bytes 786440 | tf_op jit(solution)/shard_map/ppermute | solution.py:389
  79.6 7.2 %collective-permute-start.19 = (bf16[32,3072]{1,0:T(8,128)(2,1)S(1)}, bf16[32,3072]{1,0:T(8,128)(2,1)S(1)}, u32[]{:S(2)}, u32[]{:S(2)}) collective-permute-start(bf16[32,3072]{1,0:T(8,128)(2,1)S(1)} %collective-permute-done.18.p3), channel_id=1, source_target_pairs={{0,16},{16,0},{1,17},{17,1},{2,18},{18,2},{3,19},{19,3},{4,20},{20... | collective-permute-start | bytes 589832 | tf_op jit(solution)/shard_map/ppermute | solution.py:390
  86.8 11.0 %copy-start.6 = (bf16[12,8,1024]{2,1,0:T(8,128)(2,1)S(1)}, bf16[12,8,1024]{2,1,0:T(8,128)(2,1)}, u32[]{:S(2)}) copy-start(bf16[12,8,1024]{2,1,0:T(8,128)(2,1)} %param.8) | copy-start | bytes 589828
  86.8 11.1 %copy-start.8 = (f32[1024]{0:T(1024)S(1)}, f32[1024]{0:T(1024)}, u32[]{:S(2)}) copy-start(f32[1024]{0:T(1024)} %param.14) | copy-start | bytes 12292
  87.5 42.1 %collective-permute-start.20 = (bf16[256,3072]{1,0:T(8,128)(2,1)S(1)}, bf16[256,3072]{1,0:T(8,128)(2,1)S(1)}, u32[]{:S(2)}, u32[]{:S(2)}) collective-permute-start(bf16[256,3072]{1,0:T(8,128)(2,1)S(1)} %place.3.rest_0_.rest_5_.rest_10_), channel_id=1, source_target_pairs={{0,1},{1,2},{2,3},{3,0},{16,19},{17,16},{18,17},{19,18},{4,5},{5,6... | collective-permute-start | bytes 4718600 | tf_op jit(solution)/shard_map/ppermute | solution.py:388
  92.3 4.3 %collective-permute-start.9 = (bf16[256,1024]{1,0:T(8,128)(2,1)S(1)}, bf16[256,1024]{1,0:T(8,128)(2,1)S(1)}, u32[]{:S(2)}, u32[]{:S(2)}) collective-permute-start(bf16[256,1024]{1,0:T(8,128)(2,1)S(1)} %collective-permute-done.8.x_ref.p1), channel_id=1, source_target_pairs={{0,16},{16,0},{1,17},{17,1},{2,18},{18,2},{3,19},{19,3},{4,20},{20... | collective-permute-start | bytes 1572872 | tf_op jit(solution)/shard_map/ppermute | solution.py:390
  94.3 3.6 %collective-permute-start.11 = (bf16[128,1024]{1,0:T(8,128)(2,1)S(1)}, bf16[128,1024]{1,0:T(8,128)(2,1)S(1)}, u32[]{:S(2)}, u32[]{:S(2)}) collective-permute-start(bf16[128,1024]{1,0:T(8,128)(2,1)S(1)} %collective-permute-done.10.p3.rest_0_), channel_id=1, source_target_pairs={{0,16},{16,0},{1,17},{17,1},{2,18},{18,2},{3,19},{19,3},{4,20},{20... | collective-permute-start | bytes 786440 | tf_op jit(solution)/shard_map/ppermute | solution.py:390
  99.7 15.4 %collective-permute-start.12 = (bf16[96,1024]{1,0:T(8,128)(2,1)S(1)}, bf16[96,1024]{1,0:T(8,128)(2,1)S(1)}, u32[]{:S(2)}, u32[]{:S(2)}) collective-permute-start(bf16[96,1024]{1,0:T(8,128)(2,1)S(1)} %get-tuple-element.14.x0), channel_id=1, source_target_pairs={{0,4},{4,8},{8,12},{12,16},{16,20},{20,24},{24,28},{28,32},{32,36}... | collective-permute-start | bytes 589832 | tf_op jit(solution)/shard_map/ppermute | solution.py:423
  115.2 9.6 %collective-permute-start.13 = (bf16[96,1024]{1,0:T(8,128)(2,1)S(1)}, bf16[96,1024]{1,0:T(8,128)(2,1)S(1)}, u32[]{:S(2)}, u32[]{:S(2)}) collective-permute-start(bf16[96,1024]{1,0:T(8,128)(2,1)S(1)} %get-tuple-element.18), channel_id=1, source_target_pairs={{0,1},{1,2},{2,3},{3,0},{4,5},{5,6},{6,7},{7,4},{8,9},{9,10},{10,1... | collective-permute-start | bytes 589832 | tf_op jit(solution)/shard_map/ppermute | solution.py:427
  117.1 9.8 %collective-permute-start.14 = (bf16[96,1024]{1,0:T(8,128)(2,1)S(1)}, bf16[96,1024]{1,0:T(8,128)(2,1)S(1)}, u32[]{:S(2)}, u32[]{:S(2)}) collective-permute-start(bf16[96,1024]{1,0:T(8,128)(2,1)S(1)} %get-tuple-element.17), channel_id=1, source_target_pairs={{0,2},{1,3},{2,0},{3,1},{4,6},{5,7},{6,4},{7,5},{8,10},{9,11},{10,... | collective-permute-start | bytes 589832 | tf_op jit(solution)/shard_map/ppermute | solution.py:427
  122.5 7.0 %collective-permute-start.15 = (bf16[96,1024]{1,0:T(8,128)(2,1)S(1)}, bf16[96,1024]{1,0:T(8,128)(2,1)S(1)}, u32[]{:S(2)}, u32[]{:S(2)}) collective-permute-start(bf16[96,1024]{1,0:T(8,128)(2,1)S(1)} %get-tuple-element.16), channel_id=1, source_target_pairs={{0,3},{1,0},{2,1},{3,2},{4,7},{5,4},{6,5},{7,6},{8,11},{9,8},{10,9... | collective-permute-start | bytes 589832 | tf_op jit(solution)/shard_map/ppermute | solution.py:427
  130.2 13.0 %collective-permute-start.22 = (bf16[128,3072]{1,0:T(8,128)(2,1)S(1)}, bf16[128,3072]{1,0:T(8,128)(2,1)S(1)}, u32[]{:S(2)}, u32[]{:S(2)}) collective-permute-start(bf16[128,3072]{1,0:T(8,128)(2,1)S(1)} %half.7), channel_id=1, source_target_pairs={{0,1},{1,2},{2,3},{3,0},{16,19},{17,16},{18,17},{19,18},{4,5},{5,6... | collective-permute-start | bytes 2359304 | tf_op jit(solution)/shard_map/ppermute | solution.py:389
  134.2 12.1 %collective-permute-start.21 = (bf16[256,3072]{1,0:T(8,128)(2,1)S(1)}, bf16[256,3072]{1,0:T(8,128)(2,1)S(1)}, u32[]{:S(2)}, u32[]{:S(2)}) collective-permute-start(bf16[256,3072]{1,0:T(8,128)(2,1)S(1)} %collective-permute-done.20.x_ref.rest_1_.rest_6_.rest_11_), channel_id=1, source_target_pairs={{0,16},{16,0},{1,17},{17,1},{2,18},{18,2},{3,19},{19,3},{4,20},{20... | collective-permute-start | bytes 4718600 | tf_op jit(solution)/shard_map/ppermute | solution.py:390
  143.2 5.0 %collective-permute-start.23 = (bf16[128,3072]{1,0:T(8,128)(2,1)S(1)}, bf16[128,3072]{1,0:T(8,128)(2,1)S(1)}, u32[]{:S(2)}, u32[]{:S(2)}) collective-permute-start(bf16[128,3072]{1,0:T(8,128)(2,1)S(1)} %collective-permute-done.22.rest_3_.rest_8_.rest_13_), channel_id=1, source_target_pairs={{0,16},{16,0},{1,17},{17,1},{2,18},{18,2},{3,19},{19,3},{4,20},{20... | collective-permute-start | bytes 2359304 | tf_op jit(solution)/shard_map/ppermute | solution.py:390

commit v4 on v3

--- a/solution.py
+++ b/solution.py
@@ -259,10 +259,10 @@
     return [pl.ds(pl.multiple_of(start, half), deep if n < 3 else half) for n, start in enumerate(starts)]
 
 
-def project_kernel(at_ref, x_ref, tok_ref, gain_ref, p0, p1, p2, p3, p4, hid_ref, norm_ref):
+def project_kernel(at_ref, x_ref, tok_ref, gain_ref, p0, p1, p2, p3, hid_ref, norm_ref):
     width = x_ref.shape[1]
     total = None
-    for lanes, ref in zip(piece_lanes(at_ref, width // 4), (p0, p1, p2, p3, p4)):
+    for lanes, ref in zip(piece_lanes(at_ref, width // 4), unpacked(p0, p1, p2, p3)):
         term = jnp.dot(x_ref[:, lanes], ref[...], preferred_element_type=jnp.float32)
         total = term if total is None else total + term
     hidden = (tok_ref[...].astype(jnp.float32) + total).astype(jnp.bfloat16)
@@ -287,14 +287,15 @@
     )(at, x, tok, gain, *pieces)
 
 
-def global_kernel(at_ref, x0, x1, x2, x3, x4, *rest):
+def global_kernel(at_ref, own_ref, slots_ref, *rest):
     weights, (out_ref, xbuf) = rest[:15], rest[15:]
-    width = x0.shape[1]
+    width = own_ref.shape[1]
 
     @pl.when(pl.program_id(0) == 0)
     def _():
-        for at, ref in enumerate((x0, x1, x2, x3, x4)):
-            xbuf[CELLS * at : CELLS * at + CELLS] = ref[...]
+        xbuf[0:CELLS] = own_ref[...]
+        for at in range(4):
+            xbuf[CELLS * at + CELLS : CELLS * at + 2 * CELLS] = slots_ref[at]
 
     spans = piece_lanes(at_ref, width // 4)
 
@@ -313,10 +314,13 @@
         out_ref[:, lanes] = pair_attention(q[:, lanes], k[:, lanes], v[:, lanes], None)
 
 
-def global_layer(at, blocks, pieces):
-    cells, width = blocks[0].shape
+def global_layer(at, own, slots, pieces):
+    cells, width = own.shape
     steps = width // 256
-    whole = pl.BlockSpec((cells, width), lambda g, c: (0, 0))
+    whole = [
+        pl.BlockSpec((cells, width), lambda g, c: (0, 0)),
+        pl.BlockSpec(slots.shape, lambda g, c: (0, 0, 0)),
+    ]
     weights = [
         pl.BlockSpec((piece.shape[0], 256), lambda g, c, t=t: (0, steps * t + g)) for t in range(3) for piece in pieces
     ]
@@ -326,16 +330,16 @@
         grid_spec=pltpu.PrefetchScalarGridSpec(
             num_scalar_prefetch=1,
             grid=(steps,),
-            in_specs=[whole] * 5 + weights,
+            in_specs=whole + weights,
             out_specs=pl.BlockSpec((cells, 256), lambda g, c: (0, g)),
             scratch_shapes=[pltpu.VMEM((5 * cells, width), jnp.bfloat16)],
         ),
         compiler_params=params(20),
         name="global",
-    )(at, *blocks, *(pieces * 3))
-
-
-def place_kernel(at_ref, p0, p1, p2, p3, p4, *rest):
+    )(at, own, slots, *(pieces * 3))
+
+
+def place_kernel(at_ref, p0, p1, p2, p3, *rest):
     out_ref = rest[-1]
     rows = p0.shape[0]
     half = rows // 2
@@ -348,7 +352,7 @@
         far + core * half,
         far + (1 - core) * half,
     )
-    for start, ref in zip(starts, (p0, p1, p2, p3, p4)):
+    for start, ref in zip(starts, unpacked(p0, p1, p2, p3)):
         to = pl.ds(pl.multiple_of(start, half), ref.shape[0])
         out_ref[to] = ref[...]
 
@@ -382,12 +386,52 @@
     )(at, x, *after)
 
 
+def pack_kernel(a_ref, b_ref, out_ref):
+    rows = a_ref.shape[0]
+    out_ref[0:rows] = a_ref[...]
+    out_ref[rows : rows + b_ref.shape[0]] = b_ref[...]
+
+
+def pack(a, b):
+    return pl.pallas_call(
+        pack_kernel,
+        out_shape=jax.ShapeDtypeStruct((a.shape[0] + b.shape[0], a.shape[1]), a.dtype),
+        in_specs=[vspec(), vspec()],
+        out_specs=vspec(),
+        compiler_params=params(8),
+        name="pack",
+    )(a, b)
+
+
+SWAP = [(0, 1), (1, 0)]
+ROLES = [(i, (i + 1) % 4) for i in range(4)] + [(4 + i, 4 + (i + 3) % 4) for i in range(4)]
+
+
 def gathered(rows, axis, at, after):
-    roles = [(i, (i + 1) % 4) for i in range(4)] + [(4 + i, 4 + (i + 3) % 4) for i in range(4)]
-    swap = [(0, 1), (1, 0)]
-    near = lax.ppermute(rows, ("c", axis), roles)
-    far = lax.ppermute(half_of(at, near, after), ("c", axis), roles)
-    return [rows, near, lax.ppermute(near, "c", swap), far, lax.ppermute(far, "c", swap)]
+    near = lax.ppermute(rows, ("c", axis), ROLES)
+    far = lax.ppermute(half_of(at, near, after), ("c", axis), ROLES)
+    return [rows, near, far, lax.ppermute(pack(near, far), "c", SWAP)]
+
+
+def unpacked(own, near, far, others):
+    rows = own.shape[0]
+    return [own, near, others.at[0:rows], far, others.at[rows : rows + rows // 2]]
+
+
+def spread_kernel(at_ref, own_ref, behind_ref, after_ref, out_ref):
+    for slot in range(4):
+        out_ref[slot] = jnp.where(slot > at_ref[1], own_ref[...], behind_ref[...])
+
+
+def spread(at, own, behind, after):
+    return pl.pallas_call(
+        spread_kernel,
+        out_shape=jax.ShapeDtypeStruct((4,) + own.shape, own.dtype),
+        in_specs=[sspec(), vspec(), vspec(), anyspec()],
+        out_specs=vspec(),
+        compiler_params=params(8),
+        name="spread",
+    )(at, own, behind, after)
 
 
 def ring(count, by):
@@ -409,25 +453,26 @@
     low = lax.ppermute(up, LAT, [(i, i + 1) for i in range(lat_count - 1)])
     high = lax.ppermute(down, LAT, [(i + 1, i) for i in range(lat_count - 1)])
     bias = bias_table(position_bias, at, up)
-    pieces_o = gathered(output_weight, "zh", at, [up])
+    pieces_o = gathered(output_weight, "zh", at, [bias])
     to_east, to_west = sides(low, high, k, v, bias)
     west = lax.ppermute(to_east, LON, ring(lon_count, 1))
     east = lax.ppermute(to_west, LON, ring(lon_count, -1))
     rows_o = place_rows(at, pieces_o, [to_east, to_west])
-    global_weight, pieces_o[3] = lax.optimization_barrier((global_weight, pieces_o[3]))
+    global_weight, to_east, pieces_o[2] = lax.optimization_barrier((global_weight, to_east, pieces_o[2]))
     pieces_g = gathered(global_weight, "zh", at, [rows_o])
     pieces_o = gathered(rows_o, "x", at, [west, east])
     local_out = attend(q, k, v, low, high, west, east, bias)
-    rows_g = place_rows(at, pieces_g, [pieces_o[3], local_out])
+    rows_g = place_rows(at, pieces_g, [pieces_o[2], local_out])
     hidden, normed = project(at, local_out, tok, norm_gain.reshape(1, width), pieces_o)
     behind = lax.ppermute(normed, LON + ("zh",), ring(lon_count * zs, 1))
-    blocks = [normed]
-    for by in range(1, xs):
-        sent = jnp.where(x + by < xs, normed, behind)
-        blocks.append(lax.ppermute(sent, "x", ring(xs, by)))
-    blocks.append(behind)
-    pieces_g = gathered(rows_g, "x", at, blocks[1:xs])
-    attended = global_layer(at, blocks, pieces_g)
+    near = lax.ppermute(rows_g, ("c", "x"), ROLES)
+    half = half_of(at, near, [behind])
+    far = lax.ppermute(half, ("c", "x"), ROLES)
+    slots = lax.all_to_all(spread(at, normed, behind, half), "x", 0, 0)
+    near_other = lax.ppermute(near, "c", SWAP)
+    late, slots = lax.optimization_barrier((far, slots))
+    far_other = lax.ppermute(late, "c", SWAP)
+    attended = global_layer(at, normed, slots, [rows_g, near, near_other, late, far_other])
     return hidden.reshape(tokens.shape), attended.reshape(tokens.shape)
 
 

time: 158 us -> 148 us (0.937)
  waiting for transfers between devices: 40.9 us -> 21.6 us
  blocking collectives: 0 us -> 15.3 us
  starting transfers between devices: 89.4 us -> 82.9 us
    ppermute x19 -> x13, waiting for transfers between devices: 27.7 us -> 11 us  [the longest x3 4.56 us: gathered(): far = lax.ppermute(half_of(at, near, after), ('c', axis), ROLES)]
    all_to_all x0 -> x1, blocking collectives: none -> 15.3 us  [body(): slots = lax.all_to_all(spread(at, normed, behind, half), 'x', 0, 0)]
    ppermute x19 -> x13, starting transfers between devices: 74.5 us -> 69.4 us  [the longest x3 24.1 us: gathered(): near = lax.ppermute(rows, ('c', axis), ROLES)]
    ppermute x1, waiting for transfers between devices: 13.2 us -> 10.5 us  [body(): behind = lax.ppermute(normed, LON + ('zh',), ring(lon_count * zs, 1))]
    ppermute x1, starting transfers between devices: 5.55 us -> 3.59 us  [body(): west = lax.ppermute(to_east, LON, ring(lon_count, 1))]
  transfers between devices with their start and end apart: 24 -> 18, of which waited for: 9 -> 7; matrix products, arithmetic and copies ran while one was open for 1% -> 1% of each run, Pallas kernels for 7% -> 8%
where the time goes in v4:
time: 148 us; the launch traced here: 147 us
  starting transfers between devices  82.9 us (56%)
  Pallas kernels  23 us (16%)
  waiting for transfers between devices  21.6 us (15%)
  blocking collectives  15.3 us (10%)
  local copies, waits for them, and re-layouts  3.03 us (2%)
    ppermute x3, starting transfers between devices, gathered(): near = lax.ppermute(rows, ('c', axis), ROLES)  24.1 us
    ppermute x3, starting transfers between devices, gathered(): far = lax.ppermute(half_of(at, near, after), ('c', axis), ROLES)  23.3 us
    all_to_all x1, blocking collectives, body(): slots = lax.all_to_all(spread(at, normed, behind, half), 'x', 0, 0)  15.3 us
    ppermute x1, waiting for transfers between devices, body(): behind = lax.ppermute(normed, LON + ('zh',), ring(lon_count * zs, 1))  10.5 us
    pallas_call x1, Pallas kernels, global_layer(): pl.pallas_call(global_kernel, out_shape=jax.ShapeDtypeStruct((cells, widt...  8.56 us
    ppermute x3, starting transfers between devices, gathered(): return [rows, near, far, lax.ppermute(pack(near, far), 'c', SWAP)]  6.26 us
    ppermute x1, starting transfers between devices, body(): near = lax.ppermute(rows_g, ('c', 'x'), ROLES)  5.16 us
    ppermute x1, starting transfers between devices, body(): low = lax.ppermute(up, LAT, [(i, i + 1) for i in range(lat_count - 1)])  4.59 us
  transfers between devices with their start and end apart: 18, of which 7 were waited for; matrix products, arithmetic and copies ran while one was open for 1% of the time, Pallas kernels for 8%

profile of v4, /device:TPU:1, one launch (start us, length us, event | category | flops | bytes accessed | tf_op | source)
XLA Modules:
  0.0 146.8 jit_solution(6861775929460153128)
XLA Ops:
  0.6 0.0 copy-start
  0.6 0.9 copy-done
  1.6 0.9 copy-done.2
  2.5 1.0 edges.1
  3.5 1.3 collective-permute-start.1
  4.8 4.6 %collective-permute-start = (bf16[2,80,1024]{2,1,0:T(8,128)(2,1)S(1)}, bf16[2,80,1024]{2,1,0:T(8,128)(2,1)S(1)}, u32[]{:S(2)}, u32[]{:S(2)}) collective-permute-start(bf16[2,80,1024]{2,1,0:T(8,128)(2,1)S(1)} %get-tuple-element.11.after_ref), channel_id=1, source_target_pairs={{0,1},{1,2},{2,3},{3,4},{4,5},{5,6},{6,7},{7,8},{8,9},{9,10},{10,1... | collective-permute-start | bytes 983048 | tf_op jit(solution)/shard_map/ppermute | solution.py:453
  9.4 11.9 %collective-permute-start.4 = (bf16[64,1024]{1,0:T(8,128)(2,1)}, bf16[64,1024]{1,0:T(8,128)(2,1)S(1)}, u32[]{:S(2)}, u32[]{:S(2)}) collective-permute-start(bf16[64,1024]{1,0:T(8,128)(2,1)} %p0.1), channel_id=1, source_target_pairs={{0,4},{4,8},{8,12},{12,0},{16,28},{20,16},{24,20},{28,24},{1,5},{5... | collective-permute-start | bytes 393224 | tf_op jit(solution)/shard_map/ppermute | solution.py:411
  21.3 0.9 copy.11
  22.2 0.1 reshape.31
  22.3 0.1 stack.19.place_ref.at_ref
  22.4 3.8 %bias.1.after_ref.bias_ref.rest_0_ = f32[16,96,512]{2,1,0:T(8,128)S(1)} custom-call(s32[5]{0:T(128)S(1)} %stack.19.place_ref.at_ref, f32[16,256]{1,0:T(8,128)S(1)} %pad.4.table_ref, bf16[2,80,1024]{2,1,0:T(8,128)(2,1)S(1)} %get-tuple-element.11.after_ref), custom_call_target="tpu_custom_call" | custom-call | tf_op jit(solution)/shard_map/bias/pallas_call | solution.py:183
  26.3 0.0 copy-start.1
  26.3 0.0 copy-start.3
  26.3 2.3 %collective-permute-done.4.x_ref.a_ref.p1 = bf16[64,1024]{1,0:T(8,128)(2,1)S(1)} collective-permute-done((bf16[64,1024]{1,0:T(8,128)(2,1)}, bf16[64,1024]{1,0:T(8,128)(2,1)S(1)}, u32[]{:S(2)}, u32[]{:S(2)}) %collective-permute-start.4) | collective-permute-done | bytes 131104 | tf_op jit(solution)/shard_map/ppermute | solution.py:411
  28.6 0.6 half.4
  29.2 8.3 %collective-permute-start.5 = (bf16[32,1024]{1,0:T(8,128)(2,1)S(1)}, bf16[32,1024]{1,0:T(8,128)(2,1)S(1)}, u32[]{:S(2)}, u32[]{:S(2)}) collective-permute-start(bf16[32,1024]{1,0:T(8,128)(2,1)S(1)} %half.4), channel_id=1, source_target_pairs={{0,4},{4,8},{8,12},{12,0},{16,28},{20,16},{24,20},{28,24},{1,5},{5... | collective-permute-start | bytes 196616 | tf_op jit(solution)/shard_map/ppermute | solution.py:412
  37.5 0.4 sides.1
  38.0 0.8 collective-permute-done.5.b_ref.p2
  38.8 5.9 %collective-permute-start.10 = (bf16[64,3072]{1,0:T(8,128)(2,1)S(1)}, bf16[64,3072]{1,0:T(8,128)(2,1)S(1)}, u32[]{:S(2)}, u32[]{:S(2)}) collective-permute-start(bf16[64,3072]{1,0:T(8,128)(2,1)S(1)} %copy-done.4), channel_id=1, source_target_pairs={{0,4},{4,8},{8,12},{12,0},{16,28},{20,16},{24,20},{28,24},{1,5},{5... | collective-permute-start | bytes 1179656 | tf_op jit(solution)/shard_map/ppermute | solution.py:411
  44.7 1.9 %collective-permute-start.6 = (bf16[96,1024]{1,0:T(8,128)(2,1)S(1)}, bf16[96,1024]{1,0:T(8,128)(2,1)S(1)}, u32[]{:S(2)}, u32[]{:S(2)}) collective-permute-start(bf16[96,1024]{1,0:T(8,128)(2,1)S(1)} %pack.3), channel_id=1, source_target_pairs={{0,16},{16,0},{1,17},{17,1},{2,18},{18,2},{3,19},{19,3},{4,20},{20... | collective-permute-start | bytes 589832 | tf_op jit(solution)/shard_map/ppermute | solution.py:413
  46.7 3.6 %collective-permute-start.2 = (bf16[2,128,1024]{2,1,0:T(8,128)(2,1)S(1)}, bf16[2,128,1024]{2,1,0:T(8,128)(2,1)S(1)}, u32[]{:S(2)}, u32[]{:S(2)}) collective-permute-start(bf16[2,128,1024]{2,1,0:T(8,128)(2,1)S(1)} %get-tuple-element.13.rest_0_), channel_id=1, source_target_pairs={{0,16},{16,32},{32,48},{48,64},{64,80},{80,96},{96,112},{112,128},... | collective-permute-start | bytes 1572872 | tf_op jit(solution)/shard_map/ppermute | solution.py:458
  50.3 1.9 %collective-permute-start.3 = (bf16[2,128,1024]{2,1,0:T(8,128)(2,1)S(1)}, bf16[2,128,1024]{2,1,0:T(8,128)(2,1)S(1)}, u32[]{:S(2)}, u32[]{:S(2)}) collective-permute-start(bf16[2,128,1024]{2,1,0:T(8,128)(2,1)S(1)} %get-tuple-element.14.rest_1_), channel_id=1, source_target_pairs={{0,496},{16,0},{32,16},{48,32},{64,48},{80,64},{96,80},{112,96},{1... | collective-permute-start | bytes 1572872 | tf_op jit(solution)/shard_map/ppermute | solution.py:459
  52.2 0.6 place.2.p0.rest_0_
  52.8 6.4 %collective-permute-start.7 = (bf16[256,1024]{1,0:T(8,128)(2,1)S(1)}, bf16[256,1024]{1,0:T(8,128)(2,1)S(1)}, u32[]{:S(2)}, u32[]{:S(2)}) collective-permute-start(bf16[256,1024]{1,0:T(8,128)(2,1)S(1)} %place.2.p0.rest_0_), channel_id=1, source_target_pairs={{0,1},{1,2},{2,3},{3,0},{16,19},{17,16},{18,17},{19,18},{4,5},{5,6... | collective-permute-start | bytes 1572872 | tf_op jit(solution)/shard_map/ppermute | solution.py:411
  59.2 0.6 half.6
  59.8 5.9 %collective-permute-start.11 = (bf16[32,3072]{1,0:T(8,128)(2,1)S(1)}, bf16[32,3072]{1,0:T(8,128)(2,1)S(1)}, u32[]{:S(2)}, u32[]{:S(2)}) collective-permute-start(bf16[32,3072]{1,0:T(8,128)(2,1)S(1)} %half.6), channel_id=1, source_target_pairs={{0,4},{4,8},{8,12},{12,0},{16,28},{20,16},{24,20},{28,24},{1,5},{5... | collective-permute-start | bytes 589832 | tf_op jit(solution)/shard_map/ppermute | solution.py:412
  65.7 3.5 %collective-permute-done.11.b_ref.p2 = bf16[32,3072]{1,0:T(8,128)(2,1)S(1)} collective-permute-done((bf16[32,3072]{1,0:T(8,128)(2,1)S(1)}, bf16[32,3072]{1,0:T(8,128)(2,1)S(1)}, u32[]{:S(2)}, u32[]{:S(2)}) %collective-permute-start.11) | collective-permute-done | bytes 196640 | tf_op jit(solution)/shard_map/ppermute | solution.py:412
  69.2 2.4 %collective-permute-start.12 = (bf16[96,3072]{1,0:T(8,128)(2,1)S(1)}, bf16[96,3072]{1,0:T(8,128)(2,1)S(1)}, u32[]{:S(2)}, u32[]{:S(2)}) collective-permute-start(bf16[96,3072]{1,0:T(8,128)(2,1)S(1)} %pack.5), channel_id=1, source_target_pairs={{0,16},{16,0},{1,17},{17,1},{2,18},{18,2},{3,19},{19,3},{4,20},{20... | collective-permute-start | bytes 1769480 | tf_op jit(solution)/shard_map/ppermute | solution.py:413
  71.6 0.6 half.5
  72.2 9.1 %collective-permute-start.8 = (bf16[128,1024]{1,0:T(8,128)(2,1)S(1)}, bf16[128,1024]{1,0:T(8,128)(2,1)S(1)}, u32[]{:S(2)}, u32[]{:S(2)}) collective-permute-start(bf16[128,1024]{1,0:T(8,128)(2,1)S(1)} %half.5), channel_id=1, source_target_pairs={{0,1},{1,2},{2,3},{3,0},{16,19},{17,16},{18,17},{19,18},{4,5},{5,6... | collective-permute-start | bytes 786440 | tf_op jit(solution)/shard_map/ppermute | solution.py:412
  81.4 3.0 %local.1.x_ref.rest_1_ = bf16[96,1024]{1,0:T(8,128)(2,1)S(1)} custom-call(bf16[96,1024]{1,0:T(8,128)(2,1)S(1)} %bitcast.17, bf16[96,1024]{1,0:T(8,128)(2,1)S(1)} %bitcast.13, bf16[96,1024]{1,0:T(8,128)(2,1)S(1)} %bitcast.16, bf16[2,80,1024]{2,1,0:T(8,128)(2,1)S(1)} %collective-permute-done.low_ref, bf16[2,80,1024]{2,1,0:T(8,128)(2,1)S(1)} %collective-permute-done.1.high_ref, ...), custom_call_target="tpu_custom_call" | custom-call | tf_op jit(solution)/shard_map/local/pallas_call | solution.py:234
  84.4 0.3 collective-permute-done.8.b_ref.p2.rest_0_
  84.7 0.7 place.3.rest_0_.rest_5_.rest_10_
  85.4 5.2 %collective-permute-start.13 = (bf16[256,3072]{1,0:T(8,128)(2,1)S(1)}, bf16[256,3072]{1,0:T(8,128)(2,1)S(1)}, u32[]{:S(2)}, u32[]{:S(2)}) collective-permute-start(bf16[256,3072]{1,0:T(8,128)(2,1)S(1)} %place.3.rest_0_.rest_5_.rest_10_), channel_id=1, source_target_pairs={{0,1},{1,2},{2,3},{3,0},{16,19},{17,16},{18,17},{19,18},{4,5},{5,6... | collective-permute-start | bytes 4718600 | tf_op jit(solution)/shard_map/ppermute | solution.py:468
  90.5 0.1 pack.4
  90.6 1.9 %collective-permute-start.9 = (bf16[384,1024]{1,0:T(8,128)(2,1)S(1)}, bf16[384,1024]{1,0:T(8,128)(2,1)S(1)}, u32[]{:S(2)}, u32[]{:S(2)}) collective-permute-start(bf16[384,1024]{1,0:T(8,128)(2,1)S(1)} %pack.4), channel_id=1, source_target_pairs={{0,16},{16,0},{1,17},{17,1},{2,18},{18,2},{3,19},{19,3},{4,20},{20... | collective-permute-start | bytes 2359304 | tf_op jit(solution)/shard_map/ppermute | solution.py:413
  92.5 2.3 %collective-permute-done.9.p3 = bf16[384,1024]{1,0:T(8,128)(2,1)S(1)} collective-permute-done((bf16[384,1024]{1,0:T(8,128)(2,1)S(1)}, bf16[384,1024]{1,0:T(8,128)(2,1)S(1)}, u32[]{:S(2)}, u32[]{:S(2)}) %collective-permute-start.9) | collective-permute-done | bytes 786464 | tf_op jit(solution)/shard_map/ppermute | solution.py:413
  94.8 1.9 %project.1 = (bf16[96,1024]{1,0:T(8,128)(2,1)}, bf16[96,1024]{1,0:T(8,128)(2,1)S(1)}) custom-call(s32[5]{0:T(128)S(1)} %stack.19.place_ref.at_ref, bf16[96,1024]{1,0:T(8,128)(2,1)S(1)} %local.1.x_ref.rest_1_, bf16[96,1024]{1,0:T(8,128)(2,1)S(1)} %bitcast.18, f32[1,1024]{1,0:T(1,128)S(1)} %bitcast.19, bf16[256,1024]{1,0:T(8,128)(2,1)S(1)} %place.2.p0.rest_0_, ...), custom_call_target="tpu_custom_call" | custom-call | tf_op jit(solution)/shard_map/project/pallas_call | solution.py:280
  96.7 2.1 %collective-permute-start.14 = (bf16[96,1024]{1,0:T(8,128)(2,1)S(1)}, bf16[96,1024]{1,0:T(8,128)(2,1)S(1)}, u32[]{:S(2)}, u32[]{:S(2)}) collective-permute-start(bf16[96,1024]{1,0:T(8,128)(2,1)S(1)} %get-tuple-element.16.own_ref), channel_id=1, source_target_pairs={{0,4},{4,8},{8,12},{12,16},{16,20},{20,24},{24,28},{28,32},{32,36}... | collective-permute-start | bytes 589832 | tf_op jit(solution)/shard_map/ppermute | solution.py:467
  98.7 10.5 %collective-permute-done.14.rest_0_.behind_ref = bf16[96,1024]{1,0:T(8,128)(2,1)S(1)} collective-permute-done((bf16[96,1024]{1,0:T(8,128)(2,1)S(1)}, bf16[96,1024]{1,0:T(8,128)(2,1)S(1)}, u32[]{:S(2)}, u32[]{:S(2)}) %collective-permute-start.14) | collective-permute-done | bytes 196640 | tf_op jit(solution)/shard_map/ppermute | solution.py:467
  109.3 0.6 half.7.after_ref
  109.9 4.6 %collective-permute-start.15 = (bf16[128,3072]{1,0:T(8,128)(2,1)S(1)}, bf16[128,3072]{1,0:T(8,128)(2,1)S(1)}, u32[]{:S(2)}, u32[]{:S(2)}) collective-permute-start(bf16[128,3072]{1,0:T(8,128)(2,1)S(1)} %half.7.after_ref), channel_id=1, source_target_pairs={{0,1},{1,2},{2,3},{3,0},{16,19},{17,16},{18,17},{19,18},{4,5},{5,6... | collective-permute-start | bytes 2359304 | tf_op jit(solution)/shard_map/ppermute | solution.py:470
  114.5 1.9 %collective-permute-start.16 = (bf16[256,3072]{1,0:T(8,128)(2,1)S(1)}, bf16[256,3072]{1,0:T(8,128)(2,1)S(1)}, u32[]{:S(2)}, u32[]{:S(2)}) collective-permute-start(bf16[256,3072]{1,0:T(8,128)(2,1)S(1)} %collective-permute-done.13.x_ref.rest_1_.rest_6_.rest_11_), channel_id=1, source_target_pairs={{0,16},{16,0},{1,17},{17,1},{2,18},{18,2},{3,19},{19,3},{4,20},{20... | collective-permute-start | bytes 4718600 | tf_op jit(solution)/shard_map/ppermute | solution.py:472
  116.4 0.6 spread.1
  117.0 15.3 %all_to_all.5.slots_ref = bf16[4,96,1024]{2,1,0:T(8,128)(2,1)S(1)} all-to-all(bf16[4,96,1024]{2,1,0:T(8,128)(2,1)S(1)} %spread.1), channel_id=1, replica_groups=mesh['zl'=2,'y'=8,'c'=2,'zh'=4,'x'=4] {'x'}, dimensions={0} | all-to-all | bytes 1572864 | tf_op jit(solution)/shard_map/all_to_all | solution.py:471
  132.4 4.0 %collective-permute-start.17 = (bf16[128,3072]{1,0:T(8,128)(2,1)S(1)}, bf16[128,3072]{1,0:T(8,128)(2,1)S(1)}, u32[]{:S(2)}, u32[]{:S(2)}) collective-permute-start(bf16[128,3072]{1,0:T(8,128)(2,1)S(1)} %collective-permute-done.15.rest_3_.rest_8_.rest_13_), channel_id=1, source_target_pairs={{0,16},{16,0},{1,17},{17,1},{2,18},{18,2},{3,19},{19,3},{4,20},{20... | collective-permute-start | bytes 2359304 | tf_op jit(solution)/shard_map/ppermute | solution.py:474
  136.4 1.9 %collective-permute-done.17.rest_4_.rest_9_.rest_14_ = bf16[128,3072]{1,0:T(8,128)(2,1)S(1)} collective-permute-done((bf16[128,3072]{1,0:T(8,128)(2,1)S(1)}, bf16[128,3072]{1,0:T(8,128)(2,1)S(1)}, u32[]{:S(2)}, u32[]{:S(2)}) %collective-permute-start.17) | collective-permute-done | bytes 786464 | tf_op jit(solution)/shard_map/ppermute | solution.py:474
  138.3 8.6 %global.1 = bf16[96,1024]{1,0:T(8,128)(2,1)} custom-call(s32[5]{0:T(128)S(1)} %stack.19.place_ref.at_ref, bf16[96,1024]{1,0:T(8,128)(2,1)S(1)} %get-tuple-element.16.own_ref, bf16[4,96,1024]{2,1,0:T(8,128)(2,1)S(1)} %all_to_all.5.slots_ref, bf16[256,3072]{1,0:T(8,128)(2,1)S(1)} %place.3.rest_0_.rest_5_.rest_10_, ...), custom_call_target="tpu_custom_call" | custom-call | tf_op jit(solution)/shard_map/global/pallas_call | solution.py:327
  (27 shorter events, 0.1 us)
Async XLA Ops:
  0.6 0.9 copy-start
  1.6 0.9 copy-start.2
  3.5 34.0 %collective-permute-start.1 = (bf16[2,80,1024]{2,1,0:T(8,128)(2,1)S(1)}, bf16[2,80,1024]{2,1,0:T(8,128)(2,1)S(1)}, u32[]{:S(2)}, u32[]{:S(2)}) collective-permute-start(bf16[2,80,1024]{2,1,0:T(8,128)(2,1)S(1)} %get-tuple-element.12), channel_id=1, source_target_pairs={{1,0},{2,1},{3,2},{4,3},{5,4},{6,5},{7,6},{8,7},{9,8},{10,9},{11,1... | collective-permute-start | bytes 983048 | tf_op jit(solution)/shard_map/ppermute | solution.py:454
  4.8 32.7 %collective-permute-start = (bf16[2,80,1024]{2,1,0:T(8,128)(2,1)S(1)}, bf16[2,80,1024]{2,1,0:T(8,128)(2,1)S(1)}, u32[]{:S(2)}, u32[]{:S(2)}) collective-permute-start(bf16[2,80,1024]{2,1,0:T(8,128)(2,1)S(1)} %get-tuple-element.11.after_ref), channel_id=1, source_target_pairs={{0,1},{1,2},{2,3},{3,4},{4,5},{5,6},{6,7},{7,8},{8,9},{9,10},{10,1... | collective-permute-start | bytes 983048 | tf_op jit(solution)/shard_map/ppermute | solution.py:453
  9.4 19.2 %collective-permute-start.4 = (bf16[64,1024]{1,0:T(8,128)(2,1)}, bf16[64,1024]{1,0:T(8,128)(2,1)S(1)}, u32[]{:S(2)}, u32[]{:S(2)}) collective-permute-start(bf16[64,1024]{1,0:T(8,128)(2,1)} %p0.1), channel_id=1, source_target_pairs={{0,4},{4,8},{8,12},{12,0},{16,28},{20,16},{24,20},{28,24},{1,5},{5... | collective-permute-start | bytes 393224 | tf_op jit(solution)/shard_map/ppermute | solution.py:411
  26.3 11.2 %copy-start.1 = (bf16[12,8,1024]{2,1,0:T(8,128)(2,1)S(1)}, bf16[12,8,1024]{2,1,0:T(8,128)(2,1)}, u32[]{:S(2)}) copy-start(bf16[12,8,1024]{2,1,0:T(8,128)(2,1)} %param.10) | copy-start | bytes 589828
  26.3 11.2 %copy-start.3 = (bf16[12,8,1024]{2,1,0:T(8,128)(2,1)S(1)}, bf16[12,8,1024]{2,1,0:T(8,128)(2,1)}, u32[]{:S(2)}) copy-start(bf16[12,8,1024]{2,1,0:T(8,128)(2,1)} %param.11) | copy-start | bytes 589828
  29.2 9.6 %copy-start.4 = (bf16[64,3072]{1,0:T(8,128)(2,1)S(1)}, bf16[64,3072]{1,0:T(8,128)(2,1)}, u32[]{:S(2)}) copy-start(bf16[64,3072]{1,0:T(8,128)(2,1)} %p0.2) | copy-start | bytes 1179652
  29.2 23.0 %copy-start.7 = (bf16[64,1024]{1,0:T(8,128)(2,1)S(1)}, bf16[64,1024]{1,0:T(8,128)(2,1)}, u32[]{:S(2)}) copy-start(bf16[64,1024]{1,0:T(8,128)(2,1)} %p0.1) | copy-start | bytes 393220
  29.2 9.6 %collective-permute-start.5 = (bf16[32,1024]{1,0:T(8,128)(2,1)S(1)}, bf16[32,1024]{1,0:T(8,128)(2,1)S(1)}, u32[]{:S(2)}, u32[]{:S(2)}) collective-permute-start(bf16[32,1024]{1,0:T(8,128)(2,1)S(1)} %half.4), channel_id=1, source_target_pairs={{0,4},{4,8},{8,12},{12,0},{16,28},{20,16},{24,20},{28,24},{1,5},{5... | collective-permute-start | bytes 196616 | tf_op jit(solution)/shard_map/ppermute | solution.py:412
  38.8 20.4 %collective-permute-start.10 = (bf16[64,3072]{1,0:T(8,128)(2,1)S(1)}, bf16[64,3072]{1,0:T(8,128)(2,1)S(1)}, u32[]{:S(2)}, u32[]{:S(2)}) collective-permute-start(bf16[64,3072]{1,0:T(8,128)(2,1)S(1)} %copy-done.4), channel_id=1, source_target_pairs={{0,4},{4,8},{8,12},{12,0},{16,28},{20,16},{24,20},{28,24},{1,5},{5... | collective-permute-start | bytes 1179656 | tf_op jit(solution)/shard_map/ppermute | solution.py:411
  44.7 7.5 %collective-permute-start.6 = (bf16[96,1024]{1,0:T(8,128)(2,1)S(1)}, bf16[96,1024]{1,0:T(8,128)(2,1)S(1)}, u32[]{:S(2)}, u32[]{:S(2)}) collective-permute-start(bf16[96,1024]{1,0:T(8,128)(2,1)S(1)} %pack.3), channel_id=1, source_target_pairs={{0,16},{16,0},{1,17},{17,1},{2,18},{18,2},{3,19},{19,3},{4,20},{20... | collective-permute-start | bytes 589832 | tf_op jit(solution)/shard_map/ppermute | solution.py:413
  46.7 25.0 %collective-permute-start.2 = (bf16[2,128,1024]{2,1,0:T(8,128)(2,1)S(1)}, bf16[2,128,1024]{2,1,0:T(8,128)(2,1)S(1)}, u32[]{:S(2)}, u32[]{:S(2)}) collective-permute-start(bf16[2,128,1024]{2,1,0:T(8,128)(2,1)S(1)} %get-tuple-element.13.rest_0_), channel_id=1, source_target_pairs={{0,16},{16,32},{32,48},{48,64},{64,80},{80,96},{96,112},{112,128},... | collective-permute-start | bytes 1572872 | tf_op jit(solution)/shard_map/ppermute | solution.py:458
  50.3 21.4 %collective-permute-start.3 = (bf16[2,128,1024]{2,1,0:T(8,128)(2,1)S(1)}, bf16[2,128,1024]{2,1,0:T(8,128)(2,1)S(1)}, u32[]{:S(2)}, u32[]{:S(2)}) collective-permute-start(bf16[2,128,1024]{2,1,0:T(8,128)(2,1)S(1)} %get-tuple-element.14.rest_1_), channel_id=1, source_target_pairs={{0,496},{16,0},{32,16},{48,32},{64,48},{80,64},{96,80},{112,96},{1... | collective-permute-start | bytes 1572872 | tf_op jit(solution)/shard_map/ppermute | solution.py:459
  52.8 18.8 %collective-permute-start.7 = (bf16[256,1024]{1,0:T(8,128)(2,1)S(1)}, bf16[256,1024]{1,0:T(8,128)(2,1)S(1)}, u32[]{:S(2)}, u32[]{:S(2)}) collective-permute-start(bf16[256,1024]{1,0:T(8,128)(2,1)S(1)} %place.2.p0.rest_0_), channel_id=1, source_target_pairs={{0,1},{1,2},{2,3},{3,0},{16,19},{17,16},{18,17},{19,18},{4,5},{5,6... | collective-permute-start | bytes 1572872 | tf_op jit(solution)/shard_map/ppermute | solution.py:411
  59.8 21.6 %copy-start.5 = (bf16[12,8,1024]{2,1,0:T(8,128)(2,1)S(1)}, bf16[12,8,1024]{2,1,0:T(8,128)(2,1)}, u32[]{:S(2)}) copy-start(bf16[12,8,1024]{2,1,0:T(8,128)(2,1)} %param.9) | copy-start | bytes 589828
  59.8 9.4 %collective-permute-start.11 = (bf16[32,3072]{1,0:T(8,128)(2,1)S(1)}, bf16[32,3072]{1,0:T(8,128)(2,1)S(1)}, u32[]{:S(2)}, u32[]{:S(2)}) collective-permute-start(bf16[32,3072]{1,0:T(8,128)(2,1)S(1)} %half.6), channel_id=1, source_target_pairs={{0,4},{4,8},{8,12},{12,0},{16,28},{20,16},{24,20},{28,24},{1,5},{5... | collective-permute-start | bytes 589832 | tf_op jit(solution)/shard_map/ppermute | solution.py:412
  69.2 15.5 %collective-permute-start.12 = (bf16[96,3072]{1,0:T(8,128)(2,1)S(1)}, bf16[96,3072]{1,0:T(8,128)(2,1)S(1)}, u32[]{:S(2)}, u32[]{:S(2)}) collective-permute-start(bf16[96,3072]{1,0:T(8,128)(2,1)S(1)} %pack.5), channel_id=1, source_target_pairs={{0,16},{16,0},{1,17},{17,1},{2,18},{18,2},{3,19},{19,3},{4,20},{20... | collective-permute-start | bytes 1769480 | tf_op jit(solution)/shard_map/ppermute | solution.py:413
  72.2 12.5 %collective-permute-start.8 = (bf16[128,1024]{1,0:T(8,128)(2,1)S(1)}, bf16[128,1024]{1,0:T(8,128)(2,1)S(1)}, u32[]{:S(2)}, u32[]{:S(2)}) collective-permute-start(bf16[128,1024]{1,0:T(8,128)(2,1)S(1)} %half.5), channel_id=1, source_target_pairs={{0,1},{1,2},{2,3},{3,0},{16,19},{17,16},{18,17},{19,18},{4,5},{5,6... | collective-permute-start | bytes 786440 | tf_op jit(solution)/shard_map/ppermute | solution.py:412
  85.3 9.4 %copy-start.6 = (bf16[12,8,1024]{2,1,0:T(8,128)(2,1)S(1)}, bf16[12,8,1024]{2,1,0:T(8,128)(2,1)}, u32[]{:S(2)}) copy-start(bf16[12,8,1024]{2,1,0:T(8,128)(2,1)} %param.8) | copy-start | bytes 589828
  85.4 9.4 %copy-start.8 = (f32[1024]{0:T(1024)S(1)}, f32[1024]{0:T(1024)}, u32[]{:S(2)}) copy-start(f32[1024]{0:T(1024)} %param.14) | copy-start | bytes 12292
  85.4 23.9 %collective-permute-start.13 = (bf16[256,3072]{1,0:T(8,128)(2,1)S(1)}, bf16[256,3072]{1,0:T(8,128)(2,1)S(1)}, u32[]{:S(2)}, u32[]{:S(2)}) collective-permute-start(bf16[256,3072]{1,0:T(8,128)(2,1)S(1)} %place.3.rest_0_.rest_5_.rest_10_), channel_id=1, source_target_pairs={{0,1},{1,2},{2,3},{3,0},{16,19},{17,16},{18,17},{19,18},{4,5},{5,6... | collective-permute-start | bytes 4718600 | tf_op jit(solution)/shard_map/ppermute | solution.py:468
  90.6 4.2 %collective-permute-start.9 = (bf16[384,1024]{1,0:T(8,128)(2,1)S(1)}, bf16[384,1024]{1,0:T(8,128)(2,1)S(1)}, u32[]{:S(2)}, u32[]{:S(2)}) collective-permute-start(bf16[384,1024]{1,0:T(8,128)(2,1)S(1)} %pack.4), channel_id=1, source_target_pairs={{0,16},{16,0},{1,17},{17,1},{2,18},{18,2},{3,19},{19,3},{4,20},{20... | collective-permute-start | bytes 2359304 | tf_op jit(solution)/shard_map/ppermute | solution.py:413
  96.7 12.6 %collective-permute-start.14 = (bf16[96,1024]{1,0:T(8,128)(2,1)S(1)}, bf16[96,1024]{1,0:T(8,128)(2,1)S(1)}, u32[]{:S(2)}, u32[]{:S(2)}) collective-permute-start(bf16[96,1024]{1,0:T(8,128)(2,1)S(1)} %get-tuple-element.16.own_ref), channel_id=1, source_target_pairs={{0,4},{4,8},{8,12},{12,16},{16,20},{20,24},{24,28},{28,32},{32,36}... | collective-permute-start | bytes 589832 | tf_op jit(solution)/shard_map/ppermute | solution.py:467
  109.9 22.5 %collective-permute-start.15 = (bf16[128,3072]{1,0:T(8,128)(2,1)S(1)}, bf16[128,3072]{1,0:T(8,128)(2,1)S(1)}, u32[]{:S(2)}, u32[]{:S(2)}) collective-permute-start(bf16[128,3072]{1,0:T(8,128)(2,1)S(1)} %half.7.after_ref), channel_id=1, source_target_pairs={{0,1},{1,2},{2,3},{3,0},{16,19},{17,16},{18,17},{19,18},{4,5},{5,6... | collective-permute-start | bytes 2359304 | tf_op jit(solution)/shard_map/ppermute | solution.py:470
  114.5 23.8 %collective-permute-start.16 = (bf16[256,3072]{1,0:T(8,128)(2,1)S(1)}, bf16[256,3072]{1,0:T(8,128)(2,1)S(1)}, u32[]{:S(2)}, u32[]{:S(2)}) collective-permute-start(bf16[256,3072]{1,0:T(8,128)(2,1)S(1)} %collective-permute-done.13.x_ref.rest_1_.rest_6_.rest_11_), channel_id=1, source_target_pairs={{0,16},{16,0},{1,17},{17,1},{2,18},{18,2},{3,19},{19,3},{4,20},{20... | collective-permute-start | bytes 4718600 | tf_op jit(solution)/shard_map/ppermute | solution.py:472
  132.4 5.9 %collective-permute-start.17 = (bf16[128,3072]{1,0:T(8,128)(2,1)S(1)}, bf16[128,3072]{1,0:T(8,128)(2,1)S(1)}, u32[]{:S(2)}, u32[]{:S(2)}) collective-permute-start(bf16[128,3072]{1,0:T(8,128)(2,1)S(1)} %collective-permute-done.15.rest_3_.rest_8_.rest_13_), channel_id=1, source_target_pairs={{0,16},{16,0},{1,17},{17,1},{2,18},{18,2},{3,19},{19,3},{4,20},{20... | collective-permute-start | bytes 2359304 | tf_op jit(solution)/shard_map/ppermute | solution.py:474

commit v5 on v4

--- a/solution.py
+++ b/solution.py
@@ -287,15 +287,14 @@
     )(at, x, tok, gain, *pieces)
 
 
-def global_kernel(at_ref, own_ref, slots_ref, *rest):
+def global_kernel(at_ref, own_ref, x1, x2, x3, x4, *rest):
     weights, (out_ref, xbuf) = rest[:15], rest[15:]
     width = own_ref.shape[1]
 
     @pl.when(pl.program_id(0) == 0)
     def _():
-        xbuf[0:CELLS] = own_ref[...]
-        for at in range(4):
-            xbuf[CELLS * at + CELLS : CELLS * at + 2 * CELLS] = slots_ref[at]
+        for at, ref in enumerate((own_ref, x1, x2, x3, x4)):
+            xbuf[CELLS * at : CELLS * at + CELLS] = ref[...]
 
     spans = piece_lanes(at_ref, width // 4)
 
@@ -314,13 +313,10 @@
         out_ref[:, lanes] = pair_attention(q[:, lanes], k[:, lanes], v[:, lanes], None)
 
 
-def global_layer(at, own, slots, pieces):
-    cells, width = own.shape
+def global_layer(at, blocks, pieces):
+    cells, width = blocks[0].shape
     steps = width // 256
-    whole = [
-        pl.BlockSpec((cells, width), lambda g, c: (0, 0)),
-        pl.BlockSpec(slots.shape, lambda g, c: (0, 0, 0)),
-    ]
+    whole = [pl.BlockSpec((cells, width), lambda g, c: (0, 0))] * len(blocks)
     weights = [
         pl.BlockSpec((piece.shape[0], 256), lambda g, c, t=t: (0, steps * t + g)) for t in range(3) for piece in pieces
     ]
@@ -336,7 +332,7 @@
         ),
         compiler_params=params(20),
         name="global",
-    )(at, own, slots, *(pieces * 3))
+    )(at, *blocks, *(pieces * 3))
 
 
 def place_kernel(at_ref, p0, p1, p2, p3, *rest):
@@ -418,19 +414,19 @@
     return [own, near, others.at[0:rows], far, others.at[rows : rows + rows // 2]]
 
 
-def spread_kernel(at_ref, own_ref, behind_ref, after_ref, out_ref):
-    for slot in range(4):
-        out_ref[slot] = jnp.where(slot > at_ref[1], own_ref[...], behind_ref[...])
-
-
-def spread(at, own, behind, after):
-    return pl.pallas_call(
-        spread_kernel,
-        out_shape=jax.ShapeDtypeStruct((4,) + own.shape, own.dtype),
+def choose_kernel(at_ref, own_ref, behind_ref, after_ref, *outs):
+    for by, ref in enumerate(outs, 1):
+        ref[...] = jnp.where(at_ref[1] + by < 4, own_ref[...], behind_ref[...])
+
+
+def choose(at, own, behind, after):
+    return pl.pallas_call(
+        choose_kernel,
+        out_shape=[jax.ShapeDtypeStruct(own.shape, own.dtype)] * 3,
         in_specs=[sspec(), vspec(), vspec(), anyspec()],
-        out_specs=vspec(),
+        out_specs=[vspec()] * 3,
         compiler_params=params(8),
-        name="spread",
+        name="choose",
     )(at, own, behind, after)
 
 
@@ -468,11 +464,13 @@
     near = lax.ppermute(rows_g, ("c", "x"), ROLES)
     half = half_of(at, near, [behind])
     far = lax.ppermute(half, ("c", "x"), ROLES)
-    slots = lax.all_to_all(spread(at, normed, behind, half), "x", 0, 0)
+    blocks = [normed, behind]
+    for by, sent in enumerate(choose(at, normed, behind, half), 1):
+        blocks.append(lax.ppermute(sent, "x", ring(xs, by)))
     near_other = lax.ppermute(near, "c", SWAP)
-    late, slots = lax.optimization_barrier((far, slots))
+    late, *blocks = lax.optimization_barrier((far, *blocks))
     far_other = lax.ppermute(late, "c", SWAP)
-    attended = global_layer(at, normed, slots, [rows_g, near, near_other, late, far_other])
+    attended = global_layer(at, blocks, [rows_g, near, near_other, late, far_other])
     return hidden.reshape(tokens.shape), attended.reshape(tokens.shape)
 
 

time: 148 us -> 148 us (level)
  blocking collectives: 15.3 us -> 0 us
  starting transfers between devices: 82.9 us -> 91 us
  waiting for transfers between devices: 21.6 us -> 28.8 us
    all_to_all x1 -> x0, blocking collectives: 15.3 us -> none  [body(): slots = lax.all_to_all(spread(at, normed, behind, half), 'x', 0, 0)]
    ppermute x0 -> x3, starting transfers between devices: none -> 8.41 us  [body(): blocks.append(lax.ppermute(sent, 'x', ring(xs, by)))]
    ppermute x0 -> x3, waiting for transfers between devices: none -> 7.18 us  [body(): blocks.append(lax.ppermute(sent, 'x', ring(xs, by)))]
  transfers between devices with their start and end apart: 18 -> 21, of which waited for: 7 -> 10; matrix products, arithmetic and copies ran while one was open for 1% -> 1% of each run, Pallas kernels for 8% -> 8%
where the time goes in v5:
time: 148 us; the launch traced here: 147 us
  starting transfers between devices  91 us (61%)
  waiting for transfers between devices  28.8 us (19%)
  Pallas kernels  23 us (16%)
  local copies, waits for them, and re-layouts  3.03 us (2%)
    ppermute x3, starting transfers between devices, gathered(): near = lax.ppermute(rows, ('c', axis), ROLES)  24.1 us
    ppermute x3, starting transfers between devices, gathered(): far = lax.ppermute(half_of(at, near, after), ('c', axis), ROLES)  23.3 us
    ppermute x1, waiting for transfers between devices, body(): behind = lax.ppermute(normed, LON + ('zh',), ring(lon_count * zs, 1))  10.5 us
    pallas_call x1, Pallas kernels, global_layer(): pl.pallas_call(global_kernel, out_shape=jax.ShapeDtypeStruct((cells, widt...  8.56 us
    ppermute x3, starting transfers between devices, body(): blocks.append(lax.ppermute(sent, 'x', ring(xs, by)))  8.41 us
    ppermute x3, waiting for transfers between devices, body(): blocks.append(lax.ppermute(sent, 'x', ring(xs, by)))  7.18 us
    ppermute x3, starting transfers between devices, gathered(): return [rows, near, far, lax.ppermute(pack(near, far), 'c', SWAP)]  6.26 us
    ppermute x1, starting transfers between devices, body(): near = lax.ppermute(rows_g, ('c', 'x'), ROLES)  5.16 us
  transfers between devices with their start and end apart: 21, of which 10 were waited for; matrix products, arithmetic and copies ran while one was open for 1% of the time, Pallas kernels for 8%

profile of v5, /device:TPU:1, one launch (start us, length us, event | category | flops | bytes accessed | tf_op | source)
XLA Modules:
  0.0 146.9 jit_solution(12266773639134243764)
XLA Ops:
  0.6 0.9 copy-done
  1.6 0.9 copy-done.2
  2.5 1.0 edges.1
  3.5 1.3 collective-permute-start.1
  4.8 4.6 %collective-permute-start = (bf16[2,80,1024]{2,1,0:T(8,128)(2,1)S(1)}, bf16[2,80,1024]{2,1,0:T(8,128)(2,1)S(1)}, u32[]{:S(2)}, u32[]{:S(2)}) collective-permute-start(bf16[2,80,1024]{2,1,0:T(8,128)(2,1)S(1)} %get-tuple-element.18.after_ref), channel_id=1, source_target_pairs={{0,1},{1,2},{2,3},{3,4},{4,5},{5,6},{6,7},{7,8},{8,9},{9,10},{10,1... | collective-permute-start | bytes 983048 | tf_op jit(solution)/shard_map/ppermute | solution.py:449
  9.4 11.9 %collective-permute-start.4 = (bf16[64,1024]{1,0:T(8,128)(2,1)}, bf16[64,1024]{1,0:T(8,128)(2,1)S(1)}, u32[]{:S(2)}, u32[]{:S(2)}) collective-permute-start(bf16[64,1024]{1,0:T(8,128)(2,1)} %p0.1), channel_id=1, source_target_pairs={{0,4},{4,8},{8,12},{12,0},{16,28},{20,16},{24,20},{28,24},{1,5},{5... | collective-permute-start | bytes 393224 | tf_op jit(solution)/shard_map/ppermute | solution.py:407
  21.3 0.9 copy.11
  22.2 0.1 reshape.31
  22.4 3.8 %bias.1.after_ref.bias_ref.rest_0_ = f32[16,96,512]{2,1,0:T(8,128)S(1)} custom-call(s32[5]{0:T(128)S(1)} %stack.19.place_ref.at_ref, f32[16,256]{1,0:T(8,128)S(1)} %pad.4.table_ref, bf16[2,80,1024]{2,1,0:T(8,128)(2,1)S(1)} %get-tuple-element.18.after_ref), custom_call_target="tpu_custom_call" | custom-call | tf_op jit(solution)/shard_map/bias/pallas_call | solution.py:183
  26.3 2.3 %collective-permute-done.4.x_ref.a_ref.p1 = bf16[64,1024]{1,0:T(8,128)(2,1)S(1)} collective-permute-done((bf16[64,1024]{1,0:T(8,128)(2,1)}, bf16[64,1024]{1,0:T(8,128)(2,1)S(1)}, u32[]{:S(2)}, u32[]{:S(2)}) %collective-permute-start.4) | collective-permute-done | bytes 131104 | tf_op jit(solution)/shard_map/ppermute | solution.py:407
  28.6 0.6 half.4
  29.2 8.3 %collective-permute-start.5 = (bf16[32,1024]{1,0:T(8,128)(2,1)S(1)}, bf16[32,1024]{1,0:T(8,128)(2,1)S(1)}, u32[]{:S(2)}, u32[]{:S(2)}) collective-permute-start(bf16[32,1024]{1,0:T(8,128)(2,1)S(1)} %half.4), channel_id=1, source_target_pairs={{0,4},{4,8},{8,12},{12,0},{16,28},{20,16},{24,20},{28,24},{1,5},{5... | collective-permute-start | bytes 196616 | tf_op jit(solution)/shard_map/ppermute | solution.py:408
  37.5 0.4 sides.1
  38.0 0.8 collective-permute-done.5.b_ref.p2
  38.8 5.9 %collective-permute-start.10 = (bf16[64,3072]{1,0:T(8,128)(2,1)S(1)}, bf16[64,3072]{1,0:T(8,128)(2,1)S(1)}, u32[]{:S(2)}, u32[]{:S(2)}) collective-permute-start(bf16[64,3072]{1,0:T(8,128)(2,1)S(1)} %copy-done.4), channel_id=1, source_target_pairs={{0,4},{4,8},{8,12},{12,0},{16,28},{20,16},{24,20},{28,24},{1,5},{5... | collective-permute-start | bytes 1179656 | tf_op jit(solution)/shard_map/ppermute | solution.py:407
  44.7 1.9 %collective-permute-start.6 = (bf16[96,1024]{1,0:T(8,128)(2,1)S(1)}, bf16[96,1024]{1,0:T(8,128)(2,1)S(1)}, u32[]{:S(2)}, u32[]{:S(2)}) collective-permute-start(bf16[96,1024]{1,0:T(8,128)(2,1)S(1)} %pack.3), channel_id=1, source_target_pairs={{0,16},{16,0},{1,17},{17,1},{2,18},{18,2},{3,19},{19,3},{4,20},{20... | collective-permute-start | bytes 589832 | tf_op jit(solution)/shard_map/ppermute | solution.py:409
  46.7 3.6 %collective-permute-start.2 = (bf16[2,128,1024]{2,1,0:T(8,128)(2,1)S(1)}, bf16[2,128,1024]{2,1,0:T(8,128)(2,1)S(1)}, u32[]{:S(2)}, u32[]{:S(2)}) collective-permute-start(bf16[2,128,1024]{2,1,0:T(8,128)(2,1)S(1)} %get-tuple-element.20.rest_0_), channel_id=1, source_target_pairs={{0,16},{16,32},{32,48},{48,64},{64,80},{80,96},{96,112},{112,128},... | collective-permute-start | bytes 1572872 | tf_op jit(solution)/shard_map/ppermute | solution.py:454
  50.3 1.9 %collective-permute-start.3 = (bf16[2,128,1024]{2,1,0:T(8,128)(2,1)S(1)}, bf16[2,128,1024]{2,1,0:T(8,128)(2,1)S(1)}, u32[]{:S(2)}, u32[]{:S(2)}) collective-permute-start(bf16[2,128,1024]{2,1,0:T(8,128)(2,1)S(1)} %get-tuple-element.21.rest_1_), channel_id=1, source_target_pairs={{0,496},{16,0},{32,16},{48,32},{64,48},{80,64},{96,80},{112,96},{1... | collective-permute-start | bytes 1572872 | tf_op jit(solution)/shard_map/ppermute | solution.py:455
  52.2 0.6 place.2.p0.rest_0_
  52.8 6.4 %collective-permute-start.7 = (bf16[256,1024]{1,0:T(8,128)(2,1)S(1)}, bf16[256,1024]{1,0:T(8,128)(2,1)S(1)}, u32[]{:S(2)}, u32[]{:S(2)}) collective-permute-start(bf16[256,1024]{1,0:T(8,128)(2,1)S(1)} %place.2.p0.rest_0_), channel_id=1, source_target_pairs={{0,1},{1,2},{2,3},{3,0},{16,19},{17,16},{18,17},{19,18},{4,5},{5,6... | collective-permute-start | bytes 1572872 | tf_op jit(solution)/shard_map/ppermute | solution.py:407
  59.2 0.6 half.6
  59.8 5.9 %collective-permute-start.11 = (bf16[32,3072]{1,0:T(8,128)(2,1)S(1)}, bf16[32,3072]{1,0:T(8,128)(2,1)S(1)}, u32[]{:S(2)}, u32[]{:S(2)}) collective-permute-start(bf16[32,3072]{1,0:T(8,128)(2,1)S(1)} %half.6), channel_id=1, source_target_pairs={{0,4},{4,8},{8,12},{12,0},{16,28},{20,16},{24,20},{28,24},{1,5},{5... | collective-permute-start | bytes 589832 | tf_op jit(solution)/shard_map/ppermute | solution.py:408
  65.7 3.5 %collective-permute-done.11.b_ref.p2 = bf16[32,3072]{1,0:T(8,128)(2,1)S(1)} collective-permute-done((bf16[32,3072]{1,0:T(8,128)(2,1)S(1)}, bf16[32,3072]{1,0:T(8,128)(2,1)S(1)}, u32[]{:S(2)}, u32[]{:S(2)}) %collective-permute-start.11) | collective-permute-done | bytes 196640 | tf_op jit(solution)/shard_map/ppermute | solution.py:408
  69.2 2.4 %collective-permute-start.12 = (bf16[96,3072]{1,0:T(8,128)(2,1)S(1)}, bf16[96,3072]{1,0:T(8,128)(2,1)S(1)}, u32[]{:S(2)}, u32[]{:S(2)}) collective-permute-start(bf16[96,3072]{1,0:T(8,128)(2,1)S(1)} %pack.5), channel_id=1, source_target_pairs={{0,16},{16,0},{1,17},{17,1},{2,18},{18,2},{3,19},{19,3},{4,20},{20... | collective-permute-start | bytes 1769480 | tf_op jit(solution)/shard_map/ppermute | solution.py:409
  71.6 0.6 half.5
  72.2 9.1 %collective-permute-start.8 = (bf16[128,1024]{1,0:T(8,128)(2,1)S(1)}, bf16[128,1024]{1,0:T(8,128)(2,1)S(1)}, u32[]{:S(2)}, u32[]{:S(2)}) collective-permute-start(bf16[128,1024]{1,0:T(8,128)(2,1)S(1)} %half.5), channel_id=1, source_target_pairs={{0,1},{1,2},{2,3},{3,0},{16,19},{17,16},{18,17},{19,18},{4,5},{5,6... | collective-permute-start | bytes 786440 | tf_op jit(solution)/shard_map/ppermute | solution.py:408
  81.4 3.0 %local.1.x_ref.rest_1_ = bf16[96,1024]{1,0:T(8,128)(2,1)S(1)} custom-call(bf16[96,1024]{1,0:T(8,128)(2,1)S(1)} %bitcast.17, bf16[96,1024]{1,0:T(8,128)(2,1)S(1)} %bitcast.13, bf16[96,1024]{1,0:T(8,128)(2,1)S(1)} %bitcast.16, bf16[2,80,1024]{2,1,0:T(8,128)(2,1)S(1)} %collective-permute-done.low_ref, bf16[2,80,1024]{2,1,0:T(8,128)(2,1)S(1)} %collective-permute-done.1.high_ref, ...), custom_call_target="tpu_custom_call" | custom-call | tf_op jit(solution)/shard_map/local/pallas_call | solution.py:234
  84.4 0.3 collective-permute-done.8.b_ref.p2.rest_0_
  84.7 0.7 place.3.rest_0_.rest_5_.rest_10_
  85.4 5.2 %collective-permute-start.13 = (bf16[256,3072]{1,0:T(8,128)(2,1)S(1)}, bf16[256,3072]{1,0:T(8,128)(2,1)S(1)}, u32[]{:S(2)}, u32[]{:S(2)}) collective-permute-start(bf16[256,3072]{1,0:T(8,128)(2,1)S(1)} %place.3.rest_0_.rest_5_.rest_10_), channel_id=1, source_target_pairs={{0,1},{1,2},{2,3},{3,0},{16,19},{17,16},{18,17},{19,18},{4,5},{5,6... | collective-permute-start | bytes 4718600 | tf_op jit(solution)/shard_map/ppermute | solution.py:464
  90.6 1.9 %collective-permute-start.9 = (bf16[384,1024]{1,0:T(8,128)(2,1)S(1)}, bf16[384,1024]{1,0:T(8,128)(2,1)S(1)}, u32[]{:S(2)}, u32[]{:S(2)}) collective-permute-start(bf16[384,1024]{1,0:T(8,128)(2,1)S(1)} %pack.4), channel_id=1, source_target_pairs={{0,16},{16,0},{1,17},{17,1},{2,18},{18,2},{3,19},{19,3},{4,20},{20... | collective-permute-start | bytes 2359304 | tf_op jit(solution)/shard_map/ppermute | solution.py:409
  92.5 2.3 %collective-permute-done.9.p3 = bf16[384,1024]{1,0:T(8,128)(2,1)S(1)} collective-permute-done((bf16[384,1024]{1,0:T(8,128)(2,1)S(1)}, bf16[384,1024]{1,0:T(8,128)(2,1)S(1)}, u32[]{:S(2)}, u32[]{:S(2)}) %collective-permute-start.9) | collective-permute-done | bytes 786464 | tf_op jit(solution)/shard_map/ppermute | solution.py:409
  94.8 1.9 %project.1 = (bf16[96,1024]{1,0:T(8,128)(2,1)}, bf16[96,1024]{1,0:T(8,128)(2,1)S(1)}) custom-call(s32[5]{0:T(128)S(1)} %stack.19.place_ref.at_ref, bf16[96,1024]{1,0:T(8,128)(2,1)S(1)} %local.1.x_ref.rest_1_, bf16[96,1024]{1,0:T(8,128)(2,1)S(1)} %bitcast.18, f32[1,1024]{1,0:T(1,128)S(1)} %bitcast.19, bf16[256,1024]{1,0:T(8,128)(2,1)S(1)} %place.2.p0.rest_0_, ...), custom_call_target="tpu_custom_call" | custom-call | tf_op jit(solution)/shard_map/project/pallas_call | solution.py:280
  96.7 2.1 %collective-permute-start.14 = (bf16[96,1024]{1,0:T(8,128)(2,1)S(1)}, bf16[96,1024]{1,0:T(8,128)(2,1)S(1)}, u32[]{:S(2)}, u32[]{:S(2)}) collective-permute-start(bf16[96,1024]{1,0:T(8,128)(2,1)S(1)} %get-tuple-element.28.own_ref), channel_id=1, source_target_pairs={{0,4},{4,8},{8,12},{12,16},{16,20},{20,24},{24,28},{28,32},{32,36}... | collective-permute-start | bytes 589832 | tf_op jit(solution)/shard_map/ppermute | solution.py:463
  98.7 10.5 %collective-permute-done.14.rest_0_.behind_ref.x1 = bf16[96,1024]{1,0:T(8,128)(2,1)S(1)} collective-permute-done((bf16[96,1024]{1,0:T(8,128)(2,1)S(1)}, bf16[96,1024]{1,0:T(8,128)(2,1)S(1)}, u32[]{:S(2)}, u32[]{:S(2)}) %collective-permute-start.14) | collective-permute-done | bytes 196640 | tf_op jit(solution)/shard_map/ppermute | solution.py:463
  109.3 0.6 half.7.after_ref
  109.9 4.6 %collective-permute-start.15 = (bf16[128,3072]{1,0:T(8,128)(2,1)S(1)}, bf16[128,3072]{1,0:T(8,128)(2,1)S(1)}, u32[]{:S(2)}, u32[]{:S(2)}) collective-permute-start(bf16[128,3072]{1,0:T(8,128)(2,1)S(1)} %half.7.after_ref), channel_id=1, source_target_pairs={{0,1},{1,2},{2,3},{3,0},{16,19},{17,16},{18,17},{19,18},{4,5},{5,6... | collective-permute-start | bytes 2359304 | tf_op jit(solution)/shard_map/ppermute | solution.py:466
  114.5 1.9 %collective-permute-start.19 = (bf16[256,3072]{1,0:T(8,128)(2,1)S(1)}, bf16[256,3072]{1,0:T(8,128)(2,1)S(1)}, u32[]{:S(2)}, u32[]{:S(2)}) collective-permute-start(bf16[256,3072]{1,0:T(8,128)(2,1)S(1)} %collective-permute-done.13.x_ref.rest_1_.rest_6_.rest_11_), channel_id=1, source_target_pairs={{0,16},{16,0},{1,17},{17,1},{2,18},{18,2},{3,19},{19,3},{4,20},{20... | collective-permute-start | bytes 4718600 | tf_op jit(solution)/shard_map/ppermute | solution.py:470
  116.4 0.6 choose.1
  117.0 1.9 %collective-permute-start.16 = (bf16[96,1024]{1,0:T(8,128)(2,1)S(1)}, bf16[96,1024]{1,0:T(8,128)(2,1)S(1)}, u32[]{:S(2)}, u32[]{:S(2)}) collective-permute-start(bf16[96,1024]{1,0:T(8,128)(2,1)S(1)} %get-tuple-element.25), channel_id=1, source_target_pairs={{0,1},{1,2},{2,3},{3,0},{4,5},{5,6},{6,7},{7,4},{8,9},{9,10},{10,1... | collective-permute-start | bytes 589832 | tf_op jit(solution)/shard_map/ppermute | solution.py:469
  119.0 4.4 %collective-permute-start.17 = (bf16[96,1024]{1,0:T(8,128)(2,1)S(1)}, bf16[96,1024]{1,0:T(8,128)(2,1)S(1)}, u32[]{:S(2)}, u32[]{:S(2)}) collective-permute-start(bf16[96,1024]{1,0:T(8,128)(2,1)S(1)} %get-tuple-element.26), channel_id=1, source_target_pairs={{0,2},{1,3},{2,0},{3,1},{4,6},{5,7},{6,4},{7,5},{8,10},{9,11},{10,... | collective-permute-start | bytes 589832 | tf_op jit(solution)/shard_map/ppermute | solution.py:469
  123.4 2.1 %collective-permute-start.18 = (bf16[96,1024]{1,0:T(8,128)(2,1)S(1)}, bf16[96,1024]{1,0:T(8,128)(2,1)S(1)}, u32[]{:S(2)}, u32[]{:S(2)}) collective-permute-start(bf16[96,1024]{1,0:T(8,128)(2,1)S(1)} %get-tuple-element.27), channel_id=1, source_target_pairs={{0,3},{1,0},{2,1},{3,2},{4,7},{5,4},{6,5},{7,6},{8,11},{9,8},{10,9... | collective-permute-start | bytes 589832 | tf_op jit(solution)/shard_map/ppermute | solution.py:469
  125.5 1.8 %collective-permute-done.16.x2 = bf16[96,1024]{1,0:T(8,128)(2,1)S(1)} collective-permute-done((bf16[96,1024]{1,0:T(8,128)(2,1)S(1)}, bf16[96,1024]{1,0:T(8,128)(2,1)S(1)}, u32[]{:S(2)}, u32[]{:S(2)}) %collective-permute-start.16) | collective-permute-done | bytes 196640 | tf_op jit(solution)/shard_map/ppermute | solution.py:469
  127.3 3.9 %collective-permute-done.17.x3 = bf16[96,1024]{1,0:T(8,128)(2,1)S(1)} collective-permute-done((bf16[96,1024]{1,0:T(8,128)(2,1)S(1)}, bf16[96,1024]{1,0:T(8,128)(2,1)S(1)}, u32[]{:S(2)}, u32[]{:S(2)}) %collective-permute-start.17) | collective-permute-done | bytes 196640 | tf_op jit(solution)/shard_map/ppermute | solution.py:469
  131.2 1.5 %collective-permute-done.18.x4 = bf16[96,1024]{1,0:T(8,128)(2,1)S(1)} collective-permute-done((bf16[96,1024]{1,0:T(8,128)(2,1)S(1)}, bf16[96,1024]{1,0:T(8,128)(2,1)S(1)}, u32[]{:S(2)}, u32[]{:S(2)}) %collective-permute-start.18) | collective-permute-done | bytes 196640 | tf_op jit(solution)/shard_map/ppermute | solution.py:469
  132.6 3.8 %collective-permute-start.20 = (bf16[128,3072]{1,0:T(8,128)(2,1)S(1)}, bf16[128,3072]{1,0:T(8,128)(2,1)S(1)}, u32[]{:S(2)}, u32[]{:S(2)}) collective-permute-start(bf16[128,3072]{1,0:T(8,128)(2,1)S(1)} %collective-permute-done.15.rest_3_.rest_8_.rest_13_), channel_id=1, source_target_pairs={{0,16},{16,0},{1,17},{17,1},{2,18},{18,2},{3,19},{19,3},{4,20},{20... | collective-permute-start | bytes 2359304 | tf_op jit(solution)/shard_map/ppermute | solution.py:472
  136.4 1.9 %collective-permute-done.20.rest_4_.rest_9_.rest_14_ = bf16[128,3072]{1,0:T(8,128)(2,1)S(1)} collective-permute-done((bf16[128,3072]{1,0:T(8,128)(2,1)S(1)}, bf16[128,3072]{1,0:T(8,128)(2,1)S(1)}, u32[]{:S(2)}, u32[]{:S(2)}) %collective-permute-start.20) | collective-permute-done | bytes 786464 | tf_op jit(solution)/shard_map/ppermute | solution.py:472
  138.3 8.6 %global.1 = bf16[96,1024]{1,0:T(8,128)(2,1)} custom-call(s32[5]{0:T(128)S(1)} %stack.19.place_ref.at_ref, bf16[96,1024]{1,0:T(8,128)(2,1)S(1)} %get-tuple-element.28.own_ref, bf16[96,1024]{1,0:T(8,128)(2,1)S(1)} %collective-permute-done.14.rest_0_.behind_ref.x1, bf16[96,1024]{1,0:T(8,128)(2,1)S(1)} %collective-permute-done.16.x2, ...), custom_call_target="tpu_custom_call" | custom-call | tf_op jit(solution)/shard_map/global/pallas_call | solution.py:323
  (32 shorter events, 0.3 us)
Async XLA Ops:
  0.6 0.9 copy-start
  1.6 0.9 copy-start.2
  3.5 34.0 %collective-permute-start.1 = (bf16[2,80,1024]{2,1,0:T(8,128)(2,1)S(1)}, bf16[2,80,1024]{2,1,0:T(8,128)(2,1)S(1)}, u32[]{:S(2)}, u32[]{:S(2)}) collective-permute-start(bf16[2,80,1024]{2,1,0:T(8,128)(2,1)S(1)} %get-tuple-element.19), channel_id=1, source_target_pairs={{1,0},{2,1},{3,2},{4,3},{5,4},{6,5},{7,6},{8,7},{9,8},{10,9},{11,1... | collective-permute-start | bytes 983048 | tf_op jit(solution)/shard_map/ppermute | solution.py:450
  4.8 32.7 %collective-permute-start = (bf16[2,80,1024]{2,1,0:T(8,128)(2,1)S(1)}, bf16[2,80,1024]{2,1,0:T(8,128)(2,1)S(1)}, u32[]{:S(2)}, u32[]{:S(2)}) collective-permute-start(bf16[2,80,1024]{2,1,0:T(8,128)(2,1)S(1)} %get-tuple-element.18.after_ref), channel_id=1, source_target_pairs={{0,1},{1,2},{2,3},{3,4},{4,5},{5,6},{6,7},{7,8},{8,9},{9,10},{10,1... | collective-permute-start | bytes 983048 | tf_op jit(solution)/shard_map/ppermute | solution.py:449
  9.4 19.2 %collective-permute-start.4 = (bf16[64,1024]{1,0:T(8,128)(2,1)}, bf16[64,1024]{1,0:T(8,128)(2,1)S(1)}, u32[]{:S(2)}, u32[]{:S(2)}) collective-permute-start(bf16[64,1024]{1,0:T(8,128)(2,1)} %p0.1), channel_id=1, source_target_pairs={{0,4},{4,8},{8,12},{12,0},{16,28},{20,16},{24,20},{28,24},{1,5},{5... | collective-permute-start | bytes 393224 | tf_op jit(solution)/shard_map/ppermute | solution.py:407
  26.3 11.2 %copy-start.1 = (bf16[12,8,1024]{2,1,0:T(8,128)(2,1)S(1)}, bf16[12,8,1024]{2,1,0:T(8,128)(2,1)}, u32[]{:S(2)}) copy-start(bf16[12,8,1024]{2,1,0:T(8,128)(2,1)} %param.10) | copy-start | bytes 589828
  26.3 11.2 %copy-start.3 = (bf16[12,8,1024]{2,1,0:T(8,128)(2,1)S(1)}, bf16[12,8,1024]{2,1,0:T(8,128)(2,1)}, u32[]{:S(2)}) copy-start(bf16[12,8,1024]{2,1,0:T(8,128)(2,1)} %param.11) | copy-start | bytes 589828
  29.2 9.6 %copy-start.4 = (bf16[64,3072]{1,0:T(8,128)(2,1)S(1)}, bf16[64,3072]{1,0:T(8,128)(2,1)}, u32[]{:S(2)}) copy-start(bf16[64,3072]{1,0:T(8,128)(2,1)} %p0.2) | copy-start | bytes 1179652
  29.2 23.0 %copy-start.7 = (bf16[64,1024]{1,0:T(8,128)(2,1)S(1)}, bf16[64,1024]{1,0:T(8,128)(2,1)}, u32[]{:S(2)}) copy-start(bf16[64,1024]{1,0:T(8,128)(2,1)} %p0.1) | copy-start | bytes 393220
  29.2 9.6 %collective-permute-start.5 = (bf16[32,1024]{1,0:T(8,128)(2,1)S(1)}, bf16[32,1024]{1,0:T(8,128)(2,1)S(1)}, u32[]{:S(2)}, u32[]{:S(2)}) collective-permute-start(bf16[32,1024]{1,0:T(8,128)(2,1)S(1)} %half.4), channel_id=1, source_target_pairs={{0,4},{4,8},{8,12},{12,0},{16,28},{20,16},{24,20},{28,24},{1,5},{5... | collective-permute-start | bytes 196616 | tf_op jit(solution)/shard_map/ppermute | solution.py:408
  38.8 20.4 %collective-permute-start.10 = (bf16[64,3072]{1,0:T(8,128)(2,1)S(1)}, bf16[64,3072]{1,0:T(8,128)(2,1)S(1)}, u32[]{:S(2)}, u32[]{:S(2)}) collective-permute-start(bf16[64,3072]{1,0:T(8,128)(2,1)S(1)} %copy-done.4), channel_id=1, source_target_pairs={{0,4},{4,8},{8,12},{12,0},{16,28},{20,16},{24,20},{28,24},{1,5},{5... | collective-permute-start | bytes 1179656 | tf_op jit(solution)/shard_map/ppermute | solution.py:407
  44.7 7.5 %collective-permute-start.6 = (bf16[96,1024]{1,0:T(8,128)(2,1)S(1)}, bf16[96,1024]{1,0:T(8,128)(2,1)S(1)}, u32[]{:S(2)}, u32[]{:S(2)}) collective-permute-start(bf16[96,1024]{1,0:T(8,128)(2,1)S(1)} %pack.3), channel_id=1, source_target_pairs={{0,16},{16,0},{1,17},{17,1},{2,18},{18,2},{3,19},{19,3},{4,20},{20... | collective-permute-start | bytes 589832 | tf_op jit(solution)/shard_map/ppermute | solution.py:409
  46.7 25.0 %collective-permute-start.2 = (bf16[2,128,1024]{2,1,0:T(8,128)(2,1)S(1)}, bf16[2,128,1024]{2,1,0:T(8,128)(2,1)S(1)}, u32[]{:S(2)}, u32[]{:S(2)}) collective-permute-start(bf16[2,128,1024]{2,1,0:T(8,128)(2,1)S(1)} %get-tuple-element.20.rest_0_), channel_id=1, source_target_pairs={{0,16},{16,32},{32,48},{48,64},{64,80},{80,96},{96,112},{112,128},... | collective-permute-start | bytes 1572872 | tf_op jit(solution)/shard_map/ppermute | solution.py:454
  50.3 21.4 %collective-permute-start.3 = (bf16[2,128,1024]{2,1,0:T(8,128)(2,1)S(1)}, bf16[2,128,1024]{2,1,0:T(8,128)(2,1)S(1)}, u32[]{:S(2)}, u32[]{:S(2)}) collective-permute-start(bf16[2,128,1024]{2,1,0:T(8,128)(2,1)S(1)} %get-tuple-element.21.rest_1_), channel_id=1, source_target_pairs={{0,496},{16,0},{32,16},{48,32},{64,48},{80,64},{96,80},{112,96},{1... | collective-permute-start | bytes 1572872 | tf_op jit(solution)/shard_map/ppermute | solution.py:455
  52.8 18.8 %collective-permute-start.7 = (bf16[256,1024]{1,0:T(8,128)(2,1)S(1)}, bf16[256,1024]{1,0:T(8,128)(2,1)S(1)}, u32[]{:S(2)}, u32[]{:S(2)}) collective-permute-start(bf16[256,1024]{1,0:T(8,128)(2,1)S(1)} %place.2.p0.rest_0_), channel_id=1, source_target_pairs={{0,1},{1,2},{2,3},{3,0},{16,19},{17,16},{18,17},{19,18},{4,5},{5,6... | collective-permute-start | bytes 1572872 | tf_op jit(solution)/shard_map/ppermute | solution.py:407
  59.8 21.6 %copy-start.5 = (bf16[12,8,1024]{2,1,0:T(8,128)(2,1)S(1)}, bf16[12,8,1024]{2,1,0:T(8,128)(2,1)}, u32[]{:S(2)}) copy-start(bf16[12,8,1024]{2,1,0:T(8,128)(2,1)} %param.9) | copy-start | bytes 589828
  59.8 9.4 %collective-permute-start.11 = (bf16[32,3072]{1,0:T(8,128)(2,1)S(1)}, bf16[32,3072]{1,0:T(8,128)(2,1)S(1)}, u32[]{:S(2)}, u32[]{:S(2)}) collective-permute-start(bf16[32,3072]{1,0:T(8,128)(2,1)S(1)} %half.6), channel_id=1, source_target_pairs={{0,4},{4,8},{8,12},{12,0},{16,28},{20,16},{24,20},{28,24},{1,5},{5... | collective-permute-start | bytes 589832 | tf_op jit(solution)/shard_map/ppermute | solution.py:408
  69.2 15.5 %collective-permute-start.12 = (bf16[96,3072]{1,0:T(8,128)(2,1)S(1)}, bf16[96,3072]{1,0:T(8,128)(2,1)S(1)}, u32[]{:S(2)}, u32[]{:S(2)}) collective-permute-start(bf16[96,3072]{1,0:T(8,128)(2,1)S(1)} %pack.5), channel_id=1, source_target_pairs={{0,16},{16,0},{1,17},{17,1},{2,18},{18,2},{3,19},{19,3},{4,20},{20... | collective-permute-start | bytes 1769480 | tf_op jit(solution)/shard_map/ppermute | solution.py:409
  72.2 12.5 %collective-permute-start.8 = (bf16[128,1024]{1,0:T(8,128)(2,1)S(1)}, bf16[128,1024]{1,0:T(8,128)(2,1)S(1)}, u32[]{:S(2)}, u32[]{:S(2)}) collective-permute-start(bf16[128,1024]{1,0:T(8,128)(2,1)S(1)} %half.5), channel_id=1, source_target_pairs={{0,1},{1,2},{2,3},{3,0},{16,19},{17,16},{18,17},{19,18},{4,5},{5,6... | collective-permute-start | bytes 786440 | tf_op jit(solution)/shard_map/ppermute | solution.py:408
  85.3 9.4 %copy-start.6 = (bf16[12,8,1024]{2,1,0:T(8,128)(2,1)S(1)}, bf16[12,8,1024]{2,1,0:T(8,128)(2,1)}, u32[]{:S(2)}) copy-start(bf16[12,8,1024]{2,1,0:T(8,128)(2,1)} %param.8) | copy-start | bytes 589828
  85.4 9.4 %copy-start.8 = (f32[1024]{0:T(1024)S(1)}, f32[1024]{0:T(1024)}, u32[]{:S(2)}) copy-start(f32[1024]{0:T(1024)} %param.14) | copy-start | bytes 12292
  85.4 23.9 %collective-permute-start.13 = (bf16[256,3072]{1,0:T(8,128)(2,1)S(1)}, bf16[256,3072]{1,0:T(8,128)(2,1)S(1)}, u32[]{:S(2)}, u32[]{:S(2)}) collective-permute-start(bf16[256,3072]{1,0:T(8,128)(2,1)S(1)} %place.3.rest_0_.rest_5_.rest_10_), channel_id=1, source_target_pairs={{0,1},{1,2},{2,3},{3,0},{16,19},{17,16},{18,17},{19,18},{4,5},{5,6... | collective-permute-start | bytes 4718600 | tf_op jit(solution)/shard_map/ppermute | solution.py:464
  90.6 4.2 %collective-permute-start.9 = (bf16[384,1024]{1,0:T(8,128)(2,1)S(1)}, bf16[384,1024]{1,0:T(8,128)(2,1)S(1)}, u32[]{:S(2)}, u32[]{:S(2)}) collective-permute-start(bf16[384,1024]{1,0:T(8,128)(2,1)S(1)} %pack.4), channel_id=1, source_target_pairs={{0,16},{16,0},{1,17},{17,1},{2,18},{18,2},{3,19},{19,3},{4,20},{20... | collective-permute-start | bytes 2359304 | tf_op jit(solution)/shard_map/ppermute | solution.py:409
  96.7 12.6 %collective-permute-start.14 = (bf16[96,1024]{1,0:T(8,128)(2,1)S(1)}, bf16[96,1024]{1,0:T(8,128)(2,1)S(1)}, u32[]{:S(2)}, u32[]{:S(2)}) collective-permute-start(bf16[96,1024]{1,0:T(8,128)(2,1)S(1)} %get-tuple-element.28.own_ref), channel_id=1, source_target_pairs={{0,4},{4,8},{8,12},{12,16},{16,20},{20,24},{24,28},{28,32},{32,36}... | collective-permute-start | bytes 589832 | tf_op jit(solution)/shard_map/ppermute | solution.py:463
  109.9 22.8 %collective-permute-start.15 = (bf16[128,3072]{1,0:T(8,128)(2,1)S(1)}, bf16[128,3072]{1,0:T(8,128)(2,1)S(1)}, u32[]{:S(2)}, u32[]{:S(2)}) collective-permute-start(bf16[128,3072]{1,0:T(8,128)(2,1)S(1)} %half.7.after_ref), channel_id=1, source_target_pairs={{0,1},{1,2},{2,3},{3,0},{16,19},{17,16},{18,17},{19,18},{4,5},{5,6... | collective-permute-start | bytes 2359304 | tf_op jit(solution)/shard_map/ppermute | solution.py:466
  114.5 23.8 %collective-permute-start.19 = (bf16[256,3072]{1,0:T(8,128)(2,1)S(1)}, bf16[256,3072]{1,0:T(8,128)(2,1)S(1)}, u32[]{:S(2)}, u32[]{:S(2)}) collective-permute-start(bf16[256,3072]{1,0:T(8,128)(2,1)S(1)} %collective-permute-done.13.x_ref.rest_1_.rest_6_.rest_11_), channel_id=1, source_target_pairs={{0,16},{16,0},{1,17},{17,1},{2,18},{18,2},{3,19},{19,3},{4,20},{20... | collective-permute-start | bytes 4718600 | tf_op jit(solution)/shard_map/ppermute | solution.py:470
  117.0 10.2 %collective-permute-start.16 = (bf16[96,1024]{1,0:T(8,128)(2,1)S(1)}, bf16[96,1024]{1,0:T(8,128)(2,1)S(1)}, u32[]{:S(2)}, u32[]{:S(2)}) collective-permute-start(bf16[96,1024]{1,0:T(8,128)(2,1)S(1)} %get-tuple-element.25), channel_id=1, source_target_pairs={{0,1},{1,2},{2,3},{3,0},{4,5},{5,6},{6,7},{7,4},{8,9},{9,10},{10,1... | collective-permute-start | bytes 589832 | tf_op jit(solution)/shard_map/ppermute | solution.py:469
  119.0 12.2 %collective-permute-start.17 = (bf16[96,1024]{1,0:T(8,128)(2,1)S(1)}, bf16[96,1024]{1,0:T(8,128)(2,1)S(1)}, u32[]{:S(2)}, u32[]{:S(2)}) collective-permute-start(bf16[96,1024]{1,0:T(8,128)(2,1)S(1)} %get-tuple-element.26), channel_id=1, source_target_pairs={{0,2},{1,3},{2,0},{3,1},{4,6},{5,7},{6,4},{7,5},{8,10},{9,11},{10,... | collective-permute-start | bytes 589832 | tf_op jit(solution)/shard_map/ppermute | solution.py:469
  123.4 9.3 %collective-permute-start.18 = (bf16[96,1024]{1,0:T(8,128)(2,1)S(1)}, bf16[96,1024]{1,0:T(8,128)(2,1)S(1)}, u32[]{:S(2)}, u32[]{:S(2)}) collective-permute-start(bf16[96,1024]{1,0:T(8,128)(2,1)S(1)} %get-tuple-element.27), channel_id=1, source_target_pairs={{0,3},{1,0},{2,1},{3,2},{4,7},{5,4},{6,5},{7,6},{8,11},{9,8},{10,9... | collective-permute-start | bytes 589832 | tf_op jit(solution)/shard_map/ppermute | solution.py:469
  132.6 5.6 %collective-permute-start.20 = (bf16[128,3072]{1,0:T(8,128)(2,1)S(1)}, bf16[128,3072]{1,0:T(8,128)(2,1)S(1)}, u32[]{:S(2)}, u32[]{:S(2)}) collective-permute-start(bf16[128,3072]{1,0:T(8,128)(2,1)S(1)} %collective-permute-done.15.rest_3_.rest_8_.rest_13_), channel_id=1, source_target_pairs={{0,16},{16,0},{1,17},{17,1},{2,18},{18,2},{3,19},{19,3},{4,20},{20... | collective-permute-start | bytes 2359304 | tf_op jit(solution)/shard_map/ppermute | solution.py:472
